TPU v7x, 32 devices: a whole 2x2x4 slice. The times are simulated.
32 devices in a mesh: dp: 4 (over y, x), cp: 4 (over z), tp: 2 (over core).
Axes of the slice: x: 2, y: 2, z: 4, core: 2. Of those that a mesh axis runs over, the one named last changes fastest.
Arguments:
- activations: bfloat16 [4, 4, 2, 64, 2048], P('dp', 'cp'), may hold values from -6 to 6
- document_ids: int32 [4, 512], P('dp'), may hold values from 0 to 5, as said below
- attn_gain: bfloat16 [2048], P('cp'), may hold values from 0.099609375 to 1.8984375
- w_query: bfloat16 [2048, 2048], P('cp', 'tp'), may hold values from -0.1875 to 0.1875
- w_key: bfloat16 [2048, 2048], P('cp', 'tp'), may hold values from -0.1875 to 0.1875
- w_value: bfloat16 [2048, 2048], P('cp', 'tp'), may hold values from -0.125 to 0.125
- w_out: bfloat16 [2048, 2048], P('tp', 'cp'), may hold values from -0.25 to 0.25
- mlp_gain: bfloat16 [2048], P('cp'), may hold values from 0.099609375 to 1.8984375
- w_gate: bfloat16 [2048, 8192], P('cp', 'tp'), may hold values from -0.125 to 0.125
- w_up: bfloat16 [2048, 8192], P('cp', 'tp'), may hold values from -0.125 to 0.125
- w_down: bfloat16 [8192, 2048], P('tp', 'cp'), may hold values from -0.0625 to 0.0625
- cotangent: bfloat16 [4, 4, 2, 64, 2048], P('dp', 'cp'), may hold values from -6 to 6
Outputs:
- layer_out: bfloat16 [4, 4, 2, 64, 2048], P('dp', 'cp')
- input_grad: bfloat16 [4, 4, 2, 64, 2048], P('dp', 'cp')
- attn_gain_grad: float32 [2048], P('cp')
- w_query_grad: float32 [2048, 2048], P('cp', 'tp')
- w_key_grad: float32 [2048, 2048], P('cp', 'tp')
- w_value_grad: float32 [2048, 2048], P('cp', 'tp')
- w_out_grad: float32 [2048, 2048], P('tp', 'cp')
- mlp_gain_grad: float32 [2048], P('cp')
- w_gate_grad: float32 [2048, 8192], P('cp', 'tp')
- w_up_grad: float32 [2048, 8192], P('cp', 'tp')
- w_down_grad: float32 [8192, 2048], P('tp', 'cp')
Inputs may be any that keep to these rules, and one draw needn't show every extreme that they name: `document_ids`: row b numbers the six documents of sequence b in the order of their tokens: 0 at the first token, never falling, rising by one at each new document. In every row the second document begins within the first 64 tokens and covers 512 / 2 tokens or more.
All inputs are finite; a program needn't handle non-finite values.
Results may differ from a plain program's by a relative error of at most 0.015.
Values may be sent and summed in bfloat16 or wider, within the bound.
A program may use at most 448 MiB of HBM per device.

v0:
```python
import math

import jax
import jax.numpy as jnp
from jax import lax
from jax.sharding import PartitionSpec as P

HEAD_DIM = 128


EPS = 1e-05
SHIFT = math.log(4096.0)
ROPE_BASE = 10000.0


def angles(positions):
    half_dim = HEAD_DIM // 2
    frequency = ROPE_BASE ** (-jnp.arange(half_dim, dtype=jnp.float32) / half_dim)
    angle = positions.astype(jnp.float32)[:, None] * frequency[None, :]
    return (jnp.cos(angle)[:, None, :], jnp.sin(angle)[:, None, :])


def rotate(flat, positions):
    row_count = flat.shape[0]
    heads = flat.reshape(row_count, -1, HEAD_DIM)
    cosine, sine = angles(positions)
    first = heads[..., : HEAD_DIM // 2]
    second = heads[..., HEAD_DIM // 2 :]
    turned = jnp.concatenate(
        [first * cosine - second * sine, second * cosine + first * sine], axis=-1
    )
    return turned.reshape(row_count, -1)


def unrotate(flat, positions):
    row_count = flat.shape[0]
    heads = flat.reshape(row_count, -1, HEAD_DIM)
    cosine, sine = angles(positions)
    first = heads[..., : HEAD_DIM // 2]
    second = heads[..., HEAD_DIM // 2 :]
    turned = jnp.concatenate(
        [first * cosine + second * sine, second * cosine - first * sine], axis=-1
    )
    return turned.reshape(row_count, -1)


def normalize(values):
    inverse = lax.rsqrt(jnp.mean(values * values, axis=-1, keepdims=True) + EPS)
    return (values * inverse, inverse)


def norm_back(grad_normed_out, normed, inverse, gain):
    scaled = grad_normed_out * gain
    return inverse * (scaled - normed * jnp.mean(scaled * normed, axis=-1, keepdims=True))


def contract_rows(left, right):
    return lax.dot_general(
        left, right, (((1,), (1,)), ((), ())), preferred_element_type=jnp.float32
    )


def contract_cols(left, right):
    return lax.dot_general(
        left, right, (((0,), (0,)), ((), ())), preferred_element_type=jnp.float32
    )


def visibility(query_positions, query_docs, key_positions, key_docs):
    same_doc = query_docs[:, None] == key_docs[None, :]
    earlier = key_positions[None, :] <= query_positions[:, None]
    return jnp.where(same_doc & earlier, 1.0, 0.0).astype(jnp.float32)


def merge_heads(stacked):
    return jnp.transpose(stacked, (1, 0, 2)).reshape(stacked.shape[1], -1)


def head_slice(matrix, offset):
    return lax.dynamic_slice_in_dim(matrix, offset, HEAD_DIM, 1)


def attend_forward(queries, key_rows, value_rows, visible):
    score_scale = HEAD_DIM ** (-0.5)

    def one_head(head_index):
        offset = head_index * HEAD_DIM
        scores = (
            contract_rows(head_slice(queries, offset), head_slice(key_rows, offset)) * score_scale
        )
        weights = (jax.nn.sigmoid(scores - SHIFT) * visible).astype(jnp.bfloat16)
        return jnp.dot(weights, head_slice(value_rows, offset), preferred_element_type=jnp.float32)

    stacked = lax.map(one_head, jnp.arange(queries.shape[1] // HEAD_DIM))
    return merge_heads(stacked)


def attend_back(queries, key_rows, value_rows, grad_attended, visible):
    score_scale = HEAD_DIM ** (-0.5)

    def one_head(head_index):
        offset = head_index * HEAD_DIM
        head_query = head_slice(queries, offset)
        head_key = head_slice(key_rows, offset)
        head_grad = head_slice(grad_attended, offset)
        scores = contract_rows(head_query, head_key) * score_scale
        sigma = jax.nn.sigmoid(scores - SHIFT)
        grad_weights = contract_rows(head_grad, head_slice(value_rows, offset))
        grad_scores = (grad_weights * visible * sigma * (1.0 - sigma)).astype(jnp.bfloat16)
        pieces = []
        pieces.append(
            jnp.dot(grad_scores, head_key, preferred_element_type=jnp.float32) * score_scale
        )
        weights = (sigma * visible).astype(jnp.bfloat16)
        pieces.append(contract_cols(grad_scores, head_query) * score_scale)
        pieces.append(contract_cols(weights, head_grad))
        return tuple(pieces)

    stacked = lax.map(one_head, jnp.arange(queries.shape[1] // HEAD_DIM))
    return tuple((merge_heads(piece) for piece in stacked))


def shards(
    activations,
    document_ids,
    attn_gain,
    w_query,
    w_key,
    w_value,
    w_out,
    mlp_gain,
    w_gate,
    w_up,
    w_down,
    cotangent,
):
    groups = lax.axis_size("cp")
    rank = lax.axis_index("cp")
    stretch_len = activations.shape[3]
    width = activations.shape[4]
    row_count = 2 * stretch_len
    offsets = jnp.arange(stretch_len, dtype=jnp.int32)
    my_positions = jnp.concatenate(
        [rank * stretch_len + offsets, (2 * groups - 1 - rank) * stretch_len + offsets]
    )
    all_docs = document_ids[0]
    my_docs = jnp.take(all_docs, my_positions)
    slots = jnp.arange(groups * row_count, dtype=jnp.int32)
    owners = slots // row_count
    halves = slots // stretch_len % 2
    key_positions = (
        jnp.where(halves == 0, owners, 2 * groups - 1 - owners) * stretch_len + slots % stretch_len
    )
    key_docs = jnp.take(all_docs, key_positions)
    visible = visibility(my_positions, my_docs, key_positions, key_docs)
    gathered = (
        lax.all_gather(w_query, "cp", axis=0, tiled=True),
        lax.all_gather(w_key, "cp", axis=0, tiled=True),
        lax.all_gather(w_value, "cp", axis=0, tiled=True),
        lax.all_gather(w_out, "cp", axis=1, tiled=True),
        lax.all_gather(w_gate, "cp", axis=0, tiled=True),
        lax.all_gather(w_up, "cp", axis=0, tiled=True),
        lax.all_gather(w_down, "cp", axis=1, tiled=True),
        lax.all_gather(attn_gain, "cp", axis=0, tiled=True),
        lax.all_gather(mlp_gain, "cp", axis=0, tiled=True),
    )
    (
        query_full,
        key_full,
        value_full,
        out_full,
        gate_full,
        up_full,
        down_full,
        gain_one,
        gain_two,
    ) = gathered
    gain_one = gain_one.astype(jnp.float32)
    gain_two = gain_two.astype(jnp.float32)
    inputs = activations.reshape(row_count, width).astype(jnp.float32)
    normed_one, inverse_one = normalize(inputs)
    hidden_one = (normed_one * gain_one).astype(jnp.bfloat16)
    queries = rotate(
        jnp.dot(hidden_one, query_full, preferred_element_type=jnp.float32), my_positions
    ).astype(jnp.bfloat16)
    keys_local = rotate(
        jnp.dot(hidden_one, key_full, preferred_element_type=jnp.float32), my_positions
    ).astype(jnp.bfloat16)
    values_local = jnp.dot(hidden_one, value_full, preferred_element_type=jnp.float32).astype(
        jnp.bfloat16
    )
    keys_all, values_all = (
        lax.all_gather(keys_local, "cp", axis=0, tiled=True),
        lax.all_gather(values_local, "cp", axis=0, tiled=True),
    )
    attended = attend_forward(queries, keys_all, values_all, visible).astype(jnp.bfloat16)
    branch = lax.psum(jnp.dot(attended, out_full, preferred_element_type=jnp.float32), "tp")
    middle = inputs + branch
    normed_two, inverse_two = normalize(middle)
    hidden_two = (normed_two * gain_two).astype(jnp.bfloat16)
    gate = jnp.dot(hidden_two, gate_full, preferred_element_type=jnp.float32)
    upward = jnp.dot(hidden_two, up_full, preferred_element_type=jnp.float32)
    sigma_gate = jax.nn.sigmoid(gate)
    silu_gate = gate * sigma_gate
    product = (silu_gate * upward).astype(jnp.bfloat16)
    feed = lax.psum(jnp.dot(product, down_full, preferred_element_type=jnp.float32), "tp")
    result = middle + feed
    layer_out = result.astype(jnp.bfloat16).reshape(activations.shape)
    grad_result = cotangent.reshape(row_count, width).astype(jnp.float32)
    grad_feed = grad_result.astype(jnp.bfloat16)
    grad_product = contract_rows(grad_feed, down_full)
    grad_gate = (grad_product * upward * sigma_gate * (1.0 + gate * (1.0 - sigma_gate))).astype(
        jnp.bfloat16
    )
    grad_up = (grad_product * silu_gate).astype(jnp.bfloat16)
    grad_hidden_two = lax.psum(
        contract_rows(grad_gate, gate_full) + contract_rows(grad_up, up_full), "tp"
    )
    grad_gain_two = jnp.sum(grad_hidden_two * normed_two, axis=0)
    grad_middle = grad_result + norm_back(grad_hidden_two, normed_two, inverse_two, gain_two)
    grad_down = contract_cols(product, grad_feed)
    grad_gate_w = contract_cols(hidden_two, grad_gate)
    grad_up_w = contract_cols(hidden_two, grad_up)
    share_gate, share_up, share_down, share_gain_two = (
        lax.psum_scatter(grad_gate_w, "cp", scatter_dimension=0, tiled=True),
        lax.psum_scatter(grad_up_w, "cp", scatter_dimension=0, tiled=True),
        lax.psum_scatter(grad_down, "cp", scatter_dimension=1, tiled=True),
        lax.psum_scatter(grad_gain_two, "cp", scatter_dimension=0, tiled=True),
    )
    grad_branch = grad_middle.astype(jnp.bfloat16)
    grad_attended = contract_rows(grad_branch, out_full).astype(jnp.bfloat16)
    grad_queries, key_terms, value_terms = attend_back(
        queries, keys_all, values_all, grad_attended, visible
    )
    grad_keys, grad_values = (
        lax.psum_scatter(key_terms, "cp", scatter_dimension=0, tiled=True),
        lax.psum_scatter(value_terms, "cp", scatter_dimension=0, tiled=True),
    )
    grad_query_pre = unrotate(grad_queries, my_positions).astype(jnp.bfloat16)
    grad_key_pre = unrotate(grad_keys, my_positions).astype(jnp.bfloat16)
    grad_value_pre = grad_values.astype(jnp.bfloat16)
    local_hidden = (
        contract_rows(grad_query_pre, query_full)
        + contract_rows(grad_key_pre, key_full)
        + contract_rows(grad_value_pre, value_full)
    )
    grad_hidden_one = lax.psum(local_hidden, "tp")
    grad_gain_one = jnp.sum(grad_hidden_one * normed_one, axis=0)
    grad_inputs = grad_middle + norm_back(grad_hidden_one, normed_one, inverse_one, gain_one)
    grad_query_w = contract_cols(hidden_one, grad_query_pre)
    grad_key_w = contract_cols(hidden_one, grad_key_pre)
    grad_value_w = contract_cols(hidden_one, grad_value_pre)
    grad_out_w = contract_cols(attended, grad_branch)
    share_query, share_key, share_value, share_out, share_gain_one = (
        lax.psum_scatter(grad_query_w, "cp", scatter_dimension=0, tiled=True),
        lax.psum_scatter(grad_key_w, "cp", scatter_dimension=0, tiled=True),
        lax.psum_scatter(grad_value_w, "cp", scatter_dimension=0, tiled=True),
        lax.psum_scatter(grad_out_w, "cp", scatter_dimension=1, tiled=True),
        lax.psum_scatter(grad_gain_one, "cp", scatter_dimension=0, tiled=True),
    )
    summed = lax.psum(
        (
            share_gain_one,
            share_query,
            share_key,
            share_value,
            share_out,
            share_gain_two,
            share_gate,
            share_up,
            share_down,
        ),
        "dp",
    )
    input_grad = grad_inputs.astype(jnp.bfloat16).reshape(activations.shape)
    return (
        layer_out,
        input_grad,
        summed[0],
        summed[1],
        summed[2],
        summed[3],
        summed[4],
        summed[5],
        summed[6],
        summed[7],
        summed[8],
    )


def solution(mesh):
    return jax.shard_map(
        shards,
        mesh=mesh,
        in_specs=(
            P("dp", "cp", None, None, None),
            P("dp", None),
            P("cp"),
            P("cp", "tp"),
            P("cp", "tp"),
            P("cp", "tp"),
            P("tp", "cp"),
            P("cp"),
            P("cp", "tp"),
            P("cp", "tp"),
            P("tp", "cp"),
            P("dp", "cp", None, None, None),
        ),
        out_specs=(
            P("dp", "cp", None, None, None),
            P("dp", "cp", None, None, None),
            P("cp"),
            P("cp", "tp"),
            P("cp", "tp"),
            P("cp", "tp"),
            P("tp", "cp"),
            P("cp"),
            P("cp", "tp"),
            P("cp", "tp"),
            P("tp", "cp"),
        ),
        check_vma=False,
    )
```

profile of v0, /device:TPU:0, one launch (start us, length us, event | category | flops | bytes accessed | tf_op | source)
XLA Modules:
  0.0 4405.2 jit_solution(15284184898454563077)
XLA Ops:
  10.2 13.5 all-gather
  26.9 66.2 %all-gather.14.cloned.1.call-done = bf16[2048,1024]{1,0:T(8,128)(2,1)} async-done(((bf16[512,1024]{1,0:T(8,128)(2,1)}), bf16[2048,1024]{1,0:T(8,128)(2,1)}) %all-gather.14.cloned.1.call-update) | async-done | bytes 4194320 | tf_op jit(solution)/shard_map/all_gather | solution.py:158
  93.1 6.4 copy.39
  99.5 74.5 %all-gather.12.cloned.1.call-done = bf16[2048,1024]{1,0:T(8,128)(2,1)} async-done(((bf16[512,1024]{1,0:T(8,128)(2,1)}), bf16[2048,1024]{1,0:T(8,128)(2,1)}) %all-gather.12.cloned.1.call-update) | async-done | bytes 4194320 | tf_op jit(solution)/shard_map/all_gather | solution.py:157
  174.0 6.4 copy.38
  180.4 4.0 fusion.110
  187.3 67.6 %all-gather.18.cloned.1.call-done = bf16[2048,1024]{1,0:T(8,128)(2,1)} async-done(((bf16[512,1024]{1,0:T(8,128)(2,1)}), bf16[2048,1024]{1,0:T(8,128)(2,1)}) %all-gather.18.cloned.1.call-update) | async-done | bytes 4194320 | tf_op jit(solution)/shard_map/all_gather | solution.py:159
  254.9 3.6 convolution_convert_fusion.1
  263.0 20.4 all-gather.16.cloned.1.call-done
  283.4 29.4 all-gather.20.cloned.1.call-done
  312.8 21.2 while.32
  334.1 60.5 %all-gather.22.cloned.1.call-done = bf16[1024,2048]{1,0:T(8,128)(2,1)} async-done(((bf16[1024,512]{1,0:T(8,128)(2,1)}), bf16[1024,2048]{1,0:T(8,128)(2,1)}) %all-gather.22.cloned.1.call-update) | async-done | bytes 4194320 | tf_op jit(solution)/shard_map/all_gather | solution.py:160
  394.6 3.9 fusion.111
  400.7 12.0 all-gather.1
  412.7 4.1 all-reduce.11.cloned.1.call-done
  418.4 288.0 %all-gather.24.cloned.1.call-done = bf16[2048,4096]{1,0:T(8,128)(2,1)} async-done(((bf16[512,4096]{1,0:T(8,128)(2,1)}), bf16[2048,4096]{1,0:T(8,128)(2,1)}) %all-gather.24.cloned.1.call-update) | async-done | bytes 16777232 | tf_op jit(solution)/shard_map/all_gather | solution.py:161
  706.4 9.5 fusion.112
  715.9 277.2 %all-gather.26.cloned.1.call-done = bf16[2048,4096]{1,0:T(8,128)(2,1)} async-done(((bf16[512,4096]{1,0:T(8,128)(2,1)}), bf16[2048,4096]{1,0:T(8,128)(2,1)}) %all-gather.26.cloned.1.call-update) | async-done | bytes 16777232 | tf_op jit(solution)/shard_map/all_gather | solution.py:162
  993.1 9.5 fusion.113
  1002.5 277.0 %all-gather.28.cloned.1.call-done = bf16[4096,2048]{1,0:T(8,128)(2,1)} async-done(((bf16[4096,512]{1,0:T(8,128)(2,1)}), bf16[4096,2048]{1,0:T(8,128)(2,1)}) %all-gather.28.cloned.1.call-update) | async-done | bytes 16777232 | tf_op jit(solution)/shard_map/all_gather | solution.py:163
  1279.6 14.4 multiply_convert_fusion
  1294.0 13.3 fusion.115
  1307.3 12.6 convolution_add_fusion.2
  1320.0 17.8 all-reduce.13.cloned.1.call-done
  1342.9 65.4 %while.33 = (s32[]{:T(128)}, f32[8,128,128]{1,2,0:T(8,128)}, f32[8,512,128]{1,2,0:T(8,128)}, f32[8,512,128]{1,2,0:T(8,128)}, s32[8]{0:T(128)S(1)}, /*index=5*/bf...) while((s32[]{:T(128)}, f32[8,128,128]{1,2,0:T(8,128)}, ...), condition=%wide.region_9.10_spmd.clone.clone, body=%wide.region_8.9_spmd.clone.sunk.clone | while | flops 85278720 | bytes 3616991 | solution.py:119
  1409.5 4.5 fusion.85
  1414.2 39.4 reduce-scatter.10.cloned.1.call-done
  1456.3 4.7 fusion.117
  1462.0 4.7 fusion.118
  1467.2 32.5 reduce-scatter.12.cloned.1.call-done
  1499.7 5.7 fusion.88
  1505.5 14.5 fusion.119
  1520.1 14.5 fusion.120
  1535.6 14.7 fusion.121
  1550.6 9.6 fusion.114
  1567.5 78.3 %reduce-scatter.20.cloned.1.call-done = f32[1024,512]{1,0:T(8,128)} async-done(((f32[1024,2048]{1,0:T(8,128)}), f32[1024,512]{1,0:T(8,128)}) %reduce-scatter.20.cloned.1.call-update) | async-done | bytes 2097168 | tf_op jit(solution)/shard_map/reduce_scatter | solution.py:258
  1645.8 148.0 %reduce-scatter.14.cloned.1.call-done = f32[512,1024]{1,0:T(8,128)} async-done(((f32[2048,1024]{1,0:T(8,128)}), f32[512,1024]{1,0:T(8,128)}) %reduce-scatter.14.cloned.1.call-update) | async-done | bytes 2097168 | tf_op jit(solution)/shard_map/reduce_scatter | solution.py:255
  1793.8 148.0 %reduce-scatter.16.cloned.1.call-done = f32[512,1024]{1,0:T(8,128)} async-done(((f32[2048,1024]{1,0:T(8,128)}), f32[512,1024]{1,0:T(8,128)}) %reduce-scatter.16.cloned.1.call-update) | async-done | bytes 2097168 | tf_op jit(solution)/shard_map/reduce_scatter | solution.py:256
  1941.8 148.0 %reduce-scatter.18.cloned.1.call-done = f32[512,1024]{1,0:T(8,128)} async-done(((f32[2048,1024]{1,0:T(8,128)}), f32[512,1024]{1,0:T(8,128)}) %reduce-scatter.18.cloned.1.call-update) | async-done | bytes 2097168 | tf_op jit(solution)/shard_map/reduce_scatter | solution.py:257
  2089.8 555.0 %reduce-scatter.22.cloned.1.call-done = f32[512,4096]{1,0:T(8,128)} async-done(((f32[2048,4096]{1,0:T(8,128)}), f32[512,4096]{1,0:T(8,128)}) %reduce-scatter.22.cloned.1.call-update) | async-done | bytes 8388624 | tf_op jit(solution)/shard_map/reduce_scatter | solution.py:225
  2644.8 555.3 %reduce-scatter.24.cloned.1.call-done = f32[512,4096]{1,0:T(8,128)} async-done(((f32[2048,4096]{1,0:T(8,128)}), f32[512,4096]{1,0:T(8,128)}) %reduce-scatter.24.cloned.1.call-update) | async-done | bytes 8388624 | tf_op jit(solution)/shard_map/reduce_scatter | solution.py:226
  3200.2 555.0 %reduce-scatter.26.cloned.1.call-done = f32[4096,512]{1,0:T(8,128)} async-done(((f32[4096,2048]{1,0:T(8,128)}), f32[4096,512]{1,0:T(8,128)}) %reduce-scatter.26.cloned.1.call-update) | async-done | bytes 8388624 | tf_op jit(solution)/shard_map/reduce_scatter | solution.py:227
  3757.0 23.2 all-reduce.17.cloned.1.call-done
  3781.9 19.0 all-reduce.2
  3801.0 10.6 all-reduce.3
  3816.3 557.5 %all-reduce.15.cloned.1.call-done = (f32[512,1024]{1,0:T(8,128)}, f32[512,1024]{1,0:T(8,128)}, f32[512,1024]{1,0:T(8,128)}, f32[1024,512]{1,0:T(8,128)}, f32[512...) async-done(((f32[512,1024]{1,0:T(8,128)}, f32[512,1024]{1,0:T(8,128)}, f32[512,1024]{1,0:T(8,128)}, f32[1024,512]{1,0:T(8,128)}, f32[512,4096]{1,0:T(8,128)}, ...) | async-done | bytes 33554448 | tf_op jit(solution)/shard_map/psum | solution.py:261
  4381.1 8.5 copy.106
  4389.6 4.3 copy.107
  (269 shorter events, 131.0 us)
Async XLA Ops:
  7.2 16.6 copy-start
  7.2 19.5 copy-start.2
  7.2 85.9 %all-gather.14.cloned.1.call-start = ((), (), s32[]{:S(2)}) async-start(), calls=%async_computation.10 | async-start | bytes 5242880 | tf_op jit(solution)/shard_map/all_gather | solution.py:158
  7.9 166.1 %all-gather.12.cloned.1.call-start = ((), (), s32[]{:S(2)}) async-start(), calls=%async_computation.9 | async-start | bytes 5242880 | tf_op jit(solution)/shard_map/all_gather | solution.py:157
  8.7 246.2 %all-gather.18.cloned.1.call-start = ((), (), s32[]{:S(2)}) async-start(), calls=%async_computation.12 | async-start | bytes 5242880 | tf_op jit(solution)/shard_map/all_gather | solution.py:159
  9.4 274.0 %all-gather.16.cloned.1.call-start = ((), (), s32[]{:S(2)}) async-start(), calls=%async_computation.11 | async-start | bytes 1310720 | tf_op jit(solution)/shard_map/all_gather | solution.py:193
  23.7 163.4 %copy-start.24 = (f32[4,1,512]{2,1,0:T(1,128)}, f32[4,1,512]{2,1,0:T(1,128)S(1)}, u32[]{:S(2)}) copy-start(f32[4,1,512]{2,1,0:T(1,128)S(1)} %convert_element_type.165) | copy-start | bytes 24580
  26.7 159.2 %copy-start.22 = (f32[128,64]{0,1:T(8,128)}, f32[128,64]{0,1:T(8,128)S(1)}, u32[]{:S(2)}) copy-start(f32[128,64]{0,1:T(8,128)S(1)} %get-tuple-element.440) | copy-start | bytes 98308
  26.7 159.2 %copy-start.23 = (f32[128,64]{0,1:T(8,128)}, f32[128,64]{0,1:T(8,128)S(1)}, u32[]{:S(2)}) copy-start(f32[128,64]{0,1:T(8,128)S(1)} %get-tuple-element.441) | copy-start | bytes 98308
  180.4 4.2 copy-start.4
  186.9 125.9 %all-gather.20.cloned.1.call-start = ((), (), s32[]{:S(2)}) async-start(), calls=%async_computation.13 | async-start | bytes 1310720 | tf_op jit(solution)/shard_map/all_gather | solution.py:194
  187.1 75.7 %copy-start.26 = (f32[128]{0:T(128)}, f32[128]{0:T(128)S(1)}, u32[]{:S(2)}) copy-start(f32[128]{0:T(128)S(1)} %rsqrt.21) | copy-start | bytes 1540
  187.3 75.5 %copy-start.11 = (bf16[128,2048]{1,0:T(8,128)(2,1)}, bf16[128,2048]{1,0:T(8,128)(2,1)S(1)}, u32[]{:S(2)}) copy-start(bf16[128,2048]{1,0:T(8,128)(2,1)S(1)} %fusion.75) | copy-start | bytes 1572868
  258.6 136.0 %all-gather.22.cloned.1.call-start = ((), (), s32[]{:S(2)}) async-start(), calls=%async_computation.14 | async-start | bytes 5242880 | tf_op jit(solution)/shard_map/all_gather | solution.py:160
  259.2 157.6 %all-reduce.11.cloned.1.call-start = ((), (), s32[]{:S(2)}) async-start(), calls=%async_computation.15 | async-start | bytes 2097152 | tf_op jit(solution)/shard_map/psum | solution.py:197
  334.1 65.2 %copy-start.21 = (bf16[128,1024]{1,0:T(8,128)(2,1)}, bf16[128,1024]{1,0:T(8,128)(2,1)S(1)}, u32[]{:S(2)}) copy-start(bf16[128,1024]{1,0:T(8,128)(2,1)S(1)} %get-tuple-element.851) | copy-start | bytes 786436
  398.5 307.9 %all-gather.24.cloned.1.call-start = ((), (), s32[]{:S(2)}) async-start(), calls=%async_computation.16 | async-start | bytes 20971520 | tf_op jit(solution)/shard_map/all_gather | solution.py:161
  399.3 593.8 %all-gather.26.cloned.1.call-start = ((), (), s32[]{:S(2)}) async-start(), calls=%async_computation.17 | async-start | bytes 20971520 | tf_op jit(solution)/shard_map/all_gather | solution.py:162
  400.0 879.6 %all-gather.28.cloned.1.call-start = ((), (), s32[]{:S(2)}) async-start(), calls=%async_computation.18 | async-start | bytes 20971520 | tf_op jit(solution)/shard_map/all_gather | solution.py:163
  400.6 937.2 %all-reduce.13.cloned.1.call-start = ((), (), s32[]{:S(2)}) async-start(), calls=%async_computation.19 | async-start | bytes 2097152 | tf_op jit(solution)/shard_map/psum | solution.py:216
  1294.0 13.3 copy-start.13
  1319.9 133.6 %reduce-scatter.10.cloned.1.call-start = ((), (), s32[]{:S(2)}) async-start(), calls=%async_computation.20 | async-start | bytes 2621440 | tf_op jit(solution)/shard_map/reduce_scatter | solution.py:236
  1337.8 3.5 copy-start.8
  1408.3 91.4 %reduce-scatter.12.cloned.1.call-start = ((), (), s32[]{:S(2)}) async-start(), calls=%async_computation.21 | async-start | bytes 2621440 | tf_op jit(solution)/shard_map/reduce_scatter | solution.py:237
  1409.1 236.7 %reduce-scatter.20.cloned.1.call-start = ((), (), s32[]{:S(2)}) async-start(), calls=%async_computation.25 | async-start | bytes 10485760 | tf_op jit(solution)/shard_map/reduce_scatter | solution.py:258
  1414.1 379.7 %reduce-scatter.14.cloned.1.call-start = ((), (), s32[]{:S(2)}) async-start(), calls=%async_computation.22 | async-start | bytes 10485760 | tf_op jit(solution)/shard_map/reduce_scatter | solution.py:255
  1461.0 480.8 %reduce-scatter.16.cloned.1.call-start = ((), (), s32[]{:S(2)}) async-start(), calls=%async_computation.23 | async-start | bytes 10485760 | tf_op jit(solution)/shard_map/reduce_scatter | solution.py:256
  1466.7 33.0 copy-start.12
  1466.7 623.1 %reduce-scatter.18.cloned.1.call-start = ((), (), s32[]{:S(2)}) async-start(), calls=%async_computation.24 | async-start | bytes 10485760 | tf_op jit(solution)/shard_map/reduce_scatter | solution.py:257
  1505.5 1139.4 %reduce-scatter.22.cloned.1.call-start = ((), (), s32[]{:S(2)}) async-start(), calls=%async_computation.26 | async-start | bytes 41943040 | tf_op jit(solution)/shard_map/reduce_scatter | solution.py:225
  1520.1 1680.1 %reduce-scatter.24.cloned.1.call-start = ((), (), s32[]{:S(2)}) async-start(), calls=%async_computation.27 | async-start | bytes 41943040 | tf_op jit(solution)/shard_map/reduce_scatter | solution.py:226
  1534.6 2220.6 %reduce-scatter.26.cloned.1.call-start = ((), (), s32[]{:S(2)}) async-start(), calls=%async_computation.28 | async-start | bytes 41943040 | tf_op jit(solution)/shard_map/reduce_scatter | solution.py:227
  1550.3 9.9 copy-start.15
  1550.3 2230.0 %all-reduce.17.cloned.1.call-start = ((), (), s32[]{:S(2)}) async-start(), calls=%async_computation.30 | async-start | bytes 4194304 | tf_op jit(solution)/shard_map/psum | solution.py:206
  1550.5 9.7 copy-start.6
  1560.2 2.4 copy-start.5
  1567.5 2806.3 %all-reduce.15.cloned.1.call-start = ((), (), s32[]{:S(2)}) async-start(), calls=%async_computation.29 | async-start | bytes 67108864 | tf_op jit(solution)/shard_map/psum | solution.py:261
  3755.2 25.1 copy-start.3
  3755.2 25.1 copy-start.25
  3755.2 25.1 copy-start.27
  4373.8 3.3 copy-start.19
  4373.8 4.6 copy-start.18
  4377.1 2.6 copy-start.17
  4379.8 9.8 slice-start.2
  4381.1 8.5 slice-start.3
  4381.1 12.7 slice-start
  4389.6 5.2 slice-start.1
  4394.8 3.4 copy-start.1
  (8 other events, 11.0 us)
Sparse Core Ops, SparseCore 0:
  9.6 83.4 all-gather.13
  94.7 79.2 all-gather.11
  175.6 79.2 all-gather.17
  256.9 26.4 all-gather.15
  285.4 27.4 all-gather.19
  314.3 80.2 all-gather.21
  398.6 18.1 all-reduce.10
  418.4 287.9 all-gather.23
  708.1 284.9 all-gather.25
  994.6 284.9 all-gather.27
  1320.0 17.7 all-reduce.12
  1408.5 45.0 reduce-scatter.9
  1456.5 43.1 reduce-scatter.11
  1501.9 143.7 reduce-scatter.19
  1648.6 145.1 reduce-scatter.13
  1796.6 145.1 reduce-scatter.15
  1944.6 145.1 reduce-scatter.17
  2092.0 552.7 reduce-scatter.21
  2647.3 552.7 reduce-scatter.23
  3202.4 552.7 reduce-scatter.25
  3758.2 22.0 all-reduce.16
  3785.0 588.7 all-reduce.14
where the time goes:
time: 4410 us
  waiting for transfers between devices  4030 us (91%)
  matrix products  206 us (5%)
  local copies, waits for them, and re-layouts  71.1 us (2%)
  blocking collectives  55.2 us (1%)
    psum x1, waiting for transfers between devices, shards(): lax.psum((share_gain_one, share_query, share_key, share_value, share_out,...  557 us
    reduce_scatter x1, waiting for transfers between devices, shards(): lax.psum_scatter(grad_up_w, 'cp', scatter_dimension=0, tiled=True)  555 us
    reduce_scatter x1, waiting for transfers between devices, shards(): lax.psum_scatter(grad_gate_w, 'cp', scatter_dimension=0, tiled=True)  555 us
    reduce_scatter x1, waiting for transfers between devices, shards(): lax.psum_scatter(grad_down, 'cp', scatter_dimension=1, tiled=True)  555 us
    all_gather x1, waiting for transfers between devices, shards(): lax.all_gather(w_gate, 'cp', axis=0, tiled=True)  288 us
    all_gather x1, waiting for transfers between devices, shards(): lax.all_gather(w_up, 'cp', axis=0, tiled=True)  277 us
    all_gather x1, waiting for transfers between devices, shards(): lax.all_gather(w_down, 'cp', axis=1, tiled=True)  277 us
    reduce_scatter x1, waiting for transfers between devices, shards(): lax.psum_scatter(grad_key_w, 'cp', scatter_dimension=0, tiled=True)  148 us
  transfers between devices with their start and end apart: 22, of which 22 were waited for; matrix products, arithmetic and copies ran while one was open for 4% of the time, Pallas kernels for 0%

commit v1 on v0

--- a/solution.py
+++ b/solution.py
@@ -1,16 +1,936 @@
+import functools
 import math
 
 import jax
 import jax.numpy as jnp
 from jax import lax
+from jax.experimental import pallas as pl
+from jax.experimental.pallas import tpu as pltpu
 from jax.sharding import PartitionSpec as P
 
 HEAD_DIM = 128
-
-
 EPS = 1e-05
 SHIFT = math.log(4096.0)
 ROPE_BASE = 10000.0
+BF = jnp.bfloat16
+F32 = jnp.float32
+MESH = pl.DeviceIdType.MESH
+ANY = pl.ANY
+VMEM = pltpu.VMEM
+MIB = 2**20
+
+
+class Net:
+    def __init__(self, zs, send_sems, recv_sems):
+        self.zs = zs
+        self.dp, self.z, self.t = (lax.axis_index(a) for a in ("dp", "cp", "tp"))
+        self.a, self.b = lax.div(self.dp, 2), lax.rem(self.dp, 2)
+        self.send_sems, self.recv_sems = send_sems, recv_sems
+        self.used = 0
+        self.open = []
+
+    def along_z(self, s):
+        return (self.dp, lax.rem(self.z + s, self.zs), self.t)
+
+    def source_z(self, s):
+        return lax.rem(self.z + self.zs - s, self.zs)
+
+    @property
+    def over_x(self):
+        return (2 * self.a + 1 - self.b, self.z, self.t)
+
+    @property
+    def over_y(self):
+        return (2 * (1 - self.a) + self.b, self.z, self.t)
+
+    @property
+    def sibling(self):
+        return (self.dp, self.z, 1 - self.t)
+
+    def meet(self, y=True):
+        ways = [self.along_z(s) for s in range(1, self.zs)] + [self.over_x, self.sibling]
+        if y:
+            ways.append(self.over_y)
+        barrier = pltpu.get_barrier_semaphore()
+        for way in ways:
+            pl.semaphore_signal(barrier, inc=1, device_id=way, device_id_type=MESH)
+        pl.semaphore_wait(barrier, len(ways))
+
+    def send(self, src, dst, way):
+        k = self.used
+        self.used += 1
+        copy = pltpu.make_async_remote_copy(
+            src, dst, self.send_sems.at[k], self.recv_sems.at[k], device_id=way, device_id_type=MESH
+        )
+        copy.start()
+        self.open.append(copy)
+        return copy
+
+    def keep(self, src, dst):
+        k = self.used
+        self.used += 1
+        copy = pltpu.make_async_copy(src, dst, self.send_sems.at[k])
+        copy.start()
+        return copy
+
+    def finish(self):
+        for copy in self.open:
+            copy.wait_send()
+        self.open = []
+
+
+def plane_start(net, place, halves):
+    own = place(net.dp)
+    return net.send(own, own, net.over_x), net.send(own, own, net.over_y)
+
+
+def plane_relay(net, place, halves, over_x, over_y, sibling=None):
+    dx, dy = 2 * net.a + 1 - net.b, 2 * (1 - net.a) + net.b
+    dd = 2 * (1 - net.a) + 1 - net.b
+    waits = []
+    over_x.wait_recv()
+    first = halves(place(dx), 0)
+    up = net.send(first, first, net.over_y)
+    if sibling:
+        waits.append(sibling(dx))
+    over_y.wait_recv()
+    second = halves(place(dy), 1)
+    side = net.send(second, second, net.over_x)
+    if sibling:
+        waits.append(sibling(dy))
+    return up, side, dd, waits
+
+
+def plane_end(net, place, halves, state, sibling=None):
+    up, side, dd, waits = state
+    up.wait_recv()
+    side.wait_recv()
+    if sibling:
+        waits.append(sibling(dd))
+    return waits
+
+
+def rows_loop(count, step, body):
+    def one(i, carry):
+        body(pl.ds(pl.multiple_of(i * step, step), step))
+        return carry
+
+    lax.fori_loop(0, count // step, one, 0)
+
+
+def add_rows(out, terms, rows):
+    def body(at):
+        total = terms[0][at, :].astype(F32)
+        for term in terms[1:]:
+            total += term[at, :].astype(F32)
+        out[at, :] = total.astype(out.dtype)
+
+    rows_loop(rows, 16, body)
+
+
+class GatherAll:
+    def __init__(self, net, src, dst):
+        self.net, self.src, self.dst = net, src, dst
+        rows = src.shape[0] // 2
+        self.halves = lambda ref, k: ref.at[pl.ds(k * rows, rows)]
+
+    def place(self, dp, z):
+        return self.dst.at[dp, z, self.net.t]
+
+    def start(self):
+        net = self.net
+        mine = self.place(net.dp, net.z)
+        self.local = net.keep(self.src, mine)
+        self.z_sends = [net.send(self.src, mine, net.along_z(s)) for s in range(1, net.zs)]
+        self.plane = [(net.z, net.send(self.src, mine, net.over_x), net.send(self.src, mine, net.over_y))]
+        self.twin = [net.send(self.src, mine, net.sibling)]
+
+    def to_twin(self, dp, z):
+        ref = self.place(dp, z)
+        self.twin.append(self.net.send(ref, ref, self.net.sibling))
+
+    def spread(self):
+        net = self.net
+        for s in range(1, net.zs):
+            self.z_sends[s - 1].wait_recv()
+            z = net.source_z(s)
+            ref = self.place(net.dp, z)
+            self.plane.append((z, net.send(ref, ref, net.over_x), net.send(ref, ref, net.over_y)))
+            self.to_twin(net.dp, z)
+
+    def relay(self):
+        net = self.net
+        self.states = []
+        for z, over_x, over_y in self.plane:
+            place = functools.partial(self.place, z=z)
+            self.states.append(
+                (z, plane_relay(net, place, self.halves, over_x, over_y, lambda dp, z=z: self.to_twin(dp, z)))
+            )
+
+    def end(self):
+        for z, state in self.states:
+            place = functools.partial(self.place, z=z)
+            plane_end(self.net, place, self.halves, state, lambda dp, z=z: self.to_twin(dp, z))
+        for copy in self.twin:
+            copy.wait_recv()
+        self.local.wait()
+
+
+class GatherGroup:
+    def __init__(self, net, src, dst):
+        self.net, self.src, self.dst = net, src, dst
+
+    def place(self, b, z):
+        return self.dst.at[b, z, self.net.t]
+
+    def start(self):
+        net = self.net
+        mine = self.place(net.b, net.z)
+        self.local = net.keep(self.src, mine)
+        self.z_sends = [net.send(self.src, mine, net.along_z(s)) for s in range(1, net.zs)]
+        self.over = [(net.z, net.send(self.src, mine, net.over_x))]
+        self.twin = [net.send(self.src, mine, net.sibling)]
+
+    def to_twin(self, b, z):
+        ref = self.place(b, z)
+        self.twin.append(self.net.send(ref, ref, self.net.sibling))
+
+    def spread(self):
+        net = self.net
+        for s in range(1, net.zs):
+            self.z_sends[s - 1].wait_recv()
+            z = net.source_z(s)
+            ref = self.place(net.b, z)
+            self.over.append((z, net.send(ref, ref, net.over_x)))
+            self.to_twin(net.b, z)
+
+    def end(self):
+        net = self.net
+        for z, copy in self.over:
+            copy.wait_recv()
+            self.to_twin(1 - net.b, z)
+        for copy in self.twin:
+            copy.wait_recv()
+        self.local.wait()
+
+
+class SumGroup:
+    def __init__(self, net, part, own, sib, far, landed):
+        self.net, self.part, self.own, self.sib, self.far, self.landed = net, part, own, sib, far, landed
+        self.rows = part.shape[3]
+
+    def start(self):
+        net = self.net
+        self.twin, self.mine = [], []
+        for s in range(net.zs):
+            z = lax.rem(net.z + s + 1, net.zs)
+            for b in (1 - net.b, net.b):
+                self.twin.append(net.send(self.part.at[b, z, 1 - net.t], self.sib.at[b, z], net.sibling))
+                self.mine.append(net.keep(self.part.at[b, z, net.t], self.own.at[b, z]))
+
+    def run(self):
+        net = self.net
+        over = []
+        for s in range(net.zs):
+            z = lax.rem(net.z + s + 1, net.zs)
+            for j, b in enumerate((1 - net.b, net.b)):
+                self.twin[2 * s + j].wait_recv()
+                self.mine[2 * s + j].wait()
+                add_rows(self.own.at[b, z], [self.own.at[b, z], self.sib.at[b, z]], self.rows)
+                if j == 0:
+                    over.append(net.send(self.own.at[b, z], self.far.at[z], net.over_x))
+        self.z_sends = []
+        for s in range(net.zs):
+            z = lax.rem(net.z + s + 1, net.zs)
+            over[s].wait_recv()
+            out = self.landed.at[net.z] if s == net.zs - 1 else self.own.at[net.b, z]
+            add_rows(out, [self.own.at[net.b, z], self.far.at[z]], self.rows)
+            if s < net.zs - 1:
+                self.z_sends.append(net.send(out, self.landed.at[net.z], net.along_z(s + 1)))
+
+    def end(self):
+        for copy in self.z_sends:
+            copy.wait_recv()
+
+
+class SumAll:
+    def __init__(self, net, part, own, sib, one, two, landed):
+        self.net, self.part, self.own, self.sib = net, part, own, sib
+        self.one, self.two, self.landed = one, two, landed
+        self.half = part.shape[3] // 2
+
+    def order(self):
+        net = self.net
+        return [lax.rem(net.z + s + 1, net.zs) for s in range(net.zs)]
+
+    def places(self):
+        a, b = self.net.a, self.net.b
+        return [2 * (1 - a) + 1 - b, 2 * a + 1 - b, 2 * (1 - a) + b, 2 * a + b]
+
+    def start(self):
+        net = self.net
+        self.twin, self.mine = [], []
+        for z in self.order():
+            for dp in self.places():
+                self.twin.append(net.send(self.part.at[dp, z, 1 - net.t], self.sib.at[dp, z], net.sibling))
+                self.mine.append(net.keep(self.part.at[dp, z, net.t], self.own.at[dp, z]))
+
+    def upper(self, ref):
+        return ref.at[pl.ds(0, self.half)]
+
+    def lower(self, ref):
+        return ref.at[pl.ds(self.half, self.half)]
+
+    def first(self, s):
+        net = self.net
+        z = self.order()[s]
+        dd, dx, dy, me = self.places()
+        for j, dp in enumerate((dd, dx, dy, me)):
+            self.twin[4 * s + j].wait_recv()
+            self.mine[4 * s + j].wait()
+            add_rows(self.own.at[dp, z], [self.own.at[dp, z], self.sib.at[dp, z]], 2 * self.half)
+        self.ones = getattr(self, "ones", [])
+        self.ones.append(
+            (
+                net.send(self.upper(self.own.at[dd, z]), self.one.at[0, 0, z], net.over_x),
+                net.send(self.upper(self.own.at[dx, z]), self.one.at[0, 1, z], net.over_x),
+                net.send(self.lower(self.own.at[dd, z]), self.one.at[1, 0, z], net.over_y),
+                net.send(self.lower(self.own.at[dy, z]), self.one.at[1, 1, z], net.over_y),
+            )
+        )
+
+    def second(self, s):
+        net = self.net
+        z = self.order()[s]
+        dd, dx, dy, me = self.places()
+        x_dd, x_me, y_dd, y_me = self.ones[s]
+        self.twos = getattr(self, "twos", [])
+        x_dd.wait_recv()
+        out = self.upper(self.own.at[dy, z])
+        add_rows(out, [out, self.one.at[0, 0, z]], self.half)
+        up = net.send(out, self.two.at[0, z], net.over_y)
+        y_dd.wait_recv()
+        out = self.lower(self.own.at[dx, z])
+        add_rows(out, [out, self.one.at[1, 0, z]], self.half)
+        side = net.send(out, self.two.at[1, z], net.over_x)
+        self.twos.append((up, side))
+
+    def third(self, s):
+        net = self.net
+        z = self.order()[s]
+        dd, dx, dy, me = self.places()
+        _, x_me, _, y_me = self.ones[s]
+        up, side = self.twos[s]
+        last = s == net.zs - 1
+        out = self.landed.at[net.z] if last else self.own.at[me, z]
+        x_me.wait_recv()
+        up.wait_recv()
+        mine = self.own.at[me, z]
+        add_rows(self.upper(out), [self.upper(mine), self.one.at[0, 1, z], self.two.at[0, z]], self.half)
+        y_me.wait_recv()
+        side.wait_recv()
+        add_rows(self.lower(out), [self.lower(mine), self.one.at[1, 1, z], self.two.at[1, z]], self.half)
+        self.z_sends = getattr(self, "z_sends", [])
+        if not last:
+            self.z_sends.append(net.send(out, self.landed.at[net.z], net.along_z(s + 1)))
+
+    def end(self):
+        for copy in self.z_sends:
+            copy.wait_recv()
+
+
+class SpreadGrads:
+    def __init__(self, net, src, dst, halves):
+        self.net, self.src, self.dst, self.halves = net, src, dst, halves
+
+    def start(self):
+        net = self.net
+        mine = self.dst(net.dp, net.z)
+        self.local = net.keep(self.src(net.z), mine)
+        self.z_sends = [
+            net.send(self.src(lax.rem(net.z + s, net.zs)), mine, net.along_z(s)) for s in range(1, net.zs)
+        ]
+        self.plane = [
+            (net.z, net.send(self.src(net.z), mine, net.over_x), net.send(self.src(net.z), mine, net.over_y))
+        ]
+        self.states = []
+
+    def spread(self, s):
+        net = self.net
+        self.z_sends[s - 1].wait_recv()
+        z = net.source_z(s)
+        ref = self.dst(net.dp, z)
+        self.plane.append((z, net.send(ref, ref, net.over_x), net.send(ref, ref, net.over_y)))
+
+    def relay(self, s):
+        z, over_x, over_y = self.plane[s]
+        place = lambda dp: self.dst(dp, z)
+        self.states.append(plane_relay(self.net, place, self.halves, over_x, over_y))
+
+    def end(self):
+        for state in self.states:
+            plane_end(self.net, None, self.halves, state)
+        self.local.wait()
+
+
+def call(kernel, name, outs, scratch, count, args, spaces=None, vmem=40):
+    spaces = spaces or [ANY] * len(args)
+    return pl.pallas_call(
+        kernel,
+        out_shape=[jax.ShapeDtypeStruct(shape, kind) for shape, kind, _ in outs],
+        in_specs=[pl.BlockSpec(memory_space=space) for space in spaces],
+        out_specs=[pl.BlockSpec(memory_space=space) for _, _, space in outs],
+        scratch_shapes=list(scratch) + [pltpu.SemaphoreType.DMA((count,)), pltpu.SemaphoreType.DMA((count,))],
+        compiler_params=pltpu.CompilerParams(
+            collective_id=name, has_side_effects=True, vmem_limit_bytes=vmem * MIB
+        ),
+    )(*args)
+
+
+def open_kernel(zs, x, wq, wk, wv, wo, small, x_all, qkv_w, out_w, small_z, small_x, send_sems, recv_sems):
+    net = Net(zs, send_sems, recv_sems)
+    net.meet(y=False)
+    deep = wq.shape[0]
+    gather = GatherGroup(net, x.at[net.t], x_all)
+    gather.start()
+    waits, local = [], []
+
+    def cols(w, z):
+        return w.at[:, pl.ds(pl.multiple_of((net.b * zs + z) * HEAD_DIM, HEAD_DIM), HEAD_DIM)]
+
+    def rows(z):
+        return wo.at[pl.ds(pl.multiple_of((net.b * zs + z) * HEAD_DIM, HEAD_DIM), HEAD_DIM)]
+
+    mine = pl.ds(pl.multiple_of(net.z * deep, deep), deep)
+    for s in range(1, zs):
+        waits.append(net.send(small, small_z.at[net.z], net.along_z(s)))
+    waits.append(net.send(small, small_x.at[net.b], net.over_x))
+    local.append(net.keep(small, small_z.at[net.z]))
+    local.append(net.keep(small, small_x.at[net.b]))
+    for m, w in enumerate((wq, wk, wv)):
+        dst = qkv_w.at[mine, pl.ds(m * HEAD_DIM, HEAD_DIM)]
+        local.append(net.keep(cols(w, net.z), dst))
+        for s in range(1, zs):
+            waits.append(net.send(cols(w, lax.rem(net.z + s, zs)), dst, net.along_z(s)))
+    dst = out_w.at[:, mine]
+    local.append(net.keep(rows(net.z), dst))
+    for s in range(1, zs):
+        waits.append(net.send(rows(lax.rem(net.z + s, zs)), dst, net.along_z(s)))
+    gather.spread()
+    gather.end()
+    for copy in waits:
+        copy.wait_recv()
+    for copy in local:
+        copy.wait()
+    net.finish()
+
+
+def middle_kernel(
+    zs, part, x, gain, wg, wu, wd, cot, middle, h2_all, cot_all, gu_w, down_w,
+    own, sib, far, landed, x_lane, h2, gain_v, mid_v, send_sems, recv_sems,
+):
+    net = Net(zs, send_sems, recv_sems)
+    net.meet()
+    deep, wide = wg.shape[0], gu_w.shape[1] // 2
+    branch = SumGroup(net, part, own, sib, far, landed)
+    branch.start()
+    lane = net.keep(x.at[net.t], x_lane)
+    gains = net.keep(gain, gain_v)
+    waits, local = [], []
+    mine = pl.ds(pl.multiple_of(net.z * deep, deep), deep)
+
+    def block(z):
+        return pl.ds(pl.multiple_of((net.dp * zs + z) * wide, wide), wide)
+
+    def fetch(s, z):
+        srcs = (wg.at[:, block(z)], wu.at[:, block(z)], wd.at[block(z)])
+        dsts = (gu_w.at[mine, pl.ds(0, wide)], gu_w.at[mine, pl.ds(wide, wide)], down_w.at[:, mine])
+        for src, dst in zip(srcs, dsts, strict=True):
+            if s == 0:
+                local.append(net.keep(src, dst))
+            else:
+                waits.append(net.send(src, dst, net.along_z(s)))
+
+    fetch(0, net.z)
+    branch.run()
+    for s in range(1, zs):
+        fetch(s, lax.rem(net.z + s, zs))
+    lane.wait()
+    gains.wait()
+    branch.end()
+    rows, width = x_lane.shape
+
+    def body(at):
+        total = x_lane[at, :].astype(F32)
+        for z in range(zs):
+            total += landed[z, at, :].astype(F32)
+        mid_v[at, :] = total
+        inverse = lax.rsqrt(jnp.mean(total * total, axis=-1, keepdims=True) + EPS)
+        h2[at, :] = (total * inverse * gain_v[0:1, :]).astype(BF)
+
+    rows_loop(rows, 16, body)
+    out = net.keep(mid_v, middle)
+    hidden = GatherAll(net, h2, h2_all)
+    hidden.start()
+    cotan = GatherAll(net, cot.at[net.t], cot_all)
+    cotan.start()
+    hidden.spread()
+    hidden.relay()
+    cotan.spread()
+    cotan.relay()
+    hidden.end()
+    cotan.end()
+    out.wait()
+    for copy in waits:
+        copy.wait_recv()
+    for copy in local:
+        copy.wait()
+    net.finish()
+
+
+def back_kernel(
+    zs, gh_part, feed_part, gu_grad, down_grad, middle, cot, gain,
+    gbr_all, grad_mid, layer_out, gain_part, gate_out, up_out, down_out,
+    own, sib, one, two, landed, own_f, sib_f, one_f, two_f, landed_f, mid_v, cot_v, gain_v, gm_v, gbr_v, gsum_v, lo_v,
+    send_sems, recv_sems,
+):
+    net = Net(zs, send_sems, recv_sems)
+    net.meet()
+    wide = gu_grad.shape[1] // 2
+    deep = gate_out.shape[0]
+    hidden = SumAll(net, gh_part, own, sib, one, two, landed)
+    hidden.start()
+    feed = SumAll(net, feed_part, own_f, sib_f, one_f, two_f, landed_f)
+    feed.start()
+    local = [net.keep(middle, mid_v), net.keep(cot.at[net.t], cot_v), net.keep(gain, gain_v)]
+
+    def block(dp, z):
+        return pl.ds(pl.multiple_of((dp * zs + z) * wide, wide), wide)
+
+    def deep_rows(z):
+        return pl.ds(pl.multiple_of(z * deep, deep), deep)
+
+    def half_rows(ref, k):
+        n = ref.shape[0] // 2
+        return ref.at[pl.ds(k * n, n)]
+
+    grads = [
+        SpreadGrads(
+            net,
+            lambda z: gu_grad.at[deep_rows(z), pl.ds(0, wide)],
+            lambda dp, z: gate_out.at[:, block(dp, z)],
+            half_rows,
+        ),
+        SpreadGrads(
+            net,
+            lambda z: gu_grad.at[deep_rows(z), pl.ds(wide, wide)],
+            lambda dp, z: up_out.at[:, block(dp, z)],
+            half_rows,
+        ),
+        SpreadGrads(
+            net,
+            lambda z: down_grad.at[:, deep_rows(z)],
+            lambda dp, z: down_out.at[block(dp, z)],
+            half_rows,
+        ),
+    ]
+    for s in range(zs):
+        hidden.first(s)
+    for s in range(zs):
+        hidden.second(s)
+    for s in range(zs):
+        hidden.third(s)
+    for grad in grads:
+        grad.start()
+    for s in range(zs):
+        feed.first(s)
+    for copy in local:
+        copy.wait()
+    hidden.end()
+    rows = mid_v.shape[0]
+    gsum_v[...] = jnp.zeros_like(gsum_v)
+
+    def body(at):
+        mid = mid_v[at, :]
+        inverse = lax.rsqrt(jnp.mean(mid * mid, axis=-1, keepdims=True) + EPS)
+        normed = mid * inverse
+        total = landed[0, at, :].astype(F32)
+        for z in range(1, zs):
+            total += landed[z, at, :].astype(F32)
+        prod = total * normed
+        gsum_v[...] += prod[0:8, :] + prod[8:16, :]
+        scaled = total * gain_v[0:1, :]
+        grad = cot_v[at, :].astype(F32) + inverse * (
+            scaled - normed * jnp.mean(scaled * normed, axis=-1, keepdims=True)
+        )
+        gm_v[at, :] = grad
+        gbr_v[at, :] = grad.astype(BF)
+
+    rows_loop(rows, 16, body)
+    gather = GatherGroup(net, gbr_v, gbr_all)
+    gather.start()
+    outs = [net.keep(gm_v, grad_mid), net.keep(gsum_v, gain_part)]
+    for s in range(zs):
+        feed.second(s)
+    gather.spread()
+    for s in range(zs):
+        feed.third(s)
+    gather.end()
+    for s in range(1, zs):
+        for grad in grads:
+            grad.spread(s)
+    for grad in grads:
+        grad.relay(0)
+    feed.end()
+
+    def close(at):
+        total = mid_v[at, :]
+        for z in range(zs):
+            total += landed_f[z, at, :].astype(F32)
+        lo_v[at, :] = total.astype(BF)
+
+    rows_loop(rows, 16, close)
+    outs.append(net.keep(lo_v, layer_out.at[net.t]))
+    last = net.send(lo_v, layer_out.at[net.t], net.sibling)
+    for s in range(1, zs):
+        for grad in grads:
+            grad.relay(s)
+    for grad in grads:
+        grad.end()
+    last.wait_recv()
+    for copy in outs:
+        copy.wait()
+    net.finish()
+
+
+def close_kernel(
+    zs, gh_part, qkv_grad, out_grad, grad_mid, x, gain, gain_part,
+    input_grad, q_out, k_out, v_out, o_out, gains_out,
+    own, sib, far, landed, x_v, gain_v, gm_v, gsum_v, gi_v, q_own, q_far, o_own, o_far, g_far, g_land,
+    send_sems, recv_sems,
+):
+    net = Net(zs, send_sems, recv_sems)
+    net.meet()
+    deep = q_out.shape[0]
+    half = deep // 2
+    hidden = SumGroup(net, gh_part, own, sib, far, landed)
+    local = [
+        net.keep(grad_mid, gm_v), net.keep(x.at[net.t], x_v), net.keep(gain, gain_v),
+        net.keep(gain_part, gsum_v.at[1]),
+    ]
+    sums = []
+    for s in range(zs):
+        z = lax.rem(net.z + s + 1, zs)
+        at = lambda a: pl.ds(pl.multiple_of(z * deep + a * half, half), half)
+        oc = pl.ds(pl.multiple_of(z * deep, deep), deep)
+        oh = HEAD_DIM // 2
+        orow = lambda a: pl.ds(pl.multiple_of(a * oh, oh), oh)
+        sums.append(
+            (
+                z,
+                net.send(qkv_grad.at[at(1 - net.a)], q_far.at[z], net.over_y),
+                net.keep(qkv_grad.at[at(net.a)], q_own.at[z]),
+                net.send(out_grad.at[orow(1 - net.a), oc], o_far.at[z], net.over_y),
+                net.keep(out_grad.at[orow(net.a), oc], o_own.at[z]),
+            )
+        )
+    hidden.start()
+    hidden.run()
+
+    def half_rows(ref, k):
+        n = ref.shape[0] // 2
+        return ref.at[pl.ds(k * n, n)]
+
+    for z, q_in, q_mine, o_in, o_mine in sums:
+        q_in.wait_recv()
+        q_mine.wait()
+        add_rows(q_own.at[z], [q_own.at[z], q_far.at[z]], half)
+        o_in.wait_recv()
+        o_mine.wait()
+        add_rows(o_own.at[z], [o_own.at[z], o_far.at[z]], HEAD_DIM // 2)
+
+    def q_place(ref):
+        def place(dp, z):
+            a, b = lax.div(dp, 2), lax.rem(dp, 2)
+            return ref.at[
+                pl.ds(pl.multiple_of(a * half, half), half),
+                pl.ds(pl.multiple_of((b * zs + z) * HEAD_DIM, HEAD_DIM), HEAD_DIM),
+            ]
+
+        return place
+
+    def o_place(dp, z):
+        a, b = lax.div(dp, 2), lax.rem(dp, 2)
+        oh = HEAD_DIM // 2
+        return o_out.at[pl.ds(pl.multiple_of((b * zs + z) * HEAD_DIM + a * oh, oh), oh)]
+
+    grads = [
+        SpreadGrads(
+            net, lambda z, m=m: q_own.at[z, :, pl.ds(m * HEAD_DIM, HEAD_DIM)], q_place(ref), half_rows
+        )
+        for m, ref in enumerate((q_out, k_out, v_out))
+    ]
+    grads.append(SpreadGrads(net, lambda z: o_own.at[z], o_place, half_rows))
+    for grad in grads:
+        grad.start()
+    for copy in local:
+        copy.wait()
+    hidden.end()
+    rows = x_v.shape[0]
+    gsum_v[0] = jnp.zeros_like(gsum_v[0])
+
+    def body(at):
+        inputs = x_v[at, :].astype(F32)
+        inverse = lax.rsqrt(jnp.mean(inputs * inputs, axis=-1, keepdims=True) + EPS)
+        normed = inputs * inverse
+        total = landed[0, at, :].astype(F32)
+        for z in range(1, zs):
+            total += landed[z, at, :].astype(F32)
+        prod = total * normed
+        gsum_v[0] += prod[0:8, :] + prod[8:16, :]
+        scaled = total * gain_v[0:1, :]
+        grad = gm_v[at, :] + inverse * (scaled - normed * jnp.mean(scaled * normed, axis=-1, keepdims=True))
+        gi_v[at, :] = grad.astype(BF)
+
+    rows_loop(rows, 16, body)
+    out = net.keep(gi_v, input_grad.at[net.t])
+    last = net.send(gi_v, input_grad.at[net.t], net.sibling)
+    for k, way in enumerate((net.sibling, net.over_x, net.over_y)):
+        swap = net.send(gsum_v, g_far.at[k], way)
+        swap.wait()
+        net.open = [c for c in net.open if c is not swap]
+        gsum_v[...] = gsum_v[...] + g_far[k]
+    cut = lambda z: gsum_v.at[:, :, pl.ds(pl.multiple_of(z * deep, deep), deep)]
+    z_gain = [net.send(cut(lax.rem(net.z + s, zs)), g_land.at[net.z], net.along_z(s)) for s in range(1, zs)]
+    keep = net.keep(cut(net.z), g_land.at[net.z])
+    for s in range(1, zs):
+        for grad in grads:
+            grad.spread(s)
+    for s in range(zs):
+        for grad in grads:
+            grad.relay(s)
+    for grad in grads:
+        grad.end()
+    keep.wait()
+    for copy in z_gain:
+        copy.wait_recv()
+    total = g_land[0]
+    for z in range(1, zs):
+        total += g_land[z]
+    gains_out[...] = total
+    last.wait_recv()
+    out.wait()
+    net.finish()
+
+
+def rope_tables(positions):
+    half_dim = HEAD_DIM // 2
+    frequency = ROPE_BASE ** (-jnp.arange(half_dim, dtype=F32) / half_dim)
+    angle = positions.astype(F32)[:, None] * frequency[None, :]
+    return jnp.cos(angle), jnp.sin(angle)
+
+
+def turn(u, cosine, sine):
+    first, second = u[..., : HEAD_DIM // 2], u[..., HEAD_DIM // 2 :]
+    return jnp.concatenate([first * cosine - second * sine, second * cosine + first * sine], axis=-1)
+
+
+def dot(left, right, dims=((1,), (0,)), kind=F32):
+    return lax.dot_general(left, right, (dims, ((), ())), preferred_element_type=F32).astype(kind)
+
+
+def bdot(left, right, dims):
+    return lax.dot_general(left, right, (dims, ((0,), (0,))), preferred_element_type=F32)
+
+
+def heads_shards(
+    zs, activations, document_ids, attn_gain, w_query, w_key, w_value, w_out, mlp_gain, w_gate, w_up, w_down, cotangent
+):
+    stretch, width = activations.shape[3:]
+    deep = w_query.shape[0]
+    seq = document_ids.shape[1]
+    tokens = zs * 2 * stretch
+    wide = w_gate.shape[1] // (4 * zs)
+    x = activations.reshape(2, stretch, width)
+    cot = cotangent.reshape(2, stretch, width)
+    small = jnp.stack([attn_gain.astype(F32), mlp_gain.astype(F32)])
+    docs_rows = document_ids.astype(F32).reshape(seq // deep, deep)
+    small = jnp.concatenate([small, docs_rows, jnp.zeros((6 - seq // deep, deep), F32)])
+    x_all, qkv_w, out_w, small_z, small_x = call(
+        functools.partial(open_kernel, zs),
+        1,
+        [
+            ((2, zs, 2, stretch, width), BF, ANY),
+            ((width, 3 * HEAD_DIM), BF, ANY),
+            ((HEAD_DIM, width), BF, ANY),
+            ((zs, 8, deep), F32, ANY),
+            ((2, 8, deep), F32, ANY),
+        ],
+        [],
+        64,
+        (x, w_query, w_key, w_value, w_out, small),
+    )
+    gain_one = small_z[:, 0].reshape(1, width)
+    gain_two = small_z[:, 1].reshape(1, width)
+    docs = small_x[:, 2 : 2 + seq // deep].reshape(2, seq)
+    slots = jnp.arange(tokens, dtype=jnp.int32)
+    owners = slots // (2 * stretch)
+    halves = slots // stretch % 2
+    places = jnp.where(halves == 0, owners, 2 * zs - 1 - owners) * stretch + slots % stretch
+    cosine, sine = rope_tables(places)
+    docs = jnp.take(docs, places, axis=1)
+    visible = (docs[:, :, None] == docs[:, None, :]) & (places[None, None, :] <= places[None, :, None])
+
+    flat = x_all.reshape(2 * tokens, width).astype(F32)
+    inverse = lax.rsqrt(jnp.mean(flat * flat, axis=-1, keepdims=True) + EPS)
+    hidden = (flat * inverse * gain_one).astype(BF)
+    qkv = dot(hidden, qkv_w).reshape(2, tokens, 3, HEAD_DIM)
+    queries = turn(qkv[:, :, 0], cosine, sine).astype(BF)
+    keys = turn(qkv[:, :, 1], cosine, sine).astype(BF)
+    values = qkv[:, :, 2].astype(BF)
+    scale = HEAD_DIM**-0.5
+    sigma = jax.nn.sigmoid(bdot(queries, keys, ((2,), (2,))) * scale - SHIFT)
+    weights = jnp.where(visible, sigma, 0.0).astype(BF)
+    attended = bdot(weights, values, ((2,), (1,))).astype(BF).reshape(2 * tokens, HEAD_DIM)
+    part = dot(attended, out_w, kind=BF).reshape(2, zs, 2, stretch, width)
+
+    middle, h2_all, cot_all, gu_w, down_w = call(
+        functools.partial(middle_kernel, zs),
+        2,
+        [
+            ((stretch, width), F32, ANY),
+            ((4, zs, 2, stretch, width), BF, ANY),
+            ((4, zs, 2, stretch, width), BF, ANY),
+            ((width, 2 * wide), BF, ANY),
+            ((wide, width), BF, ANY),
+        ],
+        [
+            VMEM((2, zs, stretch, width), BF),
+            VMEM((2, zs, stretch, width), BF),
+            VMEM((zs, stretch, width), BF),
+            VMEM((zs, stretch, width), BF),
+            VMEM((stretch, width), BF),
+            VMEM((stretch, width), BF),
+            VMEM((8, width), F32),
+            VMEM((stretch, width), F32),
+        ],
+        160,
+        (part, x, jnp.broadcast_to(gain_two, (8, width)), w_gate, w_up, w_down, cot),
+    )
+
+    h2 = h2_all.reshape(4 * tokens, width)
+    cots = cot_all.reshape(4 * tokens, width)
+    gate_up = dot(h2, gu_w)
+    gate, upward = gate_up[:, :wide], gate_up[:, wide:]
+    grad_product = dot(cots, down_w, ((1,), (1,)))
+    sigma_gate = jax.nn.sigmoid(gate)
+    silu = gate * sigma_gate
+    product = (silu * upward).astype(BF)
+    grad_gate = (grad_product * upward * sigma_gate * (1.0 + gate * (1.0 - sigma_gate))).astype(BF)
+    grad_up = (grad_product * silu).astype(BF)
+    grad_gu = jnp.concatenate([grad_gate, grad_up], axis=1)
+    gh_part = dot(grad_gu, gu_w, ((1,), (1,)), BF).reshape(4, zs, 2, stretch, width)
+    feed_part = dot(product, down_w, kind=BF).reshape(4, zs, 2, stretch, width)
+    gu_grad = dot(h2, grad_gu, ((0,), (0,)), BF)
+    down_grad = dot(product, cots, ((0,), (0,)), BF)
+
+    half = stretch // 2
+    sum_scratch = [
+        VMEM((4, zs, stretch, width), BF),
+        VMEM((4, zs, stretch, width), BF),
+        VMEM((2, 2, zs, half, width), BF),
+        VMEM((2, zs, half, width), BF),
+        VMEM((zs, stretch, width), BF),
+    ]
+    gbr_all, grad_mid, layer_out, gain_part, gate_g, up_g, down_g = call(
+        functools.partial(back_kernel, zs),
+        3,
+        [
+            ((2, zs, 2, stretch, width), BF, ANY),
+            ((stretch, width), F32, ANY),
+            ((2, stretch, width), BF, ANY),
+            ((8, width), F32, ANY),
+            (w_gate.shape, BF, ANY),
+            (w_up.shape, BF, ANY),
+            (w_down.shape, BF, ANY),
+        ],
+        sum_scratch
+        + sum_scratch
+        + [
+            VMEM((stretch, width), F32),
+            VMEM((stretch, width), BF),
+            VMEM((8, width), F32),
+            VMEM((stretch, width), F32),
+            VMEM((stretch, width), BF),
+            VMEM((8, width), F32),
+            VMEM((stretch, width), BF),
+        ],
+        256,
+        (gh_part, feed_part, gu_grad, down_grad, middle, cot, jnp.broadcast_to(gain_two, (8, width))),
+        vmem=48,
+    )
+
+    grad_branch = gbr_all.reshape(2 * tokens, width)
+    grad_attended = dot(grad_branch, out_w, ((1,), (1,)), BF)
+    heads_grad = grad_attended.reshape(2, tokens, HEAD_DIM)
+    grad_weights = bdot(heads_grad, values, ((2,), (2,)))
+    grad_scores = jnp.where(visible, grad_weights * sigma * (1.0 - sigma), 0.0).astype(BF)
+    grad_queries = bdot(grad_scores, keys, ((2,), (1,))) * scale
+    grad_keys = bdot(grad_scores, queries, ((1,), (1,))) * scale
+    grad_values = bdot(weights, heads_grad, ((1,), (1,)))
+    grad_qkv = jnp.concatenate(
+        [turn(grad_queries, cosine, -sine), turn(grad_keys, cosine, -sine), grad_values], axis=-1
+    )
+    grad_qkv = grad_qkv.astype(BF).reshape(2 * tokens, 3 * HEAD_DIM)
+    gh_one = dot(grad_qkv, qkv_w, ((1,), (1,)), BF).reshape(2, zs, 2, stretch, width)
+    qkv_grad = dot(hidden, grad_qkv, ((0,), (0,)), BF)
+    out_grad = dot(attended, grad_branch, ((0,), (0,)), BF)
+
+    input_grad, q_g, k_g, v_g, o_g, gains_g = call(
+        functools.partial(close_kernel, zs),
+        4,
+        [
+            ((2, stretch, width), BF, ANY),
+            (w_query.shape, BF, ANY),
+            (w_key.shape, BF, ANY),
+            (w_value.shape, BF, ANY),
+            (w_out.shape, BF, ANY),
+            ((2, 8, deep), F32, VMEM),
+        ],
+        [
+            VMEM((2, zs, stretch, width), BF),
+            VMEM((2, zs, stretch, width), BF),
+            VMEM((zs, stretch, width), BF),
+            VMEM((zs, stretch, width), BF),
+            VMEM((stretch, width), BF),
+            VMEM((8, width), F32),
+            VMEM((stretch, width), F32),
+            VMEM((2, 8, width), F32),
+            VMEM((stretch, width), BF),
+            VMEM((zs, deep // 2, 3 * HEAD_DIM), BF),
+            VMEM((zs, deep // 2, 3 * HEAD_DIM), BF),
+            VMEM((zs, HEAD_DIM // 2, deep), BF),
+            VMEM((zs, HEAD_DIM // 2, deep), BF),
+            VMEM((3, 2, 8, width), F32),
+            VMEM((zs, 2, 8, deep), F32),
+        ],
+        160,
+        (gh_one, qkv_grad, out_grad, grad_mid, x, jnp.broadcast_to(gain_one, (8, width)), gain_part),
+    )
+    gain_grads = jnp.sum(gains_g, axis=1)
+    return (
+        layer_out.reshape(activations.shape),
+        input_grad.reshape(activations.shape),
+        gain_grads[0],
+        q_g.astype(F32),
+        k_g.astype(F32),
+        v_g.astype(F32),
+        o_g.astype(F32),
+        gain_grads[1],
+        gate_g.astype(F32),
+        up_g.astype(F32),
+        down_g.astype(F32),
+    )
 
 
 def angles(positions):
@@ -120,7 +1040,7 @@
     return tuple((merge_heads(piece) for piece in stacked))
 
 
-def shards(
+def rows_shards(
     activations,
     document_ids,
     attn_gain,
@@ -288,9 +1208,21 @@
     )
 
 
+def layer(sizes, *args):
+    heads = args[3].shape[1] // HEAD_DIM
+    zs = sizes["cp"]
+    fits = sizes["dp"] == 4 and sizes["tp"] == 2 and heads == 2 * zs
+    fits = fits and args[0].shape[3] % 32 == 0 and args[8].shape[1] % (4 * zs * HEAD_DIM) == 0
+    fits = fits and args[3].shape[0] % HEAD_DIM == 0 and args[1].shape[1] % args[3].shape[0] == 0
+    fits = fits and args[1].shape[1] <= 6 * args[3].shape[0]
+    if fits:
+        return heads_shards(zs, *args)
+    return rows_shards(*args)
+
+
 def solution(mesh):
     return jax.shard_map(
-        shards,
+        functools.partial(layer, dict(mesh.shape)),
         mesh=mesh,
         in_specs=(
             P("dp", "cp", None, None, None),

time: 4410 us -> 743 us (0.17)
  waiting for transfers between devices: 4030 us -> 0 us
  Pallas kernels: 0 us -> 604 us
  matrix products: 206 us -> 66.4 us
  blocking collectives: 55.2 us -> 0 us
  local copies, waits for them, and re-layouts: 71.1 us -> 23.2 us
    reduce_scatter x9 -> x0, waiting for transfers between devices: 2260 us -> none  [the longest x1 555 us: shards(): lax.psum_scatter(grad_up_w, 'cp', scatter_dimension=0, tiled=True)]
    all_gather x9 -> x0, waiting for transfers between devices: 1160 us -> none  [the longest x1 288 us: shards(): lax.all_gather(w_gate, 'cp', axis=0, tiled=True)]
    pallas_call x0 -> x4, Pallas kernels: none -> 604 us  [call(): pl.pallas_call(kernel, out_shape=[jax.ShapeDtypeStruct(shape, kind) for s...]
    psum x4 -> x0, waiting for transfers between devices: 603 us -> none  [the longest x1 557 us: shards(): lax.psum((share_gain_one, share_query, share_key, share_value, share_out,...]
    dot_general x69 -> x18, matrix products: 206 us -> 66.4 us  [the longest x12 57.9 us: dot(): lax.dot_general(left, right, (dims, ((), ())), preferred_element_type=F32)]
  transfers between devices with their start and end apart: 22 -> 0, of which waited for: 22 -> 0; matrix products, arithmetic and copies ran while one was open for 4% -> 0% of each run, Pallas kernels for 0% -> 0%
where the time goes in v1:
time: 743 us; the launch traced here: 730 us
  Pallas kernels  604 us (81%)
  matrix products  66.4 us (9%)
  other arithmetic  34.3 us (5%)
  local copies, waits for them, and re-layouts  23.2 us (3%)
    pallas_call x4, Pallas kernels, call(): pl.pallas_call(kernel, out_shape=[jax.ShapeDtypeStruct(shape, kind) for s...  604 us
    dot_general x12, matrix products, dot(): lax.dot_general(left, right, (dims, ((), ())), preferred_element_type=F32)  57.9 us

profile of v1, /device:TPU:0, one launch (start us, length us, event | category | flops | bytes accessed | tf_op | source)
XLA Modules:
  0.0 729.6 jit_solution(6490885538206269399)
XLA Ops:
  2.8 1.0 copy-done.1
  3.9 1.2 copy-done.5
  5.1 1.2 copy-done.6
  6.3 1.2 copy-done.7
  7.6 1.2 copy-done.8
  8.8 74.4 %shard_map.203 = (bf16[2,4,2,64,2048]{4,3,2,1,0:T(8,128)(2,1)S(1)}, bf16[2048,384]{1,0:T(8,128)(2,1)S(1)}, bf16[128,2048]{1,0:T(8,128)(2,1)S(1)}, f32[4,8,512]{2,1,0:T(8,128)S(1)}, f32[2,8,512]{2,1,0:T(8,128)S(1)}) custom-call(bf16[2,64,2048]{2,1,0:T(8,128)(2,1)S(1)} %bitcast.80, bf16[512,1024]{1,0:T(8,128)(2,1)S(1)} %copy-done.5, ...), custom_call_target="tpu_custom_call" | custom-call | tf_op jit(solution)/shard_map/pallas_call | solution.py:378
  83.2 0.9 multiply_reduce_fusion
  84.1 1.1 copy-done
  85.2 3.0 multiply_convert_fusion
  88.2 1.6 copy.36
  89.8 4.5 fusion.32
  94.4 1.2 fusion.6
  95.9 2.1 add_divide_fusion.1
  98.2 1.0 gather_fusion
  99.7 2.2 convolution_convert_fusion.9
  102.0 1.2 convolution_convert_fusion.3
  103.3 1.1 copy-done.3
  104.4 191.1 %shard_map.204 = (f32[64,2048]{1,0:T(8,128)S(1)}, bf16[4,4,2,64,2048]{4,3,2,1,0:T(8,128)(2,1)}, bf16[4,4,2,64,2048]{4,3,2,1,0:T(8,128)(2,1)}, bf16[2048,512]{1,0:T(8,128)(2,1)S(1)}, bf16[256,2048]{1,0:T(8,128)(2,1)S(1)}) custom-call(bf16[2,4,2,64,2048]{4,3,2,1,0:T(8,128)(2,1)S(1)} %bitcast.79, bf16[2,64,2048]{2,1,0:T(8,128)(2,1)S(1)} %bitcast.81, ...), custom_call_target="tpu_custom_call" | custom-call | tf_op jit(solution)/shard_map/pallas_call | solution.py:378
  295.6 9.9 %fusion.33 = f32[2048,512]{0,1:T(8,128)} fusion(bf16[2048,2048]{1,0:T(8,128)(2,1)} %bitcast.112, bf16[2048,512]{1,0:T(8,128)(2,1)S(1)} %get-tuple-element.42), kind=kOutput, calls=%fused_computation.104 | convolution fusion | flops 4294967296 | bytes 14680064 | tf_op jit(solution)/shard_map/dot_general | solution.py:739
  305.5 5.3 multiply_convert_fusion.3
  310.8 5.7 convolution_convert_fusion.6.down_grad
  316.6 9.4 %convolution_convert_fusion.4.gu_grad = bf16[2048,512]{1,0:T(8,128)(2,1)S(1)} fusion(bf16[2048,2048]{1,0:T(8,128)(2,1)} %bitcast.113, bf16[2048,256]{0,1:T(8,128)(2,1)S(1)} %get-tuple-element.58, bf16[2048,256]{0,1:T(8,128)(2,1)S(1)} %get-tuple-element.57), kind=kOutput, calls=%fused_computation.10 | convolution fusion | flops 4300210176 | bytes 12582912 | tf_op jit(solution)/shard_map/dot_general | solution.py:739
  325.9 5.8 convolution_convert_fusion
  331.7 6.8 convolution_convert_fusion.1
  338.5 252.2 %shard_map.205 = (bf16[2,4,2,64,2048]{4,3,2,1,0:T(8,128)(2,1)}, f32[64,2048]{1,0:T(8,128)S(1)}, bf16[2,64,2048]{2,1,0:T(8,128)(2,1)S(1)}, f32[8,2048]{1,0:T(8,12...) custom-call(bf16[4,4,2,64,2048]{4,3,2,1,0:T(8,128)(2,1)} %bitcast.90, ...), custom_call_target="tpu_custom_call" | custom-call | tf_op jit(solution)/shard_map/pallas_call | solution.py:378
  590.8 3.1 convolution_convert_fusion.7.out_grad
  594.6 1.3 convolution_convert_fusion.10
  596.2 1.5 convolution_convert_fusion.8
  597.7 1.9 select_convert_fusion
  600.5 1.0 add_convert_fusion
  601.5 1.1 copy.58
  602.6 1.7 copy.59
  604.3 1.7 copy.60
  606.1 1.7 copy.61
  607.8 2.3 concatenate.38
  610.2 3.3 fusion.1
  613.4 2.4 convolution_convert_fusion.5.qkv_grad
  615.9 2.4 convolution_convert_fusion.2
  618.3 86.6 %shard_map.206 = (bf16[2,64,2048]{2,1,0:T(8,128)(2,1)S(1)}, bf16[512,1024]{1,0:T(8,128)(2,1)S(1)}, bf16[512,1024]{1,0:T(8,128)(2,1)S(1)}, bf16[512,1024]{1,0:T(8...) custom-call(bf16[2,4,2,64,2048]{4,3,2,1,0:T(8,128)(2,1)S(1)} %bitcast.83, ...), custom_call_target="tpu_custom_call" | custom-call | tf_op jit(solution)/shard_map/pallas_call | solution.py:378
  704.9 1.6 convert_element_type.168
  706.5 1.6 convert_element_type.169
  708.1 1.6 convert_element_type.170
  709.6 1.6 convert_element_type.171
  711.9 6.8 convert_element_type.172
  718.7 4.5 convert_element_type.173
  723.2 4.6 convert_element_type.174
  727.8 0.8 copy.69
  728.6 0.8 copy.70
  (75 shorter events, 5.9 us)
Async XLA Ops:
  2.8 1.0 copy-start.1
  3.9 1.2 copy-start.5
  5.1 1.2 copy-start.6
  6.3 1.2 copy-start.7
  7.6 1.2 copy-start.8
  83.2 2.0 copy-start
  83.2 18.8 %copy-start.9 = (bf16[128,2048]{1,0:T(8,128)(2,1)}, bf16[128,2048]{1,0:T(8,128)(2,1)S(1)}, u32[]{:S(2)}) copy-start(bf16[128,2048]{1,0:T(8,128)(2,1)S(1)} %get-tuple-element.38) | copy-start | bytes 1572868
  94.3 1.5 copy-start.17
  95.8 2.1 copy-start.18
  95.8 2.1 copy-start.20
  95.9 2.1 copy-start.22
  102.0 1.3 copy-start.2
  102.0 2.4 copy-start.3
  102.0 2.4 copy-start.4
  295.6 9.9 %copy-start.25 = (bf16[4,4,2,64,2048]{4,3,2,1,0:T(8,128)(2,1)S(1)}, bf16[4,4,2,64,2048]{4,3,2,1,0:T(8,128)(2,1)}, u32[]{:S(2)}) copy-start(bf16[4,4,2,64,2048]{4,3,2,1,0:T(8,128)(2,1)} %get-tuple-element.39) | copy-start | bytes 25165828
  590.8 3.2 copy-start.11
  590.8 3.2 copy-start.10
  590.8 3.8 copy-start.15
  594.6 1.6 copy-start.26
  597.7 1.9 copy-start.21
  597.7 1.9 copy-start.23
  597.7 2.4 copy-start.19
  599.6 0.9 copy-start.24
  610.2 3.3 copy-start.16
  711.8 6.8 copy-start.14
  718.7 4.5 copy-start.13
  723.2 4.6 copy-start.12

commit v2 on v1

--- a/solution.py
+++ b/solution.py
@@ -3,6 +3,7 @@
 
 import jax
 import jax.numpy as jnp
+import numpy as np
 from jax import lax
 from jax.experimental import pallas as pl
 from jax.experimental.pallas import tpu as pltpu
@@ -177,23 +178,32 @@
 
 
 class GatherGroup:
-    def __init__(self, net, src, dst):
-        self.net, self.src, self.dst = net, src, dst
-
-    def place(self, b, z):
-        return self.dst.at[b, z, self.net.t]
+    def __init__(self, net, src, dst, own_lanes=None):
+        self.net, self.src, self.dst, self.own_lanes = net, src, dst, own_lanes
+        self.rows = src.shape[0]
+
+    def place(self, b, z, t=None):
+        t = self.net.t if t is None else t
+        last = 2 * self.net.zs - 1
+        at = ((last + 1) * b + z + t * (last - 2 * z)) * self.rows
+        return self.dst.at[pl.ds(pl.multiple_of(at, self.rows), self.rows)]
 
     def start(self):
         net = self.net
         mine = self.place(net.b, net.z)
-        self.local = net.keep(self.src, mine)
         self.z_sends = [net.send(self.src, mine, net.along_z(s)) for s in range(1, net.zs)]
         self.over = [(net.z, net.send(self.src, mine, net.over_x))]
-        self.twin = [net.send(self.src, mine, net.sibling)]
+        self.twin, self.local = [], []
+        if self.own_lanes is None:
+            self.local.append(net.keep(self.src, mine))
+            self.twin.append((net.b, net.z, net.send(self.src, mine, net.sibling)))
+        else:
+            for t in (0, 1):
+                self.local.append(net.keep(self.own_lanes.at[t], self.place(net.b, net.z, t)))
 
     def to_twin(self, b, z):
         ref = self.place(b, z)
-        self.twin.append(self.net.send(ref, ref, self.net.sibling))
+        self.twin.append((b, z, self.net.send(ref, ref, self.net.sibling)))
 
     def spread(self):
         net = self.net
@@ -204,48 +214,53 @@
             self.over.append((z, net.send(ref, ref, net.over_x)))
             self.to_twin(net.b, z)
 
-    def end(self):
+    def far(self):
         net = self.net
         for z, copy in self.over:
             copy.wait_recv()
             self.to_twin(1 - net.b, z)
-        for copy in self.twin:
+
+    def end(self):
+        for _, _, copy in self.twin:
             copy.wait_recv()
-        self.local.wait()
+        for copy in self.local:
+            copy.wait()
 
 
 class SumGroup:
-    def __init__(self, net, part, own, sib, far, landed):
-        self.net, self.part, self.own, self.sib, self.far, self.landed = net, part, own, sib, far, landed
+    def __init__(self, net, part, sib, far, landed):
+        self.net, self.part, self.sib, self.far, self.landed = net, part, sib, far, landed
         self.rows = part.shape[3]
-
-    def start(self):
-        net = self.net
-        self.twin, self.mine = [], []
-        for s in range(net.zs):
-            z = lax.rem(net.z + s + 1, net.zs)
-            for b in (1 - net.b, net.b):
-                self.twin.append(net.send(self.part.at[b, z, 1 - net.t], self.sib.at[b, z], net.sibling))
-                self.mine.append(net.keep(self.part.at[b, z, net.t], self.own.at[b, z]))
-
-    def run(self):
-        net = self.net
-        over = []
-        for s in range(net.zs):
-            z = lax.rem(net.z + s + 1, net.zs)
-            for j, b in enumerate((1 - net.b, net.b)):
-                self.twin[2 * s + j].wait_recv()
-                self.mine[2 * s + j].wait()
-                add_rows(self.own.at[b, z], [self.own.at[b, z], self.sib.at[b, z]], self.rows)
-                if j == 0:
-                    over.append(net.send(self.own.at[b, z], self.far.at[z], net.over_x))
-        self.z_sends = []
-        for s in range(net.zs):
-            z = lax.rem(net.z + s + 1, net.zs)
-            over[s].wait_recv()
-            out = self.landed.at[net.z] if s == net.zs - 1 else self.own.at[net.b, z]
-            add_rows(out, [self.own.at[net.b, z], self.far.at[z]], self.rows)
-            if s < net.zs - 1:
+        self.twin, self.over, self.z_sends = {}, [], []
+
+    def order(self):
+        return [lax.rem(self.net.z + s + 1, self.net.zs) for s in range(self.net.zs)]
+
+    def give(self, k):
+        net = self.net
+        b = net.b if k else 1 - net.b
+        for s, z in enumerate(self.order()):
+            self.twin[k, s] = net.send(self.part.at[b, 1 - net.t, z], self.sib.at[b, z], net.sibling)
+
+    def take(self, k):
+        net = self.net
+        b = net.b if k else 1 - net.b
+        for s, z in enumerate(self.order()):
+            self.twin[k, s].wait_recv()
+            own = self.part.at[b, net.t, z]
+            add_rows(own, [own, self.sib.at[b, z]], self.rows)
+            if k == 0:
+                self.over.append(net.send(own, self.far.at[z], net.over_x))
+
+    def along(self):
+        net = self.net
+        for s, z in enumerate(self.order()):
+            self.over[s].wait_recv()
+            last = s == net.zs - 1
+            own = self.part.at[net.b, net.t, z]
+            out = self.landed.at[net.z] if last else own
+            add_rows(out, [own, self.far.at[z]], self.rows)
+            if not last:
                 self.z_sends.append(net.send(out, self.landed.at[net.z], net.along_z(s + 1)))
 
     def end(self):
@@ -342,25 +357,33 @@
 class SpreadGrads:
     def __init__(self, net, src, dst, halves):
         self.net, self.src, self.dst, self.halves = net, src, dst, halves
+        self.z_sends, self.plane, self.states = [], {}, []
+
+    def mine(self):
+        return self.dst(self.net.dp, self.net.z)
 
     def start(self):
-        net = self.net
-        mine = self.dst(net.dp, net.z)
-        self.local = net.keep(self.src(net.z), mine)
-        self.z_sends = [
-            net.send(self.src(lax.rem(net.z + s, net.zs)), mine, net.along_z(s)) for s in range(1, net.zs)
-        ]
-        self.plane = [
-            (net.z, net.send(self.src(net.z), mine, net.over_x), net.send(self.src(net.z), mine, net.over_y))
-        ]
-        self.states = []
+        self.own()
+        for s in range(1, self.net.zs):
+            self.go(s)
+
+    def own(self):
+        self.local = self.net.keep(self.src(self.net.z), self.mine())
+
+    def go(self, s):
+        net = self.net
+        self.z_sends.append(net.send(self.src(lax.rem(net.z + s, net.zs)), self.mine(), net.along_z(s)))
 
     def spread(self, s):
         net = self.net
-        self.z_sends[s - 1].wait_recv()
         z = net.source_z(s)
         ref = self.dst(net.dp, z)
-        self.plane.append((z, net.send(ref, ref, net.over_x), net.send(ref, ref, net.over_y)))
+        if s:
+            self.z_sends[s - 1].wait_recv()
+            src = ref
+        else:
+            src = self.src(net.z)
+        self.plane[s] = (z, net.send(src, ref, net.over_x), net.send(src, ref, net.over_y))
 
     def relay(self, s):
         z, over_x, over_y = self.plane[s]
@@ -373,12 +396,54 @@
         self.local.wait()
 
 
-def call(kernel, name, outs, scratch, count, args, spaces=None, vmem=40):
-    spaces = spaces or [ANY] * len(args)
+def half_rows(ref, k):
+    n = ref.shape[0] // 2
+    return ref.at[pl.ds(k * n, n)]
+
+
+def aligned(i, size):
+    return pl.ds(pl.multiple_of(i * size, size), size)
+
+
+def loop(count, body):
+    def one(i, carry):
+        body(i)
+        return carry
+
+    lax.fori_loop(0, count, one, 0)
+
+
+def dot(left, right, dims=((1,), (0,)), kind=F32):
+    return lax.dot_general(left, right, (dims, ((), ())), preferred_element_type=F32).astype(kind)
+
+
+def turn(u, cosine, sine):
+    return u * cosine + pltpu.roll(u, HEAD_DIM // 2, 1) * sine
+
+
+def column(row, start, count):
+    n = row.shape[1]
+    here = lax.broadcasted_iota(jnp.int32, (count, n), 1) == start + lax.broadcasted_iota(jnp.int32, (count, n), 0)
+    return jnp.sum(jnp.where(here, row, 0.0), axis=1, keepdims=True)
+
+
+def seen(row, start, count, flip=False):
+    n = row.shape[1]
+    same = column(row, start, count) == row
+    mine = start + lax.broadcasted_iota(jnp.int32, (count, n), 0)
+    other = lax.broadcasted_iota(jnp.int32, (count, n), 1)
+    return same & ((mine <= other) if flip else (other <= mine))
+
+
+def sigma_of(left, right):
+    return jax.nn.sigmoid(dot(left, right, ((1,), (1,))) * HEAD_DIM**-0.5 - SHIFT)
+
+
+def call(kernel, name, outs, scratch, count, args, vmem):
     return pl.pallas_call(
         kernel,
         out_shape=[jax.ShapeDtypeStruct(shape, kind) for shape, kind, _ in outs],
-        in_specs=[pl.BlockSpec(memory_space=space) for space in spaces],
+        in_specs=[pl.BlockSpec(memory_space=ANY)] * len(args),
         out_specs=[pl.BlockSpec(memory_space=space) for _, _, space in outs],
         scratch_shapes=list(scratch) + [pltpu.SemaphoreType.DMA((count,)), pltpu.SemaphoreType.DMA((count,))],
         compiler_params=pltpu.CompilerParams(
@@ -387,360 +452,481 @@
     )(*args)
 
 
-def open_kernel(zs, x, wq, wk, wv, wo, small, x_all, qkv_w, out_w, small_z, small_x, send_sems, recv_sems):
-    net = Net(zs, send_sems, recv_sems)
-    net.meet(y=False)
-    deep = wq.shape[0]
-    gather = GatherGroup(net, x.at[net.t], x_all)
-    gather.start()
-    waits, local = [], []
-
-    def cols(w, z):
-        return w.at[:, pl.ds(pl.multiple_of((net.b * zs + z) * HEAD_DIM, HEAD_DIM), HEAD_DIM)]
-
-    def rows(z):
-        return wo.at[pl.ds(pl.multiple_of((net.b * zs + z) * HEAD_DIM, HEAD_DIM), HEAD_DIM)]
-
-    mine = pl.ds(pl.multiple_of(net.z * deep, deep), deep)
-    for s in range(1, zs):
-        waits.append(net.send(small, small_z.at[net.z], net.along_z(s)))
-    waits.append(net.send(small, small_x.at[net.b], net.over_x))
-    local.append(net.keep(small, small_z.at[net.z]))
-    local.append(net.keep(small, small_x.at[net.b]))
-    for m, w in enumerate((wq, wk, wv)):
-        dst = qkv_w.at[mine, pl.ds(m * HEAD_DIM, HEAD_DIM)]
-        local.append(net.keep(cols(w, net.z), dst))
-        for s in range(1, zs):
-            waits.append(net.send(cols(w, lax.rem(net.z + s, zs)), dst, net.along_z(s)))
-    dst = out_w.at[:, mine]
-    local.append(net.keep(rows(net.z), dst))
-    for s in range(1, zs):
-        waits.append(net.send(rows(lax.rem(net.z + s, zs)), dst, net.along_z(s)))
-    gather.spread()
-    gather.end()
-    for copy in waits:
-        copy.wait_recv()
-    for copy in local:
-        copy.wait()
-    net.finish()
-
-
-def middle_kernel(
-    zs, part, x, gain, wg, wu, wd, cot, middle, h2_all, cot_all, gu_w, down_w,
-    own, sib, far, landed, x_lane, h2, gain_v, mid_v, send_sems, recv_sems,
+def forward_kernel(
+    zs, x, wq, wk, wv, wo, small, cosine, sine, wg, wu, wd, cot,
+    hidden_out, qkv_out, attended_out, qkv_w_out, out_w_out, gains_out, docs_out, middle, h2_all, cot_all, gu_w, down_w,
+    x_all, h1, qkv_w, out_w, small_z, small_x, gains, docs, cos_v, sin_v, qkv, attended, part, sib, far, landed,
+    x_lane, h2, mid_v, send_sems, recv_sems,
 ):
     net = Net(zs, send_sems, recv_sems)
     net.meet()
     deep, wide = wg.shape[0], gu_w.shape[1] // 2
-    branch = SumGroup(net, part, own, sib, far, landed)
-    branch.start()
+    seq = docs.shape[1]
+    half, side = deep // 2, HEAD_DIM // 2
+    gather = GatherGroup(net, x.at[net.t], x_all, own_lanes=x)
+    gather.start()
+    small_waits = [net.send(small, small_z.at[net.z], net.along_z(s)) for s in range(1, zs)]
+    small_waits.append(net.send(small, small_x.at[net.b], net.over_x))
+    local = [net.keep(small, small_z.at[net.z]), net.keep(small, small_x.at[net.b])]
+    local += [net.keep(cosine, cos_v), net.keep(sine, sin_v)]
     lane = net.keep(x.at[net.t], x_lane)
-    gains = net.keep(gain, gain_v)
-    waits, local = [], []
-    mine = pl.ds(pl.multiple_of(net.z * deep, deep), deep)
+
+    def head(z):
+        return aligned(net.b * zs + z, HEAD_DIM)
+
+    mine = aligned(net.z, deep)
+    my_half = pl.ds(pl.multiple_of(net.a * half, half), half)
+    qkv_sends, out_sends, w_local = [], [], []
+    for m, w in enumerate((wq, wk, wv)):
+        col = pl.ds(m * HEAD_DIM, HEAD_DIM)
+        w_local.append(net.keep(w.at[:, head(net.z)], qkv_w.at[mine, col]))
+    for s in range(1, zs):
+        z = lax.rem(net.z + s, zs)
+        rows = pl.ds(pl.multiple_of(net.z * deep + net.a * half, half), half)
+        qkv_sends.append(
+            [
+                net.send(w.at[my_half, head(z)], qkv_w.at[rows, pl.ds(m * HEAD_DIM, HEAD_DIM)], net.along_z(s))
+                for m, w in enumerate((wq, wk, wv))
+            ]
+        )
+    out_rows = pl.ds(pl.multiple_of(net.a * side, side), side)
+    w_local.append(net.keep(wo.at[head(net.z)], out_w.at[:, mine]))
+    for s in range(1, zs):
+        z = lax.rem(net.z + s, zs)
+        at = pl.ds(pl.multiple_of((net.b * zs + z) * HEAD_DIM + net.a * side, side), side)
+        out_sends.append(net.send(wo.at[at], out_w.at[out_rows, mine], net.along_z(s)))
+
+    cotan = GatherAll(net, cot.at[net.t], cot_all)
+    cotan.start()
+    mlp_waits, mlp_local = [], []
 
     def block(z):
-        return pl.ds(pl.multiple_of((net.dp * zs + z) * wide, wide), wide)
-
-    def fetch(s, z):
-        srcs = (wg.at[:, block(z)], wu.at[:, block(z)], wd.at[block(z)])
-        dsts = (gu_w.at[mine, pl.ds(0, wide)], gu_w.at[mine, pl.ds(wide, wide)], down_w.at[:, mine])
-        for src, dst in zip(srcs, dsts, strict=True):
-            if s == 0:
-                local.append(net.keep(src, dst))
-            else:
-                waits.append(net.send(src, dst, net.along_z(s)))
-
-    fetch(0, net.z)
-    branch.run()
+        return aligned(net.dp * zs + z, wide)
+
+    mlp = (
+        (lambda z: wg.at[:, block(z)], gu_w.at[mine, pl.ds(0, wide)]),
+        (lambda z: wu.at[:, block(z)], gu_w.at[mine, pl.ds(wide, wide)]),
+        (lambda z: wd.at[block(z)], down_w.at[:, mine]),
+    )
+    for src, dst in mlp:
+        mlp_local.append(net.keep(src(net.z), dst))
+
+    def fetch(k):
+        src, dst = mlp[k]
+        for s in range(1, zs):
+            mlp_waits.append(net.send(src(lax.rem(net.z + s, zs)), dst, net.along_z(s)))
+
+    fetch(0)
+
+    for copy in small_waits:
+        copy.wait_recv()
+    for copy in local:
+        copy.wait()
+    for z in range(zs):
+        gains[0:1, z * deep : (z + 1) * deep] = small_z[z, 0:1, :]
+        gains[1:2, z * deep : (z + 1) * deep] = small_z[z, 1:2, :]
+    for b in range(2):
+        for k in range(seq // deep):
+            docs[b : b + 1, k * deep : (k + 1) * deep] = small_x[b, 2 + k : 3 + k, :]
+
+    def norm_block(ref_at):
+        def body(i):
+            at = pl.ds(pl.multiple_of(ref_at + i * 16, 16), 16)
+            rows = x_all[at, :].astype(F32)
+            inverse = lax.rsqrt(jnp.mean(rows * rows, axis=-1, keepdims=True) + EPS)
+            h1[at, :] = (rows * inverse * gains[0:1, :]).astype(BF)
+
+        loop(x.shape[1] // 16, body)
+
+    rows = x.shape[1]
+    last = 2 * zs - 1
+
+    def offset(b, z, t):
+        return ((last + 1) * b + z + t * (last - 2 * z)) * rows
+
+    gather.spread()
+    for copy in gather.local:
+        copy.wait()
+    gather.local = []
+    for t in (0, 1):
+        norm_block(offset(net.b, net.z, t))
     for s in range(1, zs):
-        fetch(s, lax.rem(net.z + s, zs))
+        norm_block(offset(net.b, net.source_z(s), net.t))
+    qkv_y = []
+    for s in range(1, zs):
+        for copy in qkv_sends[s - 1]:
+            copy.wait_recv()
+        at = qkv_w.at[pl.ds(pl.multiple_of(net.source_z(s) * deep + net.a * half, half), half)]
+        qkv_y.append(net.send(at, at, net.over_y))
+    gather.far()
+    for z, _ in gather.over:
+        norm_block(offset(1 - net.b, z, net.t))
+    out_y = []
+    for s in range(1, zs):
+        out_sends[s - 1].wait_recv()
+        at = out_w.at[out_rows, aligned(net.source_z(s), deep)]
+        out_y.append(net.send(at, at, net.over_y))
+    for b, z, copy in gather.twin:
+        copy.wait_recv()
+        norm_block(offset(b, z, 1 - net.t))
+    for copy in qkv_y:
+        copy.wait_recv()
+    for copy in w_local:
+        copy.wait()
+    cotan.spread()
+    for copy in out_y:
+        copy.wait_recv()
+
+    branch = SumGroup(net, part, sib, far, landed)
+    tile = 128
+    for k in range(2):
+        b = net.b if k else 1 - net.b
+        base = b * seq
+
+        def project(i):
+            at = pl.ds(pl.multiple_of(base + i * 256, 256), 256)
+            pos = aligned(i, 256)
+            pre = dot(h1[at, :], qkv_w[...])
+            c, s = cos_v[pos, :], sin_v[pos, :]
+            qkv[at, 0:HEAD_DIM] = turn(pre[:, 0:HEAD_DIM], c, s).astype(BF)
+            qkv[at, HEAD_DIM : 2 * HEAD_DIM] = turn(pre[:, HEAD_DIM : 2 * HEAD_DIM], c, s).astype(BF)
+            qkv[at, 2 * HEAD_DIM : 3 * HEAD_DIM] = pre[:, 2 * HEAD_DIM : 3 * HEAD_DIM].astype(BF)
+
+        loop(seq // 256, project)
+        every = pl.ds(pl.multiple_of(base, seq), seq)
+        row = docs[pl.ds(b, 1), :]
+
+        def attend(i):
+            at = pl.ds(pl.multiple_of(base + i * tile, tile), tile)
+            sigma = sigma_of(qkv[at, 0:HEAD_DIM], qkv[every, HEAD_DIM : 2 * HEAD_DIM])
+            weights = jnp.where(seen(row, i * tile, tile), sigma, 0.0).astype(BF)
+            found = dot(weights, qkv[every, 2 * HEAD_DIM : 3 * HEAD_DIM], kind=BF)
+            attended[at, :] = found
+            out = dot(found, out_w[...], kind=BF)
+            for j in range(tile // rows):
+                blk = i * (tile // rows) + j
+                t = lax.div(blk, zs)
+                z = (1 - t) * blk + t * (last - blk)
+                part[b, t, z] = out[j * rows : (j + 1) * rows, :]
+
+        loop(seq // tile, attend)
+        branch.give(k)
+    saved = [
+        net.keep(h1, hidden_out), net.keep(qkv, qkv_out), net.keep(attended, attended_out),
+        net.keep(qkv_w, qkv_w_out), net.keep(out_w, out_w_out), net.keep(gains, gains_out), net.keep(docs, docs_out),
+    ]
+    branch.take(0)
+    branch.take(1)
+    branch.along()
+    cotan.relay()
     lane.wait()
-    gains.wait()
     branch.end()
-    rows, width = x_lane.shape
-
-    def body(at):
+
+    def body(i):
+        at = aligned(i, 16)
         total = x_lane[at, :].astype(F32)
         for z in range(zs):
             total += landed[z, at, :].astype(F32)
         mid_v[at, :] = total
         inverse = lax.rsqrt(jnp.mean(total * total, axis=-1, keepdims=True) + EPS)
-        h2[at, :] = (total * inverse * gain_v[0:1, :]).astype(BF)
-
-    rows_loop(rows, 16, body)
-    out = net.keep(mid_v, middle)
+        h2[at, :] = (total * inverse * gains[1:2, :]).astype(BF)
+
+    loop(rows // 16, body)
+    saved.append(net.keep(mid_v, middle))
     hidden = GatherAll(net, h2, h2_all)
     hidden.start()
-    cotan = GatherAll(net, cot.at[net.t], cot_all)
-    cotan.start()
+    fetch(1)
+    fetch(2)
     hidden.spread()
+    cotan.end()
     hidden.relay()
-    cotan.spread()
-    cotan.relay()
     hidden.end()
-    cotan.end()
-    out.wait()
-    for copy in waits:
+    for copy in saved:
+        copy.wait()
+    for copy in mlp_waits:
         copy.wait_recv()
-    for copy in local:
+    for copy in mlp_local:
         copy.wait()
     net.finish()
 
 
-def back_kernel(
-    zs, gh_part, feed_part, gu_grad, down_grad, middle, cot, gain,
-    gbr_all, grad_mid, layer_out, gain_part, gate_out, up_out, down_out,
-    own, sib, one, two, landed, own_f, sib_f, one_f, two_f, landed_f, mid_v, cot_v, gain_v, gm_v, gbr_v, gsum_v, lo_v,
-    send_sems, recv_sems,
+def backward_kernel(
+    zs, gh_part, feed_part, gu_grad, down_grad, middle, cot, x, gains_in, docs_in, cosine, sine,
+    hidden_in, qkv_in, attended_in, qkv_w_in, out_w_in,
+    layer_out, input_grad, q_out, k_out, v_out, o_out, gate_out, up_out, down_out, gains_out,
+    own, sib, one, two, landed, own_f, sib_f, one_f, two_f, landed_f, part, sib_1, far_1, landed_1,
+    h1, qkv, attended, qkv_w, out_w, gbr_all, gqkv, gains, docs, cos_v, sin_v, hg, mid_v, cot_v, x_v, gm_v, gbr_v, out_v,
+    lo_v, gsum, g_far, g_land, q_give, q_own, q_land, o_part, o_own, o_land, send_sems, recv_sems,
 ):
     net = Net(zs, send_sems, recv_sems)
     net.meet()
-    wide = gu_grad.shape[1] // 2
-    deep = gate_out.shape[0]
+    deep, wide = gate_out.shape[0], gu_grad.shape[1] // 2
+    seq = docs.shape[1]
+    half, side = deep // 2, HEAD_DIM // 2
+    rows = x.shape[1]
+    last = 2 * zs - 1
+    scale = HEAD_DIM**-0.5
     hidden = SumAll(net, gh_part, own, sib, one, two, landed)
     hidden.start()
     feed = SumAll(net, feed_part, own_f, sib_f, one_f, two_f, landed_f)
-    feed.start()
-    local = [net.keep(middle, mid_v), net.keep(cot.at[net.t], cot_v), net.keep(gain, gain_v)]
+    local = [net.keep(middle, mid_v), net.keep(cot.at[net.t], cot_v), net.keep(gains_in, gains)]
+    local += [net.keep(x.at[net.t], x_v), net.keep(docs_in, docs), net.keep(cosine, cos_v), net.keep(sine, sin_v)]
+    local += [net.keep(qkv_in, qkv), net.keep(attended_in, attended), net.keep(qkv_w_in, qkv_w)]
+    local += [net.keep(out_w_in, out_w), net.keep(hidden_in, h1)]
 
     def block(dp, z):
-        return pl.ds(pl.multiple_of((dp * zs + z) * wide, wide), wide)
-
-    def deep_rows(z):
-        return pl.ds(pl.multiple_of(z * deep, deep), deep)
-
-    def half_rows(ref, k):
-        n = ref.shape[0] // 2
-        return ref.at[pl.ds(k * n, n)]
+        return aligned(dp * zs + z, wide)
 
     grads = [
         SpreadGrads(
             net,
-            lambda z: gu_grad.at[deep_rows(z), pl.ds(0, wide)],
+            lambda z: gu_grad.at[aligned(z, deep), pl.ds(0, wide)],
             lambda dp, z: gate_out.at[:, block(dp, z)],
             half_rows,
         ),
         SpreadGrads(
             net,
-            lambda z: gu_grad.at[deep_rows(z), pl.ds(wide, wide)],
+            lambda z: gu_grad.at[aligned(z, deep), pl.ds(wide, wide)],
             lambda dp, z: up_out.at[:, block(dp, z)],
             half_rows,
         ),
         SpreadGrads(
             net,
-            lambda z: down_grad.at[:, deep_rows(z)],
+            lambda z: down_grad.at[:, aligned(z, deep)],
             lambda dp, z: down_out.at[block(dp, z)],
             half_rows,
         ),
     ]
+    grads[0].start()
+    grads[1].start()
+    feed.start()
     for s in range(zs):
         hidden.first(s)
     for s in range(zs):
         hidden.second(s)
     for s in range(zs):
         hidden.third(s)
-    for grad in grads:
-        grad.start()
     for s in range(zs):
         feed.first(s)
+    grads[2].start()
     for copy in local:
         copy.wait()
     hidden.end()
-    rows = mid_v.shape[0]
-    gsum_v[...] = jnp.zeros_like(gsum_v)
-
-    def body(at):
-        mid = mid_v[at, :]
-        inverse = lax.rsqrt(jnp.mean(mid * mid, axis=-1, keepdims=True) + EPS)
-        normed = mid * inverse
-        total = landed[0, at, :].astype(F32)
+    gsum[...] = jnp.zeros_like(gsum)
+
+    def total_of(ref, at):
+        total = ref[0, at, :].astype(F32)
         for z in range(1, zs):
-            total += landed[z, at, :].astype(F32)
+            total += ref[z, at, :].astype(F32)
+        return total
+
+    def norm_back(inputs, total, gain, k):
+        inverse = lax.rsqrt(jnp.mean(inputs * inputs, axis=-1, keepdims=True) + EPS)
+        normed = inputs * inverse
         prod = total * normed
-        gsum_v[...] += prod[0:8, :] + prod[8:16, :]
-        scaled = total * gain_v[0:1, :]
-        grad = cot_v[at, :].astype(F32) + inverse * (
-            scaled - normed * jnp.mean(scaled * normed, axis=-1, keepdims=True)
-        )
+        gsum[k] += prod[0:8, :] + prod[8:16, :]
+        scaled = total * gain
+        return inverse * (scaled - normed * jnp.mean(scaled * normed, axis=-1, keepdims=True))
+
+    def back_two(i):
+        at = aligned(i, 16)
+        grad = cot_v[at, :].astype(F32) + norm_back(mid_v[at, :], total_of(landed, at), gains[1:2, :], 1)
         gm_v[at, :] = grad
         gbr_v[at, :] = grad.astype(BF)
 
-    rows_loop(rows, 16, body)
+    loop(rows // 16, back_two)
     gather = GatherGroup(net, gbr_v, gbr_all)
     gather.start()
-    outs = [net.keep(gm_v, grad_mid), net.keep(gsum_v, gain_part)]
     for s in range(zs):
         feed.second(s)
     gather.spread()
     for s in range(zs):
         feed.third(s)
+    for s in range(zs):
+        grads[0].spread(s)
+    gather.far()
     gather.end()
-    for s in range(1, zs):
-        for grad in grads:
-            grad.spread(s)
-    for grad in grads:
-        grad.relay(0)
-    feed.end()
-
-    def close(at):
-        total = mid_v[at, :]
-        for z in range(zs):
-            total += landed_f[z, at, :].astype(F32)
-        lo_v[at, :] = total.astype(BF)
-
-    rows_loop(rows, 16, close)
-    outs.append(net.keep(lo_v, layer_out.at[net.t]))
-    last = net.send(lo_v, layer_out.at[net.t], net.sibling)
-    for s in range(1, zs):
-        for grad in grads:
-            grad.relay(s)
-    for grad in grads:
-        grad.end()
-    last.wait_recv()
-    for copy in outs:
-        copy.wait()
-    net.finish()
-
-
-def close_kernel(
-    zs, gh_part, qkv_grad, out_grad, grad_mid, x, gain, gain_part,
-    input_grad, q_out, k_out, v_out, o_out, gains_out,
-    own, sib, far, landed, x_v, gain_v, gm_v, gsum_v, gi_v, q_own, q_far, o_own, o_far, g_far, g_land,
-    send_sems, recv_sems,
-):
-    net = Net(zs, send_sems, recv_sems)
-    net.meet()
-    deep = q_out.shape[0]
-    half = deep // 2
-    hidden = SumGroup(net, gh_part, own, sib, far, landed)
-    local = [
-        net.keep(grad_mid, gm_v), net.keep(x.at[net.t], x_v), net.keep(gain, gain_v),
-        net.keep(gain_part, gsum_v.at[1]),
-    ]
-    sums = []
+
+    branch = SumGroup(net, part, sib_1, far_1, landed_1)
+    tile = 128
+    for k in range(2):
+        b = net.b if k else 1 - net.b
+        base = b * seq
+        every = pl.ds(pl.multiple_of(base, seq), seq)
+        row = docs[pl.ds(b, 1), :]
+
+        def heads_grad(i):
+            at = pl.ds(pl.multiple_of(base + i * 256, 256), 256)
+            hg[aligned(i, 256), :] = dot(gbr_all[at, :], out_w[...], ((1,), (1,)), BF)
+
+        loop(seq // 256, heads_grad)
+
+        def by_query(i):
+            at = pl.ds(pl.multiple_of(base + i * tile, tile), tile)
+            pos = aligned(i, tile)
+            keys = qkv[every, HEAD_DIM : 2 * HEAD_DIM]
+            sigma = sigma_of(qkv[at, 0:HEAD_DIM], keys)
+            gw = dot(hg[pos, :], qkv[every, 2 * HEAD_DIM : 3 * HEAD_DIM], ((1,), (1,)))
+            gs = jnp.where(seen(row, i * tile, tile), gw * sigma * (1.0 - sigma), 0.0).astype(BF)
+            gq = dot(gs, keys) * scale
+            gqkv[at, 0:HEAD_DIM] = turn(gq, cos_v[pos, :], -sin_v[pos, :]).astype(BF)
+
+        loop(seq // tile, by_query)
+
+        def by_key(i):
+            at = pl.ds(pl.multiple_of(base + i * tile, tile), tile)
+            pos = aligned(i, tile)
+            queries = qkv[every, 0:HEAD_DIM]
+            sigma = sigma_of(qkv[at, HEAD_DIM : 2 * HEAD_DIM], queries)
+            gw = dot(qkv[at, 2 * HEAD_DIM : 3 * HEAD_DIM], hg[...], ((1,), (1,)))
+            mask = seen(row, i * tile, tile, flip=True)
+            gs = jnp.where(mask, gw * sigma * (1.0 - sigma), 0.0).astype(BF)
+            weights = jnp.where(mask, sigma, 0.0).astype(BF)
+            gk = dot(gs, queries) * scale
+            gqkv[at, HEAD_DIM : 2 * HEAD_DIM] = turn(gk, cos_v[pos, :], -sin_v[pos, :]).astype(BF)
+            gqkv[at, 2 * HEAD_DIM : 3 * HEAD_DIM] = dot(weights, hg[...], kind=BF)
+
+        loop(seq // tile, by_key)
+
+        def back_one(i):
+            at = pl.ds(pl.multiple_of(base + i * tile, tile), tile)
+            out = dot(gqkv[at, :], qkv_w[...], ((1,), (1,)), BF)
+            for j in range(tile // rows):
+                blk = i * (tile // rows) + j
+                t = lax.div(blk, zs)
+                z = (1 - t) * blk + t * (last - blk)
+                part[b, t, z] = out[j * rows : (j + 1) * rows, :]
+
+        loop(seq // tile, back_one)
+        branch.give(k)
+    branch.take(0)
+    branch.take(1)
+
+    def qkv_grad(z, a):
+        at = pl.ds(pl.multiple_of(z * deep + a * half, half), half)
+        return dot(h1[:, at], gqkv[...], ((0,), (0,)), BF)
+
+    def out_grad(z):
+        o_part[z] = dot(attended[...], gbr_all[:, aligned(z, deep)], ((0,), (0,)), BF)
+
+    def theirs(z):
+        q_give[z] = qkv_grad(z, 1 - net.a)
+
+    def ours(z):
+        q_own[z] = qkv_grad(z, net.a)
+
+    def side_rows(a):
+        return pl.ds(pl.multiple_of(a * side, side), side)
+
+    loop(zs, out_grad)
+    loop(zs, theirs)
+    swaps = []
     for s in range(zs):
         z = lax.rem(net.z + s + 1, zs)
-        at = lambda a: pl.ds(pl.multiple_of(z * deep + a * half, half), half)
-        oc = pl.ds(pl.multiple_of(z * deep, deep), deep)
-        oh = HEAD_DIM // 2
-        orow = lambda a: pl.ds(pl.multiple_of(a * oh, oh), oh)
-        sums.append(
+        swaps.append(
             (
                 z,
-                net.send(qkv_grad.at[at(1 - net.a)], q_far.at[z], net.over_y),
-                net.keep(qkv_grad.at[at(net.a)], q_own.at[z]),
-                net.send(out_grad.at[orow(1 - net.a), oc], o_far.at[z], net.over_y),
-                net.keep(out_grad.at[orow(net.a), oc], o_own.at[z]),
+                net.send(q_give.at[z], q_land.at[z], net.over_y),
+                net.send(o_part.at[z, side_rows(1 - net.a)], o_land.at[z], net.over_y),
             )
         )
-    hidden.start()
-    hidden.run()
-
-    def half_rows(ref, k):
-        n = ref.shape[0] // 2
-        return ref.at[pl.ds(k * n, n)]
-
-    for z, q_in, q_mine, o_in, o_mine in sums:
-        q_in.wait_recv()
-        q_mine.wait()
-        add_rows(q_own.at[z], [q_own.at[z], q_far.at[z]], half)
-        o_in.wait_recv()
-        o_mine.wait()
-        add_rows(o_own.at[z], [o_own.at[z], o_far.at[z]], HEAD_DIM // 2)
+    loop(zs, ours)
+    branch.along()
 
     def q_place(ref):
         def place(dp, z):
             a, b = lax.div(dp, 2), lax.rem(dp, 2)
-            return ref.at[
-                pl.ds(pl.multiple_of(a * half, half), half),
-                pl.ds(pl.multiple_of((b * zs + z) * HEAD_DIM, HEAD_DIM), HEAD_DIM),
-            ]
+            return ref.at[pl.ds(pl.multiple_of(a * half, half), half), aligned(b * zs + z, HEAD_DIM)]
 
         return place
 
     def o_place(dp, z):
         a, b = lax.div(dp, 2), lax.rem(dp, 2)
-        oh = HEAD_DIM // 2
-        return o_out.at[pl.ds(pl.multiple_of((b * zs + z) * HEAD_DIM + a * oh, oh), oh)]
-
-    grads = [
-        SpreadGrads(
-            net, lambda z, m=m: q_own.at[z, :, pl.ds(m * HEAD_DIM, HEAD_DIM)], q_place(ref), half_rows
-        )
+        return o_out.at[pl.ds(pl.multiple_of((b * zs + z) * HEAD_DIM + a * side, side), side)]
+
+    late = [
+        SpreadGrads(net, lambda z, m=m: q_own.at[z, :, pl.ds(m * HEAD_DIM, HEAD_DIM)], q_place(ref), half_rows)
         for m, ref in enumerate((q_out, k_out, v_out))
     ]
-    grads.append(SpreadGrads(net, lambda z: o_own.at[z], o_place, half_rows))
-    for grad in grads:
-        grad.start()
-    for copy in local:
-        copy.wait()
-    hidden.end()
-    rows = x_v.shape[0]
-    gsum_v[0] = jnp.zeros_like(gsum_v[0])
-
-    def body(at):
-        inputs = x_v[at, :].astype(F32)
-        inverse = lax.rsqrt(jnp.mean(inputs * inputs, axis=-1, keepdims=True) + EPS)
-        normed = inputs * inverse
-        total = landed[0, at, :].astype(F32)
-        for z in range(1, zs):
-            total += landed[z, at, :].astype(F32)
-        prod = total * normed
-        gsum_v[0] += prod[0:8, :] + prod[8:16, :]
-        scaled = total * gain_v[0:1, :]
-        grad = gm_v[at, :] + inverse * (scaled - normed * jnp.mean(scaled * normed, axis=-1, keepdims=True))
-        gi_v[at, :] = grad.astype(BF)
-
-    rows_loop(rows, 16, body)
-    out = net.keep(gi_v, input_grad.at[net.t])
-    last = net.send(gi_v, input_grad.at[net.t], net.sibling)
+    late.append(SpreadGrads(net, lambda z: o_own.at[z], o_place, half_rows))
+    for s, (z, q_in, o_in) in enumerate(swaps):
+        q_in.wait_recv()
+        add_rows(q_own.at[z], [q_own.at[z], q_land.at[z]], half)
+        o_in.wait_recv()
+        add_rows(o_own.at[z], [o_part.at[z, side_rows(net.a)], o_land.at[z]], side)
+        for grad in late:
+            if s < zs - 1:
+                grad.go(s + 1)
+            else:
+                grad.own()
+    for s in range(zs):
+        grads[1].spread(s)
+    branch.end()
+
+    def back_last(i):
+        at = aligned(i, 16)
+        grad = gm_v[at, :] + norm_back(x_v[at, :].astype(F32), total_of(landed_1, at), gains[0:1, :], 0)
+        out_v[at, :] = grad.astype(BF)
+
+    loop(rows // 16, back_last)
+    outs = [net.keep(out_v, input_grad.at[net.t])]
+    pairs = [net.send(out_v, input_grad.at[net.t], net.sibling)]
+    for s in range(zs):
+        grads[0].relay(s)
+    feed.end()
+
+    def close(i):
+        at = aligned(i, 16)
+        lo_v[at, :] = (mid_v[at, :] + total_of(landed_f, at)).astype(BF)
+
+    loop(rows // 16, close)
+    outs.append(net.keep(lo_v, layer_out.at[net.t]))
+    pairs.append(net.send(lo_v, layer_out.at[net.t], net.sibling))
     for k, way in enumerate((net.sibling, net.over_x, net.over_y)):
-        swap = net.send(gsum_v, g_far.at[k], way)
+        swap = net.send(gsum, g_far.at[k], way)
         swap.wait()
         net.open = [c for c in net.open if c is not swap]
-        gsum_v[...] = gsum_v[...] + g_far[k]
-    cut = lambda z: gsum_v.at[:, :, pl.ds(pl.multiple_of(z * deep, deep), deep)]
+        gsum[...] = gsum[...] + g_far[k]
+
+    def cut(z):
+        return gsum.at[:, :, aligned(z, deep)]
+
     z_gain = [net.send(cut(lax.rem(net.z + s, zs)), g_land.at[net.z], net.along_z(s)) for s in range(1, zs)]
-    keep = net.keep(cut(net.z), g_land.at[net.z])
-    for s in range(1, zs):
-        for grad in grads:
+    outs.append(net.keep(cut(net.z), g_land.at[net.z]))
+    for s in range(zs):
+        for grad in late:
             grad.spread(s)
     for s in range(zs):
-        for grad in grads:
+        grads[2].spread(s)
+    for s in range(zs):
+        grads[1].relay(s)
+    for s in range(zs):
+        for grad in late:
             grad.relay(s)
-    for grad in grads:
+    for s in range(zs):
+        grads[2].relay(s)
+    for grad in grads + late:
         grad.end()
-    keep.wait()
-    for copy in z_gain:
+    for copy in outs:
+        copy.wait()
+    for copy in z_gain + pairs:
         copy.wait_recv()
     total = g_land[0]
     for z in range(1, zs):
         total += g_land[z]
     gains_out[...] = total
-    last.wait_recv()
-    out.wait()
     net.finish()
 
 
-def rope_tables(positions):
+def rope_tables(seq):
     half_dim = HEAD_DIM // 2
-    frequency = ROPE_BASE ** (-jnp.arange(half_dim, dtype=F32) / half_dim)
-    angle = positions.astype(F32)[:, None] * frequency[None, :]
-    return jnp.cos(angle), jnp.sin(angle)
-
-
-def turn(u, cosine, sine):
-    first, second = u[..., : HEAD_DIM // 2], u[..., HEAD_DIM // 2 :]
-    return jnp.concatenate([first * cosine - second * sine, second * cosine + first * sine], axis=-1)
-
-
-def dot(left, right, dims=((1,), (0,)), kind=F32):
-    return lax.dot_general(left, right, (dims, ((), ())), preferred_element_type=F32).astype(kind)
-
-
-def bdot(left, right, dims):
-    return lax.dot_general(left, right, (dims, ((0,), (0,))), preferred_element_type=F32)
+    frequency = ROPE_BASE ** (-np.arange(half_dim, dtype=np.float32) / half_dim)
+    angle = np.arange(seq, dtype=np.float32)[:, None] * frequency.astype(np.float32)[None, :]
+    cosine, sine = np.cos(angle), np.sin(angle)
+    return (
+        np.concatenate([cosine, cosine], axis=1).astype(np.float32),
+        np.concatenate([-sine, sine], axis=1).astype(np.float32),
+    )
 
 
 def heads_shards(
@@ -749,55 +935,26 @@
     stretch, width = activations.shape[3:]
     deep = w_query.shape[0]
     seq = document_ids.shape[1]
-    tokens = zs * 2 * stretch
+    pair = 2 * seq
     wide = w_gate.shape[1] // (4 * zs)
     x = activations.reshape(2, stretch, width)
     cot = cotangent.reshape(2, stretch, width)
     small = jnp.stack([attn_gain.astype(F32), mlp_gain.astype(F32)])
     docs_rows = document_ids.astype(F32).reshape(seq // deep, deep)
     small = jnp.concatenate([small, docs_rows, jnp.zeros((6 - seq // deep, deep), F32)])
-    x_all, qkv_w, out_w, small_z, small_x = call(
-        functools.partial(open_kernel, zs),
+    cosine, sine = (jnp.asarray(table) for table in rope_tables(seq))
+    half = stretch // 2
+    hidden, qkv, attended, qkv_w, out_w, gains, docs, middle, h2_all, cot_all, gu_w, down_w = call(
+        functools.partial(forward_kernel, zs),
         1,
         [
-            ((2, zs, 2, stretch, width), BF, ANY),
+            ((pair, width), BF, ANY),
+            ((pair, 3 * HEAD_DIM), BF, ANY),
+            ((pair, HEAD_DIM), BF, ANY),
             ((width, 3 * HEAD_DIM), BF, ANY),
             ((HEAD_DIM, width), BF, ANY),
-            ((zs, 8, deep), F32, ANY),
-            ((2, 8, deep), F32, ANY),
-        ],
-        [],
-        64,
-        (x, w_query, w_key, w_value, w_out, small),
-    )
-    gain_one = small_z[:, 0].reshape(1, width)
-    gain_two = small_z[:, 1].reshape(1, width)
-    docs = small_x[:, 2 : 2 + seq // deep].reshape(2, seq)
-    slots = jnp.arange(tokens, dtype=jnp.int32)
-    owners = slots // (2 * stretch)
-    halves = slots // stretch % 2
-    places = jnp.where(halves == 0, owners, 2 * zs - 1 - owners) * stretch + slots % stretch
-    cosine, sine = rope_tables(places)
-    docs = jnp.take(docs, places, axis=1)
-    visible = (docs[:, :, None] == docs[:, None, :]) & (places[None, None, :] <= places[None, :, None])
-
-    flat = x_all.reshape(2 * tokens, width).astype(F32)
-    inverse = lax.rsqrt(jnp.mean(flat * flat, axis=-1, keepdims=True) + EPS)
-    hidden = (flat * inverse * gain_one).astype(BF)
-    qkv = dot(hidden, qkv_w).reshape(2, tokens, 3, HEAD_DIM)
-    queries = turn(qkv[:, :, 0], cosine, sine).astype(BF)
-    keys = turn(qkv[:, :, 1], cosine, sine).astype(BF)
-    values = qkv[:, :, 2].astype(BF)
-    scale = HEAD_DIM**-0.5
-    sigma = jax.nn.sigmoid(bdot(queries, keys, ((2,), (2,))) * scale - SHIFT)
-    weights = jnp.where(visible, sigma, 0.0).astype(BF)
-    attended = bdot(weights, values, ((2,), (1,))).astype(BF).reshape(2 * tokens, HEAD_DIM)
-    part = dot(attended, out_w, kind=BF).reshape(2, zs, 2, stretch, width)
-
-    middle, h2_all, cot_all, gu_w, down_w = call(
-        functools.partial(middle_kernel, zs),
-        2,
-        [
+            ((8, width), F32, ANY),
+            ((8, seq), F32, ANY),
             ((stretch, width), F32, ANY),
             ((4, zs, 2, stretch, width), BF, ANY),
             ((4, zs, 2, stretch, width), BF, ANY),
@@ -805,21 +962,33 @@
             ((wide, width), BF, ANY),
         ],
         [
-            VMEM((2, zs, stretch, width), BF),
+            VMEM((pair, width), BF),
+            VMEM((pair, width), BF),
+            VMEM((width, 3 * HEAD_DIM), BF),
+            VMEM((HEAD_DIM, width), BF),
+            VMEM((zs, 8, deep), F32),
+            VMEM((2, 8, deep), F32),
+            VMEM((8, width), F32),
+            VMEM((8, seq), F32),
+            VMEM((seq, HEAD_DIM), F32),
+            VMEM((seq, HEAD_DIM), F32),
+            VMEM((pair, 3 * HEAD_DIM), BF),
+            VMEM((pair, HEAD_DIM), BF),
+            VMEM((2, 2, zs, stretch, width), BF),
             VMEM((2, zs, stretch, width), BF),
             VMEM((zs, stretch, width), BF),
             VMEM((zs, stretch, width), BF),
             VMEM((stretch, width), BF),
             VMEM((stretch, width), BF),
-            VMEM((8, width), F32),
             VMEM((stretch, width), F32),
         ],
-        160,
-        (part, x, jnp.broadcast_to(gain_two, (8, width)), w_gate, w_up, w_down, cot),
-    )
-
-    h2 = h2_all.reshape(4 * tokens, width)
-    cots = cot_all.reshape(4 * tokens, width)
+        240,
+        (x, w_query, w_key, w_value, w_out, small, cosine, sine, w_gate, w_up, w_down, cot),
+        52,
+    )
+
+    h2 = h2_all.reshape(4 * seq, width)
+    cots = cot_all.reshape(4 * seq, width)
     gate_up = dot(h2, gu_w)
     gate, upward = gate_up[:, :wide], gate_up[:, wide:]
     grad_product = dot(cots, down_w, ((1,), (1,)))
@@ -834,7 +1003,6 @@
     gu_grad = dot(h2, grad_gu, ((0,), (0,)), BF)
     down_grad = dot(product, cots, ((0,), (0,)), BF)
 
-    half = stretch // 2
     sum_scratch = [
         VMEM((4, zs, stretch, width), BF),
         VMEM((4, zs, stretch, width), BF),
@@ -842,80 +1010,63 @@
         VMEM((2, zs, half, width), BF),
         VMEM((zs, stretch, width), BF),
     ]
-    gbr_all, grad_mid, layer_out, gain_part, gate_g, up_g, down_g = call(
-        functools.partial(back_kernel, zs),
-        3,
+    layer_out, input_grad, q_g, k_g, v_g, o_g, gate_g, up_g, down_g, gains_g = call(
+        functools.partial(backward_kernel, zs),
+        2,
         [
-            ((2, zs, 2, stretch, width), BF, ANY),
-            ((stretch, width), F32, ANY),
             ((2, stretch, width), BF, ANY),
-            ((8, width), F32, ANY),
-            (w_gate.shape, BF, ANY),
-            (w_up.shape, BF, ANY),
-            (w_down.shape, BF, ANY),
-        ],
-        sum_scratch
-        + sum_scratch
-        + [
-            VMEM((stretch, width), F32),
-            VMEM((stretch, width), BF),
-            VMEM((8, width), F32),
-            VMEM((stretch, width), F32),
-            VMEM((stretch, width), BF),
-            VMEM((8, width), F32),
-            VMEM((stretch, width), BF),
-        ],
-        256,
-        (gh_part, feed_part, gu_grad, down_grad, middle, cot, jnp.broadcast_to(gain_two, (8, width))),
-        vmem=48,
-    )
-
-    grad_branch = gbr_all.reshape(2 * tokens, width)
-    grad_attended = dot(grad_branch, out_w, ((1,), (1,)), BF)
-    heads_grad = grad_attended.reshape(2, tokens, HEAD_DIM)
-    grad_weights = bdot(heads_grad, values, ((2,), (2,)))
-    grad_scores = jnp.where(visible, grad_weights * sigma * (1.0 - sigma), 0.0).astype(BF)
-    grad_queries = bdot(grad_scores, keys, ((2,), (1,))) * scale
-    grad_keys = bdot(grad_scores, queries, ((1,), (1,))) * scale
-    grad_values = bdot(weights, heads_grad, ((1,), (1,)))
-    grad_qkv = jnp.concatenate(
-        [turn(grad_queries, cosine, -sine), turn(grad_keys, cosine, -sine), grad_values], axis=-1
-    )
-    grad_qkv = grad_qkv.astype(BF).reshape(2 * tokens, 3 * HEAD_DIM)
-    gh_one = dot(grad_qkv, qkv_w, ((1,), (1,)), BF).reshape(2, zs, 2, stretch, width)
-    qkv_grad = dot(hidden, grad_qkv, ((0,), (0,)), BF)
-    out_grad = dot(attended, grad_branch, ((0,), (0,)), BF)
-
-    input_grad, q_g, k_g, v_g, o_g, gains_g = call(
-        functools.partial(close_kernel, zs),
-        4,
-        [
             ((2, stretch, width), BF, ANY),
             (w_query.shape, BF, ANY),
             (w_key.shape, BF, ANY),
             (w_value.shape, BF, ANY),
             (w_out.shape, BF, ANY),
+            (w_gate.shape, BF, ANY),
+            (w_up.shape, BF, ANY),
+            (w_down.shape, BF, ANY),
             ((2, 8, deep), F32, VMEM),
         ],
-        [
-            VMEM((2, zs, stretch, width), BF),
+        sum_scratch
+        + sum_scratch
+        + [
+            VMEM((2, 2, zs, stretch, width), BF),
             VMEM((2, zs, stretch, width), BF),
             VMEM((zs, stretch, width), BF),
             VMEM((zs, stretch, width), BF),
+            VMEM((pair, width), BF),
+            VMEM((pair, 3 * HEAD_DIM), BF),
+            VMEM((pair, HEAD_DIM), BF),
+            VMEM((width, 3 * HEAD_DIM), BF),
+            VMEM((HEAD_DIM, width), BF),
+            VMEM((pair, width), BF),
+            VMEM((pair, 3 * HEAD_DIM), BF),
+            VMEM((8, width), F32),
+            VMEM((8, seq), F32),
+            VMEM((seq, HEAD_DIM), F32),
+            VMEM((seq, HEAD_DIM), F32),
+            VMEM((seq, HEAD_DIM), BF),
+            VMEM((stretch, width), F32),
             VMEM((stretch, width), BF),
-            VMEM((8, width), F32),
+            VMEM((stretch, width), BF),
             VMEM((stretch, width), F32),
+            VMEM((stretch, width), BF),
+            VMEM((stretch, width), BF),
+            VMEM((stretch, width), BF),
             VMEM((2, 8, width), F32),
-            VMEM((stretch, width), BF),
+            VMEM((3, 2, 8, width), F32),
+            VMEM((zs, 2, 8, deep), F32),
             VMEM((zs, deep // 2, 3 * HEAD_DIM), BF),
             VMEM((zs, deep // 2, 3 * HEAD_DIM), BF),
+            VMEM((zs, deep // 2, 3 * HEAD_DIM), BF),
+            VMEM((zs, HEAD_DIM, deep), BF),
             VMEM((zs, HEAD_DIM // 2, deep), BF),
             VMEM((zs, HEAD_DIM // 2, deep), BF),
-            VMEM((3, 2, 8, width), F32),
-            VMEM((zs, 2, 8, deep), F32),
         ],
-        160,
-        (gh_one, qkv_grad, out_grad, grad_mid, x, jnp.broadcast_to(gain_one, (8, width)), gain_part),
+        400,
+        (
+            gh_part, feed_part, gu_grad, down_grad, middle, cot, x, gains, docs, cosine, sine,
+            hidden, qkv, attended, qkv_w, out_w,
+        ),
+        60,
     )
     gain_grads = jnp.sum(gains_g, axis=1)
     return (

time: 743 us -> 575 us (0.77); the launches traced: 730 us -> 572 us
  Pallas kernels: 604 us -> 504 us
  matrix products: 66.4 us -> 37.6 us
  local copies, waits for them, and re-layouts: 23.2 us -> 4.23 us
  other arithmetic: 34.3 us -> 25.5 us
    pallas_call x4 -> x2, Pallas kernels: 604 us -> 504 us  [call(): pl.pallas_call(kernel, out_shape=[jax.ShapeDtypeStruct(shape, kind) for s...]
    dot_general x12 -> x6, matrix products: 57.9 us -> 37.6 us  [dot(): lax.dot_general(left, right, (dims, ((), ())), preferred_element_type=F32)]
    concatenate x5 -> x0, local copies, waits for them, and re-layouts: 8.58 us -> none  [heads_shards(): jnp.concatenate([turn(grad_queries, cosine, -sine), turn(grad_keys, cosin...]
    dot_general x6 -> x0, matrix products: 8.5 us -> none  [bdot(): lax.dot_general(left, right, (dims, ((0,), (0,))), preferred_element_type...]
where the time goes in v2:
time: 575 us; the launch traced here: 572 us
  Pallas kernels  504 us (88%)
  matrix products  37.6 us (7%)
  other arithmetic  25.5 us (4%)
    pallas_call x2, Pallas kernels, call(): pl.pallas_call(kernel, out_shape=[jax.ShapeDtypeStruct(shape, kind) for s...  504 us
    dot_general x6, matrix products, dot(): lax.dot_general(left, right, (dims, ((), ())), preferred_element_type=F32)  37.6 us

profile of v2, /device:TPU:0, one launch (start us, length us, event | category | flops | bytes accessed | tf_op | source)
XLA Modules:
  0.0 572.4 jit_solution(15124663340736203347)
XLA Ops:
  0.7 0.1 pad.5.clone
  0.7 0.7 convert_element_type.47
  1.4 0.7 stack.16
  2.1 0.7 stack.17
  2.8 0.1 maximum_maximum_fusion.small
  2.9 0.9 copy-done
  3.8 0.9 copy-done.1
  4.7 197.2 %shard_map.221 = (bf16[1024,2048]{1,0:T(8,128)(2,1)}, bf16[1024,384]{1,0:T(8,128)(2,1)}, bf16[1024,128]{1,0:T(8,128)(2,1)S(1)}, bf16[2048,384]{1,0:T(8,128)(2,1)...) custom-call(bf16[2,64,2048]{2,1,0:T(8,128)(2,1)} %bitcast.24, ...), custom_call_target="tpu_custom_call" | custom-call | tf_op jit(solution)/shard_map/pallas_call | solution.py:443
  202.0 0.0 copy-start.2
  202.0 0.0 copy-start.3
  202.0 0.0 copy-start.4
  202.0 0.0 copy-start.5
  202.0 0.0 copy-start.6
  202.0 0.0 copy-start.12
  202.0 0.0 slice-start
  202.1 8.3 %fusion.4 = f32[2048,512]{0,1:T(8,128)S(1)} fusion(bf16[2048,2048]{1,0:T(8,128)(2,1)} %bitcast.34, bf16[2048,512]{1,0:T(8,128)(2,1)} %get-tuple-element.36), kind=kOutput, calls=%fused_computation.14 | convolution fusion | flops 4294967296 | bytes 14680064 | tf_op jit(solution)/shard_map/dot_general | solution.py:417
  210.4 0.0 copy-done.2
  210.4 0.0 copy-done.3
  210.4 0.0 copy-done.4
  210.4 0.0 copy-done.5
  210.4 0.0 copy-done.6
  210.4 0.0 copy-done.12
  210.4 0.0 copy-start.15
  210.4 0.0 slice-start.1
  210.4 6.7 %multiply_convert_fusion.2 = (bf16[2048,256]{0,1:T(8,128)(2,1)S(1)}, bf16[2048,256]{0,1:T(8,128)(2,1)S(1)}, bf16[2048,256]{0,1:T(8,128)(2,1)S(1)}) fusion(f32[2048,512]{0,1:T(8,128)S(1)} %fusion.4, bf16[2048,2048]{1,0:T(8,128)(2,1)} %bitcast.38, bf16[256,2048]{1,0:T(8,128)(2,1)S(1)} %copy-done.12), kind=kOutput, calls=%fused_computation.7 | convolution fusion | flops 2155347968 | bytes 16777216 | tf_op jit(solution)/shard_map/dot_general | solution.py:417
  217.2 3.4 convolution_convert_fusion.3.down_grad
  220.6 6.6 %convolution_convert_fusion.2.gu_grad = bf16[2048,512]{1,0:T(8,128)(2,1)} fusion(bf16[2048,2048]{1,0:T(8,128)(2,1)S(1)} %bitcast.37, bf16[2048,256]{0,1:T(8,128)(2,1)S(1)} %get-tuple-element.56, bf16[2048,256]{0,1:T(8,128)(2,1)S(1)} %get-tuple-element.55), kind=kOutput, calls=%fused_computation.2 | convolution fusion | flops 4300210176 | bytes 12582912 | tf_op jit(solution)/shard_map/dot_general | solution.py:417
  227.2 0.0 copy-done.16
  227.2 6.8 %convolution_convert_fusion.1 = bf16[2048,2048]{1,0:T(8,128)(2,1)} fusion(bf16[2048,512]{1,0:T(8,128)(2,1)S(1)} %copy-done.16, bf16[2048,256]{0,1:T(8,128)(2,1)S(1)} %get-tuple-element.56, bf16[2048,256]{0,1:T(8,128)(2,1)S(1)} %get-tuple-element.55), kind=kOutput, calls=%fused_computation.1 | convolution fusion | flops 4303355904 | bytes 12582912 | tf_op jit(solution)/shard_map/dot_general | solution.py:417
  234.0 5.8 %convolution_convert_fusion = bf16[2048,2048]{1,0:T(8,128)(2,1)} fusion(bf16[2048,256]{0,1:T(8,128)(2,1)S(1)} %get-tuple-element.57, bf16[256,2048]{1,0:T(8,128)(2,1)S(1)} %copy-done.12), kind=kOutput, calls=%fused_computation | convolution fusion | flops 2151677952 | bytes 10485760 | tf_op jit(solution)/shard_map/dot_general | solution.py:417
  239.8 306.9 %shard_map.222 = (bf16[2,64,2048]{2,1,0:T(8,128)(2,1)}, bf16[2,64,2048]{2,1,0:T(8,128)(2,1)}, bf16[512,1024]{1,0:T(8,128)(2,1)}, bf16[512,1024]{1,0:T(8,128)(2,1...) custom-call(bf16[4,4,2,64,2048]{4,3,2,1,0:T(8,128)(2,1)} %bitcast.23, ...), custom_call_target="tpu_custom_call" | custom-call | tf_op jit(solution)/shard_map/pallas_call | solution.py:443
  546.7 0.9 reduce_sum.9
  547.6 0.6 fusion.3
  548.2 2.9 convert_element_type.55
  551.1 2.9 convert_element_type.56
  554.0 0.0 copy-done.11
  554.0 1.6 convert_element_type.57
  555.6 0.0 copy-done.10
  555.6 1.6 convert_element_type.58
  557.2 4.5 convert_element_type.59
  561.7 0.0 copy-done.8
  561.7 4.5 convert_element_type.60
  566.2 0.0 copy-done.7
  566.2 4.6 convert_element_type.61
  570.8 0.0 copy-done.14
  570.8 0.8 copy.27
  571.6 0.0 copy-done.13
  571.6 0.8 copy.28
  (16 shorter events, 0.0 us)
Async XLA Ops:
  2.8 0.9 copy-start
  3.8 0.9 copy-start.1
  202.0 8.4 %copy-start.2 = (bf16[128,2048]{1,0:T(8,128)(2,1)}, bf16[128,2048]{1,0:T(8,128)(2,1)S(1)}, u32[]{:S(2)}) copy-start(bf16[128,2048]{1,0:T(8,128)(2,1)S(1)} %get-tuple-element.44.out_w_in) | copy-start | bytes 1572868
  202.0 8.4 %copy-start.3 = (f32[64,2048]{1,0:T(8,128)}, f32[64,2048]{1,0:T(8,128)S(1)}, u32[]{:S(2)}) copy-start(f32[64,2048]{1,0:T(8,128)S(1)} %get-tuple-element.37.middle) | copy-start | bytes 1572868
  202.0 8.4 %copy-start.4 = (bf16[1024,128]{1,0:T(8,128)(2,1)}, bf16[1024,128]{1,0:T(8,128)(2,1)S(1)}, u32[]{:S(2)}) copy-start(bf16[1024,128]{1,0:T(8,128)(2,1)S(1)} %get-tuple-element.42.attended_in) | copy-start | bytes 786436
  202.0 8.4 %copy-start.5 = (f32[8,2048]{1,0:T(8,128)}, f32[8,2048]{1,0:T(8,128)S(1)}, u32[]{:S(2)}) copy-start(f32[8,2048]{1,0:T(8,128)S(1)} %get-tuple-element.38.gains_in) | copy-start | bytes 196612
  202.0 8.4 %copy-start.6 = (f32[8,512]{1,0:T(8,128)}, f32[8,512]{1,0:T(8,128)S(1)}, u32[]{:S(2)}) copy-start(f32[8,512]{1,0:T(8,128)S(1)} %get-tuple-element.39.docs_in) | copy-start | bytes 49156
  202.0 8.4 %copy-start.12 = (bf16[256,2048]{1,0:T(8,128)(2,1)S(1)}, bf16[256,2048]{1,0:T(8,128)(2,1)}, u32[]{:S(2)}) copy-start(bf16[256,2048]{1,0:T(8,128)(2,1)} %get-tuple-element.34) | copy-start | bytes 3145732
  202.0 18.5 %slice-start = ((s8[8388608]{0:T(1024)(128)(4,1)}), s8[4194304]{0:T(1024)(128)(4,1)S(1)}, s32[]{:S(2)}) async-start(s8[8388608]{0:T(1024)(128)(4,1)} %bitcast.35), calls=%async_computation | async-start | bytes 8388608
  210.4 6.8 %copy-start.15 = (bf16[4,4,2,64,2048]{4,3,2,1,0:T(8,128)(2,1)S(1)}, bf16[4,4,2,64,2048]{4,3,2,1,0:T(8,128)(2,1)}, u32[]{:S(2)}) copy-start(bf16[4,4,2,64,2048]{4,3,2,1,0:T(8,128)(2,1)} %get-tuple-element.33) | copy-start | bytes 25165828
  210.4 10.2 %slice-start.1 = ((s8[8388608]{0:T(1024)(128)(4,1)}), s8[4194304]{0:T(1024)(128)(4,1)S(1)}, s32[]{:S(2)}) async-start(s8[8388608]{0:T(1024)(128)(4,1)} %bitcast.35), calls=%async_computation.1 | async-start | bytes 8388608
  220.6 6.6 %copy-start.16 = (bf16[2048,512]{1,0:T(8,128)(2,1)S(1)}, bf16[2048,512]{1,0:T(8,128)(2,1)}, u32[]{:S(2)}) copy-start(bf16[2048,512]{1,0:T(8,128)(2,1)} %get-tuple-element.36) | copy-start | bytes 6291460
  546.7 7.3 %copy-start.11 = (bf16[512,1024]{1,0:T(8,128)(2,1)S(1)}, bf16[512,1024]{1,0:T(8,128)(2,1)}, u32[]{:S(2)}) copy-start(bf16[512,1024]{1,0:T(8,128)(2,1)} %get-tuple-element.50) | copy-start | bytes 3145732
  548.2 7.4 %copy-start.10 = (bf16[1024,512]{1,0:T(8,128)(2,1)S(1)}, bf16[1024,512]{1,0:T(8,128)(2,1)}, u32[]{:S(2)}) copy-start(bf16[1024,512]{1,0:T(8,128)(2,1)} %get-tuple-element.51) | copy-start | bytes 3145732
  551.1 6.1 %copy-start.9 = (bf16[512,4096]{1,0:T(8,128)(2,1)S(1)}, bf16[512,4096]{1,0:T(8,128)(2,1)}, u32[]{:S(2)}) copy-start(bf16[512,4096]{1,0:T(8,128)(2,1)} %get-tuple-element.52) | copy-start | bytes 12582916
  557.2 4.5 copy-start.8
  561.7 4.5 copy-start.7
  566.2 4.6 copy-start.14
  566.2 5.4 copy-start.13

commit v3 on v2

--- a/solution.py
+++ b/solution.py
@@ -57,15 +57,27 @@
             pl.semaphore_signal(barrier, inc=1, device_id=way, device_id_type=MESH)
         pl.semaphore_wait(barrier, len(ways))
 
-    def send(self, src, dst, way):
-        k = self.used
+    def slot(self):
         self.used += 1
+        return self.used - 1
+
+    def send(self, src, dst, way, arrive=None, when=None):
+        k = self.slot()
+        arrive = k if arrive is None else arrive
         copy = pltpu.make_async_remote_copy(
-            src, dst, self.send_sems.at[k], self.recv_sems.at[k], device_id=way, device_id_type=MESH
+            src, dst, self.send_sems.at[k], self.recv_sems.at[arrive], device_id=way, device_id_type=MESH
         )
-        copy.start()
-        self.open.append(copy)
+        if when is None:
+            copy.start()
+        else:
+            pl.when(when)(copy.start)
+        self.open.append((copy, when))
         return copy
+
+    def arrival(self, ref, slot):
+        return pltpu.make_async_remote_copy(
+            ref, ref, self.send_sems.at[0], self.recv_sems.at[slot], device_id=self.sibling, device_id_type=MESH
+        )
 
     def keep(self, src, dst):
         k = self.used
@@ -75,40 +87,63 @@
         return copy
 
     def finish(self):
-        for copy in self.open:
-            copy.wait_send()
+        for copy, when in self.open:
+            if when is None:
+                copy.wait_send()
+            else:
+                pl.when(when)(copy.wait_send)
         self.open = []
 
 
-def plane_start(net, place, halves):
-    own = place(net.dp)
-    return net.send(own, own, net.over_x), net.send(own, own, net.over_y)
+class LineGather:
+    def __init__(self, net, src, place):
+        self.net, self.src, self.place = net, src, place
+        self.h, self.low = lax.div(net.z, 2), lax.rem(net.z, 2)
+        self.mate = (net.dp, net.z + 1 - 2 * self.low, net.t)
+        self.gate = (net.dp, 2 - self.h, net.t)
+        self.hands_on = self.h != self.low
+
+    def start(self):
+        net = self.net
+        mine = self.place(net.z)
+        self.near = net.send(self.src, mine, self.mate)
+        self.slots = [net.slot(), net.slot()]
+        net.send(self.src, mine, self.gate, arrive=self.slots[0] + self.low)
+
+    def take(self, s):
+        net = self.net
+        if s == 1:
+            self.near.wait_recv()
+            return net.z + 1 - 2 * self.low
+        z = 2 * (1 - self.h) + s - 2
+        ref = self.place(z)
+        net.arrival(ref, self.slots[s - 2]).wait_recv()
+        net.send(ref, ref, self.mate, arrive=self.slots[s - 2], when=self.hands_on)
+        return z
 
 
 def plane_relay(net, place, halves, over_x, over_y, sibling=None):
     dx, dy = 2 * net.a + 1 - net.b, 2 * (1 - net.a) + net.b
-    dd = 2 * (1 - net.a) + 1 - net.b
-    waits = []
+    relays = []
     over_x.wait_recv()
-    first = halves(place(dx), 0)
-    up = net.send(first, first, net.over_y)
+    first = halves(place(dx), 0) if halves else place(dx)
+    relays.append(net.send(first, first, net.over_y))
     if sibling:
-        waits.append(sibling(dx))
+        sibling(dx)
     over_y.wait_recv()
-    second = halves(place(dy), 1)
-    side = net.send(second, second, net.over_x)
+    if halves:
+        second = halves(place(dy), 1)
+        relays.append(net.send(second, second, net.over_x))
     if sibling:
-        waits.append(sibling(dy))
-    return up, side, dd, waits
-
-
-def plane_end(net, place, halves, state, sibling=None):
-    up, side, dd, waits = state
-    up.wait_recv()
-    side.wait_recv()
+        sibling(dy)
+    return relays
+
+
+def plane_end(net, relays, sibling=None):
+    for copy in relays:
+        copy.wait_recv()
     if sibling:
-        waits.append(sibling(dd))
-    return waits
+        sibling(2 * (1 - net.a) + 1 - net.b)
 
 
 def rows_loop(count, step, body):
@@ -141,37 +176,32 @@
     def start(self):
         net = self.net
         mine = self.place(net.dp, net.z)
+        self.line = LineGather(net, self.src, lambda z: self.place(net.dp, z))
+        self.line.start()
         self.local = net.keep(self.src, mine)
-        self.z_sends = [net.send(self.src, mine, net.along_z(s)) for s in range(1, net.zs)]
         self.plane = [(net.z, net.send(self.src, mine, net.over_x), net.send(self.src, mine, net.over_y))]
         self.twin = [net.send(self.src, mine, net.sibling)]
+        self.states = []
 
     def to_twin(self, dp, z):
         ref = self.place(dp, z)
         self.twin.append(self.net.send(ref, ref, self.net.sibling))
 
-    def spread(self):
-        net = self.net
-        for s in range(1, net.zs):
-            self.z_sends[s - 1].wait_recv()
-            z = net.source_z(s)
-            ref = self.place(net.dp, z)
-            self.plane.append((z, net.send(ref, ref, net.over_x), net.send(ref, ref, net.over_y)))
-            self.to_twin(net.dp, z)
-
-    def relay(self):
-        net = self.net
-        self.states = []
-        for z, over_x, over_y in self.plane:
-            place = functools.partial(self.place, z=z)
-            self.states.append(
-                (z, plane_relay(net, place, self.halves, over_x, over_y, lambda dp, z=z: self.to_twin(dp, z)))
-            )
+    def spread(self, s):
+        net = self.net
+        z = self.line.take(s)
+        ref = self.place(net.dp, z)
+        self.plane.append((z, net.send(ref, ref, net.over_x), net.send(ref, ref, net.over_y)))
+        self.to_twin(net.dp, z)
+
+    def relay(self, s):
+        z, over_x, over_y = self.plane[s]
+        place = functools.partial(self.place, z=z)
+        self.states.append((z, plane_relay(self.net, place, self.halves, over_x, over_y, lambda dp: self.to_twin(dp, z))))
 
     def end(self):
-        for z, state in self.states:
-            place = functools.partial(self.place, z=z)
-            plane_end(self.net, place, self.halves, state, lambda dp, z=z: self.to_twin(dp, z))
+        for z, relays in self.states:
+            plane_end(self.net, relays, lambda dp, z=z: self.to_twin(dp, z))
         for copy in self.twin:
             copy.wait_recv()
         self.local.wait()
@@ -191,7 +221,8 @@
     def start(self):
         net = self.net
         mine = self.place(net.b, net.z)
-        self.z_sends = [net.send(self.src, mine, net.along_z(s)) for s in range(1, net.zs)]
+        self.line = LineGather(net, self.src, lambda z: self.place(net.b, z))
+        self.line.start()
         self.over = [(net.z, net.send(self.src, mine, net.over_x))]
         self.twin, self.local = [], []
         if self.own_lanes is None:
@@ -205,20 +236,19 @@
         ref = self.place(b, z)
         self.twin.append((b, z, self.net.send(ref, ref, self.net.sibling)))
 
-    def spread(self):
-        net = self.net
-        for s in range(1, net.zs):
-            self.z_sends[s - 1].wait_recv()
-            z = net.source_z(s)
-            ref = self.place(net.b, z)
-            self.over.append((z, net.send(ref, ref, net.over_x)))
-            self.to_twin(net.b, z)
-
-    def far(self):
-        net = self.net
-        for z, copy in self.over:
-            copy.wait_recv()
-            self.to_twin(1 - net.b, z)
+    def spread(self, s):
+        net = self.net
+        z = self.line.take(s)
+        ref = self.place(net.b, z)
+        self.over.append((z, net.send(ref, ref, net.over_x)))
+        self.to_twin(net.b, z)
+        return z
+
+    def far(self, s):
+        z, copy = self.over[s]
+        copy.wait_recv()
+        self.to_twin(1 - self.net.b, z)
+        return z
 
     def end(self):
         for _, _, copy in self.twin:
@@ -387,12 +417,11 @@
 
     def relay(self, s):
         z, over_x, over_y = self.plane[s]
-        place = lambda dp: self.dst(dp, z)
-        self.states.append(plane_relay(self.net, place, self.halves, over_x, over_y))
+        self.states.append(plane_relay(self.net, lambda dp: self.dst(dp, z), self.halves, over_x, over_y))
 
     def end(self):
-        for state in self.states:
-            plane_end(self.net, None, self.halves, state)
+        for relays in self.states:
+            plane_end(self.net, relays)
         self.local.wait()
 
 
@@ -497,7 +526,6 @@
         out_sends.append(net.send(wo.at[at], out_w.at[out_rows, mine], net.along_z(s)))
 
     cotan = GatherAll(net, cot.at[net.t], cot_all)
-    cotan.start()
     mlp_waits, mlp_local = [], []
 
     def block(z):
@@ -515,8 +543,6 @@
         src, dst = mlp[k]
         for s in range(1, zs):
             mlp_waits.append(net.send(src(lax.rem(net.z + s, zs)), dst, net.along_z(s)))
-
-    fetch(0)
 
     for copy in small_waits:
         copy.wait_recv()
@@ -544,23 +570,23 @@
     def offset(b, z, t):
         return ((last + 1) * b + z + t * (last - 2 * z)) * rows
 
-    gather.spread()
     for copy in gather.local:
         copy.wait()
     gather.local = []
     for t in (0, 1):
         norm_block(offset(net.b, net.z, t))
     for s in range(1, zs):
-        norm_block(offset(net.b, net.source_z(s), net.t))
+        norm_block(offset(net.b, gather.spread(s), net.t))
+    cotan.start()
+    fetch(0)
     qkv_y = []
     for s in range(1, zs):
+        norm_block(offset(1 - net.b, gather.far(s - 1), net.t))
         for copy in qkv_sends[s - 1]:
             copy.wait_recv()
         at = qkv_w.at[pl.ds(pl.multiple_of(net.source_z(s) * deep + net.a * half, half), half)]
         qkv_y.append(net.send(at, at, net.over_y))
-    gather.far()
-    for z, _ in gather.over:
-        norm_block(offset(1 - net.b, z, net.t))
+    norm_block(offset(1 - net.b, gather.far(zs - 1), net.t))
     out_y = []
     for s in range(1, zs):
         out_sends[s - 1].wait_recv()
@@ -573,7 +599,8 @@
         copy.wait_recv()
     for copy in w_local:
         copy.wait()
-    cotan.spread()
+    for s in range(1, zs):
+        cotan.spread(s)
     for copy in out_y:
         copy.wait_recv()
 
@@ -618,7 +645,8 @@
     branch.take(0)
     branch.take(1)
     branch.along()
-    cotan.relay()
+    for s in range(zs):
+        cotan.relay(s)
     lane.wait()
     branch.end()
 
@@ -635,11 +663,14 @@
     saved.append(net.keep(mid_v, middle))
     hidden = GatherAll(net, h2, h2_all)
     hidden.start()
+    hidden.spread(1)
+    hidden.spread(2)
+    hidden.spread(3)
     fetch(1)
     fetch(2)
-    hidden.spread()
     cotan.end()
-    hidden.relay()
+    for s in range(zs):
+        hidden.relay(s)
     hidden.end()
     for copy in saved:
         copy.wait()
@@ -698,17 +729,18 @@
         ),
     ]
     grads[0].start()
-    grads[1].start()
+    grads[0].spread(0)
     feed.start()
-    for s in range(zs):
-        hidden.first(s)
-    for s in range(zs):
-        hidden.second(s)
-    for s in range(zs):
-        hidden.third(s)
-    for s in range(zs):
-        feed.first(s)
-    grads[2].start()
+    for step, s in (
+        (hidden.first, 0), (hidden.first, 1), (hidden.first, 2), (hidden.second, 0), (hidden.first, 3),
+        (hidden.second, 1), (hidden.third, 0), (hidden.second, 2), (hidden.third, 1), (hidden.second, 3),
+        (hidden.third, 2), (hidden.third, 3),
+    ):
+        step(s)
+    for s in range(1, zs):
+        grads[0].spread(s)
+    feed.first(0)
+    feed.first(1)
     for copy in local:
         copy.wait()
     hidden.end()
@@ -737,14 +769,13 @@
     loop(rows // 16, back_two)
     gather = GatherGroup(net, gbr_v, gbr_all)
     gather.start()
+    for s in range(1, zs):
+        gather.spread(s)
+    grads[1].start()
     for s in range(zs):
-        feed.second(s)
-    gather.spread()
+        grads[0].relay(s)
     for s in range(zs):
-        feed.third(s)
-    for s in range(zs):
-        grads[0].spread(s)
-    gather.far()
+        gather.far(s)
     gather.end()
 
     branch = SumGroup(net, part, sib_1, far_1, landed_1)
@@ -799,8 +830,15 @@
 
         loop(seq // tile, back_one)
         branch.give(k)
-    branch.take(0)
+        if k == 0:
+            feed.first(2)
+            feed.first(3)
+            branch.take(0)
+            for s in range(zs):
+                feed.second(s)
     branch.take(1)
+    for s in range(zs):
+        grads[1].spread(s)
 
     def qkv_grad(z, a):
         at = pl.ds(pl.multiple_of(z * deep + a * half, half), half)
@@ -832,6 +870,9 @@
         )
     loop(zs, ours)
     branch.along()
+    grads[2].start()
+    for s in range(zs):
+        feed.third(s)
 
     def q_place(ref):
         def place(dp, z):
@@ -845,10 +886,10 @@
         return o_out.at[pl.ds(pl.multiple_of((b * zs + z) * HEAD_DIM + a * side, side), side)]
 
     late = [
-        SpreadGrads(net, lambda z, m=m: q_own.at[z, :, pl.ds(m * HEAD_DIM, HEAD_DIM)], q_place(ref), half_rows)
+        SpreadGrads(net, lambda z, m=m: q_own.at[z, :, pl.ds(m * HEAD_DIM, HEAD_DIM)], q_place(ref), None)
         for m, ref in enumerate((q_out, k_out, v_out))
     ]
-    late.append(SpreadGrads(net, lambda z: o_own.at[z], o_place, half_rows))
+    late.append(SpreadGrads(net, lambda z: o_own.at[z], o_place, None))
     for s, (z, q_in, o_in) in enumerate(swaps):
         q_in.wait_recv()
         add_rows(q_own.at[z], [q_own.at[z], q_land.at[z]], half)
@@ -859,8 +900,6 @@
                 grad.go(s + 1)
             else:
                 grad.own()
-    for s in range(zs):
-        grads[1].spread(s)
     branch.end()
 
     def back_last(i):
@@ -872,7 +911,9 @@
     outs = [net.keep(out_v, input_grad.at[net.t])]
     pairs = [net.send(out_v, input_grad.at[net.t], net.sibling)]
     for s in range(zs):
-        grads[0].relay(s)
+        grads[1].relay(s)
+    for s in range(zs):
+        grads[2].spread(s)
     feed.end()
 
     def close(i):
@@ -885,7 +926,7 @@
     for k, way in enumerate((net.sibling, net.over_x, net.over_y)):
         swap = net.send(gsum, g_far.at[k], way)
         swap.wait()
-        net.open = [c for c in net.open if c is not swap]
+        net.open = [c for c in net.open if c[0] is not swap]
         gsum[...] = gsum[...] + g_far[k]
 
     def cut(z):
@@ -897,14 +938,10 @@
         for grad in late:
             grad.spread(s)
     for s in range(zs):
-        grads[2].spread(s)
-    for s in range(zs):
-        grads[1].relay(s)
+        grads[2].relay(s)
     for s in range(zs):
         for grad in late:
             grad.relay(s)
-    for s in range(zs):
-        grads[2].relay(s)
     for grad in grads + late:
         grad.end()
     for copy in outs:
@@ -1362,7 +1399,7 @@
 def layer(sizes, *args):
     heads = args[3].shape[1] // HEAD_DIM
     zs = sizes["cp"]
-    fits = sizes["dp"] == 4 and sizes["tp"] == 2 and heads == 2 * zs
+    fits = sizes["dp"] == 4 and sizes["tp"] == 2 and zs == 4 and heads == 2 * zs
     fits = fits and args[0].shape[3] % 32 == 0 and args[8].shape[1] % (4 * zs * HEAD_DIM) == 0
     fits = fits and args[3].shape[0] % HEAD_DIM == 0 and args[1].shape[1] % args[3].shape[0] == 0
     fits = fits and args[1].shape[1] <= 6 * args[3].shape[0]

time: 575 us -> 531 us (0.923)
  Pallas kernels: 504 us -> 462 us
    pallas_call x2, Pallas kernels: 504 us -> 462 us  [call(): pl.pallas_call(kernel, out_shape=[jax.ShapeDtypeStruct(shape, kind) for s...]
where the time goes in v3:
time: 531 us; the launch traced here: 530 us
  Pallas kernels  462 us (87%)
  matrix products  37.6 us (7%)
  other arithmetic  25.5 us (5%)
    pallas_call x2, Pallas kernels, call(): pl.pallas_call(kernel, out_shape=[jax.ShapeDtypeStruct(shape, kind) for s...  462 us
    dot_general x6, matrix products, dot(): lax.dot_general(left, right, (dims, ((), ())), preferred_element_type=F32)  37.6 us

profile of v3, /device:TPU:0, one launch (start us, length us, event | category | flops | bytes accessed | tf_op | source)
XLA Modules:
  0.0 529.9 jit_solution(6872821625994636344)
XLA Ops:
  0.7 0.1 pad.5.clone
  0.7 0.7 convert_element_type.47
  1.4 0.7 stack.16
  2.1 0.7 stack.17
  2.8 0.1 maximum_maximum_fusion.small
  2.9 0.9 copy-done
  3.8 0.9 copy-done.1
  4.7 174.8 %shard_map.221 = (bf16[1024,2048]{1,0:T(8,128)(2,1)}, bf16[1024,384]{1,0:T(8,128)(2,1)}, bf16[1024,128]{1,0:T(8,128)(2,1)S(1)}, bf16[2048,384]{1,0:T(8,128)(2,1)...) custom-call(bf16[2,64,2048]{2,1,0:T(8,128)(2,1)} %bitcast.24, ...), custom_call_target="tpu_custom_call" | custom-call | tf_op jit(solution)/shard_map/pallas_call | solution.py:472
  179.6 0.0 copy-start.2
  179.6 0.0 copy-start.3
  179.6 0.0 copy-start.4
  179.6 0.0 copy-start.5
  179.6 0.0 copy-start.6
  179.6 0.0 copy-start.12
  179.6 0.0 slice-start
  179.6 8.3 %fusion.4 = f32[2048,512]{0,1:T(8,128)S(1)} fusion(bf16[2048,2048]{1,0:T(8,128)(2,1)} %bitcast.34, bf16[2048,512]{1,0:T(8,128)(2,1)} %get-tuple-element.36), kind=kOutput, calls=%fused_computation.14 | convolution fusion | flops 4294967296 | bytes 14680064 | tf_op jit(solution)/shard_map/dot_general | solution.py:446
  187.9 0.0 copy-done.2
  187.9 0.0 copy-done.3
  188.0 0.0 copy-done.4
  188.0 0.0 copy-done.5
  188.0 0.0 copy-done.6
  188.0 0.0 copy-done.12
  188.0 0.0 copy-start.15
  188.0 0.0 slice-start.1
  188.0 6.7 %multiply_convert_fusion.2 = (bf16[2048,256]{0,1:T(8,128)(2,1)S(1)}, bf16[2048,256]{0,1:T(8,128)(2,1)S(1)}, bf16[2048,256]{0,1:T(8,128)(2,1)S(1)}) fusion(f32[2048,512]{0,1:T(8,128)S(1)} %fusion.4, bf16[2048,2048]{1,0:T(8,128)(2,1)} %bitcast.38, bf16[256,2048]{1,0:T(8,128)(2,1)S(1)} %copy-done.12), kind=kOutput, calls=%fused_computation.7 | convolution fusion | flops 2155347968 | bytes 16777216 | tf_op jit(solution)/shard_map/dot_general | solution.py:446
  194.8 0.0 copy-done.15
  194.8 3.4 convolution_convert_fusion.3.down_grad
  198.2 6.6 %convolution_convert_fusion.2.gu_grad = bf16[2048,512]{1,0:T(8,128)(2,1)} fusion(bf16[2048,2048]{1,0:T(8,128)(2,1)S(1)} %bitcast.37, bf16[2048,256]{0,1:T(8,128)(2,1)S(1)} %get-tuple-element.56, bf16[2048,256]{0,1:T(8,128)(2,1)S(1)} %get-tuple-element.55), kind=kOutput, calls=%fused_computation.2 | convolution fusion | flops 4300210176 | bytes 12582912 | tf_op jit(solution)/shard_map/dot_general | solution.py:446
  204.8 0.0 copy-done.16
  204.8 6.8 %convolution_convert_fusion.1 = bf16[2048,2048]{1,0:T(8,128)(2,1)} fusion(bf16[2048,512]{1,0:T(8,128)(2,1)S(1)} %copy-done.16, bf16[2048,256]{0,1:T(8,128)(2,1)S(1)} %get-tuple-element.56, bf16[2048,256]{0,1:T(8,128)(2,1)S(1)} %get-tuple-element.55), kind=kOutput, calls=%fused_computation.1 | convolution fusion | flops 4303355904 | bytes 12582912 | tf_op jit(solution)/shard_map/dot_general | solution.py:446
  211.6 5.8 %convolution_convert_fusion = bf16[2048,2048]{1,0:T(8,128)(2,1)} fusion(bf16[2048,256]{0,1:T(8,128)(2,1)S(1)} %get-tuple-element.57, bf16[256,2048]{1,0:T(8,128)(2,1)S(1)} %copy-done.12), kind=kOutput, calls=%fused_computation | convolution fusion | flops 2151677952 | bytes 10485760 | tf_op jit(solution)/shard_map/dot_general | solution.py:446
  217.4 286.8 %shard_map.222 = (bf16[2,64,2048]{2,1,0:T(8,128)(2,1)}, bf16[2,64,2048]{2,1,0:T(8,128)(2,1)}, bf16[512,1024]{1,0:T(8,128)(2,1)}, bf16[512,1024]{1,0:T(8,128)(2,1...) custom-call(bf16[4,4,2,64,2048]{4,3,2,1,0:T(8,128)(2,1)} %bitcast.23, ...), custom_call_target="tpu_custom_call" | custom-call | tf_op jit(solution)/shard_map/pallas_call | solution.py:472
  504.2 0.9 reduce_sum.9
  505.1 0.6 fusion.3
  505.7 2.9 convert_element_type.55
  508.6 2.9 convert_element_type.56
  511.5 0.0 copy-done.11
  511.5 1.6 convert_element_type.57
  513.1 0.0 copy-done.10
  513.1 1.6 convert_element_type.58
  514.7 0.0 copy-done.9
  514.7 4.5 convert_element_type.59
  519.2 0.0 copy-done.8
  519.2 4.5 convert_element_type.60
  523.7 4.6 convert_element_type.61
  528.3 0.8 copy.27
  529.1 0.0 copy-done.13
  529.1 0.8 copy.28
  (16 shorter events, 0.0 us)
Async XLA Ops:
  2.8 0.9 copy-start
  3.8 0.9 copy-start.1
  179.6 8.4 %copy-start.2 = (bf16[128,2048]{1,0:T(8,128)(2,1)}, bf16[128,2048]{1,0:T(8,128)(2,1)S(1)}, u32[]{:S(2)}) copy-start(bf16[128,2048]{1,0:T(8,128)(2,1)S(1)} %get-tuple-element.44.out_w_in) | copy-start | bytes 1572868
  179.6 8.4 %copy-start.3 = (f32[64,2048]{1,0:T(8,128)}, f32[64,2048]{1,0:T(8,128)S(1)}, u32[]{:S(2)}) copy-start(f32[64,2048]{1,0:T(8,128)S(1)} %get-tuple-element.37.middle) | copy-start | bytes 1572868
  179.6 8.4 %copy-start.4 = (bf16[1024,128]{1,0:T(8,128)(2,1)}, bf16[1024,128]{1,0:T(8,128)(2,1)S(1)}, u32[]{:S(2)}) copy-start(bf16[1024,128]{1,0:T(8,128)(2,1)S(1)} %get-tuple-element.42.attended_in) | copy-start | bytes 786436
  179.6 8.4 %copy-start.5 = (f32[8,2048]{1,0:T(8,128)}, f32[8,2048]{1,0:T(8,128)S(1)}, u32[]{:S(2)}) copy-start(f32[8,2048]{1,0:T(8,128)S(1)} %get-tuple-element.38.gains_in) | copy-start | bytes 196612
  179.6 8.4 %copy-start.6 = (f32[8,512]{1,0:T(8,128)}, f32[8,512]{1,0:T(8,128)S(1)}, u32[]{:S(2)}) copy-start(f32[8,512]{1,0:T(8,128)S(1)} %get-tuple-element.39.docs_in) | copy-start | bytes 49156
  179.6 8.4 %copy-start.12 = (bf16[256,2048]{1,0:T(8,128)(2,1)S(1)}, bf16[256,2048]{1,0:T(8,128)(2,1)}, u32[]{:S(2)}) copy-start(bf16[256,2048]{1,0:T(8,128)(2,1)} %get-tuple-element.34) | copy-start | bytes 3145732
  179.6 18.5 %slice-start = ((s8[8388608]{0:T(1024)(128)(4,1)}), s8[4194304]{0:T(1024)(128)(4,1)S(1)}, s32[]{:S(2)}) async-start(s8[8388608]{0:T(1024)(128)(4,1)} %bitcast.35), calls=%async_computation | async-start | bytes 8388608
  188.0 6.8 %copy-start.15 = (bf16[4,4,2,64,2048]{4,3,2,1,0:T(8,128)(2,1)S(1)}, bf16[4,4,2,64,2048]{4,3,2,1,0:T(8,128)(2,1)}, u32[]{:S(2)}) copy-start(bf16[4,4,2,64,2048]{4,3,2,1,0:T(8,128)(2,1)} %get-tuple-element.33) | copy-start | bytes 25165828
  188.0 10.2 %slice-start.1 = ((s8[8388608]{0:T(1024)(128)(4,1)}), s8[4194304]{0:T(1024)(128)(4,1)S(1)}, s32[]{:S(2)}) async-start(s8[8388608]{0:T(1024)(128)(4,1)} %bitcast.35), calls=%async_computation.1 | async-start | bytes 8388608
  198.2 6.6 %copy-start.16 = (bf16[2048,512]{1,0:T(8,128)(2,1)S(1)}, bf16[2048,512]{1,0:T(8,128)(2,1)}, u32[]{:S(2)}) copy-start(bf16[2048,512]{1,0:T(8,128)(2,1)} %get-tuple-element.36) | copy-start | bytes 6291460
  504.2 7.3 %copy-start.11 = (bf16[512,1024]{1,0:T(8,128)(2,1)S(1)}, bf16[512,1024]{1,0:T(8,128)(2,1)}, u32[]{:S(2)}) copy-start(bf16[512,1024]{1,0:T(8,128)(2,1)} %get-tuple-element.50) | copy-start | bytes 3145732
  505.7 7.4 %copy-start.10 = (bf16[1024,512]{1,0:T(8,128)(2,1)S(1)}, bf16[1024,512]{1,0:T(8,128)(2,1)}, u32[]{:S(2)}) copy-start(bf16[1024,512]{1,0:T(8,128)(2,1)} %get-tuple-element.51) | copy-start | bytes 3145732
  508.6 6.1 %copy-start.9 = (bf16[512,4096]{1,0:T(8,128)(2,1)S(1)}, bf16[512,4096]{1,0:T(8,128)(2,1)}, u32[]{:S(2)}) copy-start(bf16[512,4096]{1,0:T(8,128)(2,1)} %get-tuple-element.52) | copy-start | bytes 12582916
  514.7 4.5 copy-start.8
  519.2 4.5 copy-start.7
  523.7 4.6 copy-start.14
  523.7 5.4 %copy-start.13 = (bf16[2,64,2048]{2,1,0:T(8,128)(2,1)S(1)}, bf16[2,64,2048]{2,1,0:T(8,128)(2,1)}, u32[]{:S(2)}) copy-start(bf16[2,64,2048]{2,1,0:T(8,128)(2,1)} %get-tuple-element.46) | copy-start | bytes 1572868

commit v4 on v3

--- a/solution.py
+++ b/solution.py
@@ -22,12 +22,13 @@
 
 
 class Net:
-    def __init__(self, zs, send_sems, recv_sems):
+    def __init__(self, zs, send_sems, recv_sems, local_sems):
         self.zs = zs
         self.dp, self.z, self.t = (lax.axis_index(a) for a in ("dp", "cp", "tp"))
         self.a, self.b = lax.div(self.dp, 2), lax.rem(self.dp, 2)
-        self.send_sems, self.recv_sems = send_sems, recv_sems
-        self.used = 0
+        self.send_sems, self.recv_sems, self.local_sems = send_sems, recv_sems, local_sems
+        self.arrivals = 0
+        self.free_locals = list(range(local_sems.shape[0]))
         self.open = []
 
     def along_z(self, s):
@@ -48,24 +49,26 @@
     def sibling(self):
         return (self.dp, self.z, 1 - self.t)
 
-    def meet(self, y=True):
-        ways = [self.along_z(s) for s in range(1, self.zs)] + [self.over_x, self.sibling]
-        if y:
-            ways.append(self.over_y)
+    @property
+    def across(self):
+        return (2 * (1 - self.a) + 1 - self.b, self.z, self.t)
+
+    def meet(self):
+        ways = [self.along_z(s) for s in range(1, self.zs)] + [self.over_x, self.over_y, self.across, self.sibling]
         barrier = pltpu.get_barrier_semaphore()
         for way in ways:
             pl.semaphore_signal(barrier, inc=1, device_id=way, device_id_type=MESH)
         pl.semaphore_wait(barrier, len(ways))
 
     def slot(self):
-        self.used += 1
-        return self.used - 1
+        self.arrivals += 1
+        return self.arrivals - 1
 
     def send(self, src, dst, way, arrive=None, when=None):
-        k = self.slot()
-        arrive = k if arrive is None else arrive
+        arrive = self.slot() if arrive is None else arrive
+        sem = self.send_sems.at[len(self.open)]
         copy = pltpu.make_async_remote_copy(
-            src, dst, self.send_sems.at[k], self.recv_sems.at[arrive], device_id=way, device_id_type=MESH
+            src, dst, sem, self.recv_sems.at[arrive], device_id=way, device_id_type=MESH
         )
         if when is None:
             copy.start()
@@ -80,11 +83,7 @@
         )
 
     def keep(self, src, dst):
-        k = self.used
-        self.used += 1
-        copy = pltpu.make_async_copy(src, dst, self.send_sems.at[k])
-        copy.start()
-        return copy
+        return Kept(self, src, dst)
 
     def finish(self):
         for copy, when in self.open:
@@ -92,7 +91,17 @@
                 copy.wait_send()
             else:
                 pl.when(when)(copy.wait_send)
-        self.open = []
+
+
+class Kept:
+    def __init__(self, net, src, dst):
+        self.net, self.slot = net, net.free_locals.pop(0)
+        self.copy = pltpu.make_async_copy(src, dst, net.local_sems.at[self.slot])
+        self.copy.start()
+
+    def wait(self):
+        self.copy.wait()
+        self.net.free_locals.append(self.slot)
 
 
 class LineGather:
@@ -122,20 +131,28 @@
         return z
 
 
-def plane_relay(net, place, halves, over_x, over_y, sibling=None):
+def plane_relay(net, place, halves, over_x, over_y, ways="xy", sibling=None):
     dx, dy = 2 * net.a + 1 - net.b, 2 * (1 - net.a) + net.b
     relays = []
-    over_x.wait_recv()
-    first = halves(place(dx), 0) if halves else place(dx)
-    relays.append(net.send(first, first, net.over_y))
-    if sibling:
-        sibling(dx)
-    over_y.wait_recv()
-    if halves:
-        second = halves(place(dy), 1)
-        relays.append(net.send(second, second, net.over_x))
-    if sibling:
-        sibling(dy)
+
+    def by_y():
+        over_x.wait_recv()
+        piece = halves(place(dx), 0) if "x" in ways else place(dx)
+        if "y" in ways:
+            relays.append(net.send(piece, piece, net.over_y))
+        if sibling:
+            sibling(dx)
+
+    def by_x():
+        over_y.wait_recv()
+        piece = halves(place(dy), 1) if "y" in ways else place(dy)
+        if "x" in ways:
+            relays.append(net.send(piece, piece, net.over_x))
+        if sibling:
+            sibling(dy)
+
+    for step in (by_x, by_y) if ways == "x" else (by_y, by_x):
+        step()
     return relays
 
 
@@ -197,7 +214,7 @@
     def relay(self, s):
         z, over_x, over_y = self.plane[s]
         place = functools.partial(self.place, z=z)
-        self.states.append((z, plane_relay(self.net, place, self.halves, over_x, over_y, lambda dp: self.to_twin(dp, z))))
+        self.states.append((z, plane_relay(self.net, place, self.halves, over_x, over_y, sibling=lambda dp: self.to_twin(dp, z))))
 
     def end(self):
         for z, relays in self.states:
@@ -298,6 +315,33 @@
             copy.wait_recv()
 
 
+class SumLine(SumGroup):
+    def take(self, k):
+        net = self.net
+        b = net.b if k else 1 - net.b
+        for s, z in enumerate(self.order()):
+            self.twin[k, s].wait_recv()
+            own, last = self.part.at[b, net.t, z], s == net.zs - 1
+            out = self.landed.at[b, net.z] if last else own
+            add_rows(out, [own, self.sib.at[b, z]], self.rows)
+            if not last:
+                self.z_sends.append(net.send(own, self.landed.at[b, net.z], net.along_z(s + 1)))
+
+    def across(self):
+        net = self.net
+        b = 1 - net.b
+        for copy in self.z_sends[: net.zs - 1]:
+            copy.wait_recv()
+        out = self.part.at[b, net.t, net.z]
+        add_rows(out, [self.landed.at[b, z] for z in range(net.zs)], self.rows)
+        self.over = net.send(out, self.far, net.over_x)
+
+    def end(self):
+        for copy in self.z_sends[self.net.zs - 1 :]:
+            copy.wait_recv()
+        self.over.wait_recv()
+
+
 class SumAll:
     def __init__(self, net, part, own, sib, one, two, landed):
         self.net, self.part, self.own, self.sib = net, part, own, sib
@@ -316,9 +360,8 @@
         net = self.net
         self.twin, self.mine = [], []
         for z in self.order():
-            for dp in self.places():
-                self.twin.append(net.send(self.part.at[dp, z, 1 - net.t], self.sib.at[dp, z], net.sibling))
-                self.mine.append(net.keep(self.part.at[dp, z, net.t], self.own.at[dp, z]))
+            self.twin.append(net.send(self.part.at[:, z, 1 - net.t], self.sib.at[:, z], net.sibling))
+            self.mine.append(net.keep(self.part.at[:, z, net.t], self.own.at[:, z]))
 
     def upper(self, ref):
         return ref.at[pl.ds(0, self.half)]
@@ -330,9 +373,9 @@
         net = self.net
         z = self.order()[s]
         dd, dx, dy, me = self.places()
-        for j, dp in enumerate((dd, dx, dy, me)):
-            self.twin[4 * s + j].wait_recv()
-            self.mine[4 * s + j].wait()
+        self.twin[s].wait_recv()
+        self.mine[s].wait()
+        for dp in (dd, dx, dy, me):
             add_rows(self.own.at[dp, z], [self.own.at[dp, z], self.sib.at[dp, z]], 2 * self.half)
         self.ones = getattr(self, "ones", [])
         self.ones.append(
@@ -385,9 +428,9 @@
 
 
 class SpreadGrads:
-    def __init__(self, net, src, dst, halves):
-        self.net, self.src, self.dst, self.halves = net, src, dst, halves
-        self.z_sends, self.plane, self.states = [], {}, []
+    def __init__(self, net, src, dst, ways):
+        self.net, self.src, self.dst, self.ways = net, src, dst, ways
+        self.z_sends, self.plane, self.states = {}, {}, []
 
     def mine(self):
         return self.dst(self.net.dp, self.net.z)
@@ -402,14 +445,14 @@
 
     def go(self, s):
         net = self.net
-        self.z_sends.append(net.send(self.src(lax.rem(net.z + s, net.zs)), self.mine(), net.along_z(s)))
+        self.z_sends[s] = net.send(self.src(lax.rem(net.z + s, net.zs)), self.mine(), net.along_z(s))
 
     def spread(self, s):
         net = self.net
         z = net.source_z(s)
         ref = self.dst(net.dp, z)
         if s:
-            self.z_sends[s - 1].wait_recv()
+            self.z_sends[s].wait_recv()
             src = ref
         else:
             src = self.src(net.z)
@@ -417,7 +460,7 @@
 
     def relay(self, s):
         z, over_x, over_y = self.plane[s]
-        self.states.append(plane_relay(self.net, lambda dp: self.dst(dp, z), self.halves, over_x, over_y))
+        self.states.append(plane_relay(self.net, lambda dp: self.dst(dp, z), half_rows, over_x, over_y, self.ways))
 
     def end(self):
         for relays in self.states:
@@ -468,13 +511,13 @@
     return jax.nn.sigmoid(dot(left, right, ((1,), (1,))) * HEAD_DIM**-0.5 - SHIFT)
 
 
-def call(kernel, name, outs, scratch, count, args, vmem):
+def call(kernel, name, outs, scratch, counts, args, vmem):
     return pl.pallas_call(
         kernel,
         out_shape=[jax.ShapeDtypeStruct(shape, kind) for shape, kind, _ in outs],
         in_specs=[pl.BlockSpec(memory_space=ANY)] * len(args),
         out_specs=[pl.BlockSpec(memory_space=space) for _, _, space in outs],
-        scratch_shapes=list(scratch) + [pltpu.SemaphoreType.DMA((count,)), pltpu.SemaphoreType.DMA((count,))],
+        scratch_shapes=list(scratch) + [pltpu.SemaphoreType.DMA((count,)) for count in counts],
         compiler_params=pltpu.CompilerParams(
             collective_id=name, has_side_effects=True, vmem_limit_bytes=vmem * MIB
         ),
@@ -485,9 +528,9 @@
     zs, x, wq, wk, wv, wo, small, cosine, sine, wg, wu, wd, cot,
     hidden_out, qkv_out, attended_out, qkv_w_out, out_w_out, gains_out, docs_out, middle, h2_all, cot_all, gu_w, down_w,
     x_all, h1, qkv_w, out_w, small_z, small_x, gains, docs, cos_v, sin_v, qkv, attended, part, sib, far, landed,
-    x_lane, h2, mid_v, send_sems, recv_sems,
+    x_lane, h2, mid_v, send_sems, recv_sems, local_sems,
 ):
-    net = Net(zs, send_sems, recv_sems)
+    net = Net(zs, send_sems, recv_sems, local_sems)
     net.meet()
     deep, wide = wg.shape[0], gu_w.shape[1] // 2
     seq = docs.shape[1]
@@ -681,15 +724,27 @@
     net.finish()
 
 
+ORDER = (
+    "g2s0", "hstart", "F0", "g0z", "F1", "F2", "S0", "F3", "S1", "fstart", "T0", "g0s0", "S2", "g0r0",
+    "T1", "S3", "fF0", "T2", "g0s1", "fF1", "T3", "g1s0", "hend", "gstart", "fF2", "gs1", "g2z", "g0s2",
+    "g0r1", "g0s3", "fF3", "fS0", "gs2", "gs3", "g2s1", "gf0", "fS1", "gf1", "g1z", "g1s1", "gf2", "gf3",
+    "gend", "g2s2", "fT0", "A0", "fS2", "g2r0", "B0", "A1", "g1s2", "g1s3", "B1", "W1", "bt0", "W2",
+    "sw0", "g2s3", "g2r1", "sw1", "sw2", "g1r0", "sw3", "Ls0", "Ls1", "bt1", "fS3", "Lr0", "g1r1", "fT1",
+    "Ls2", "fT2", "g1r2", "bx", "g1r3", "Lr1", "Ls3", "g0r2", "g2r2", "Lr2", "fT3", "bend", "gain2", "Lr3",
+    "g0r3", "fend", "gain3", "g2r3",
+)
+RELAY_WAYS = ("y", "x", "xy", "y", "xy", "xy", "xy")
+
+
 def backward_kernel(
     zs, gh_part, feed_part, gu_grad, down_grad, middle, cot, x, gains_in, docs_in, cosine, sine,
     hidden_in, qkv_in, attended_in, qkv_w_in, out_w_in,
     layer_out, input_grad, q_out, k_out, v_out, o_out, gate_out, up_out, down_out, gains_out,
     own, sib, one, two, landed, own_f, sib_f, one_f, two_f, landed_f, part, sib_1, far_1, landed_1,
     h1, qkv, attended, qkv_w, out_w, gbr_all, gqkv, gains, docs, cos_v, sin_v, hg, mid_v, cot_v, x_v, gm_v, gbr_v, out_v,
-    lo_v, gsum, g_far, g_land, q_give, q_own, q_land, o_part, o_own, o_land, send_sems, recv_sems,
+    lo_v, gsum, gall, gsum_z, g_far, g_land, q_give, q_own, q_land, o_part, o_own, o_land, send_sems, recv_sems, local_sems,
 ):
-    net = Net(zs, send_sems, recv_sems)
+    net = Net(zs, send_sems, recv_sems, local_sems)
     net.meet()
     deep, wide = gate_out.shape[0], gu_grad.shape[1] // 2
     seq = docs.shape[1]
@@ -698,7 +753,6 @@
     last = 2 * zs - 1
     scale = HEAD_DIM**-0.5
     hidden = SumAll(net, gh_part, own, sib, one, two, landed)
-    hidden.start()
     feed = SumAll(net, feed_part, own_f, sib_f, one_f, two_f, landed_f)
     local = [net.keep(middle, mid_v), net.keep(cot.at[net.t], cot_v), net.keep(gains_in, gains)]
     local += [net.keep(x.at[net.t], x_v), net.keep(docs_in, docs), net.keep(cosine, cos_v), net.keep(sine, sin_v)]
@@ -708,43 +762,48 @@
     def block(dp, z):
         return aligned(dp * zs + z, wide)
 
+    ways = iter(RELAY_WAYS)
     grads = [
         SpreadGrads(
             net,
             lambda z: gu_grad.at[aligned(z, deep), pl.ds(0, wide)],
             lambda dp, z: gate_out.at[:, block(dp, z)],
-            half_rows,
+            next(ways),
         ),
         SpreadGrads(
             net,
             lambda z: gu_grad.at[aligned(z, deep), pl.ds(wide, wide)],
             lambda dp, z: up_out.at[:, block(dp, z)],
-            half_rows,
+            next(ways),
         ),
         SpreadGrads(
             net,
             lambda z: down_grad.at[:, aligned(z, deep)],
             lambda dp, z: down_out.at[block(dp, z)],
-            half_rows,
+            next(ways),
         ),
     ]
-    grads[0].start()
-    grads[0].spread(0)
-    feed.start()
-    for step, s in (
-        (hidden.first, 0), (hidden.first, 1), (hidden.first, 2), (hidden.second, 0), (hidden.first, 3),
-        (hidden.second, 1), (hidden.third, 0), (hidden.second, 2), (hidden.third, 1), (hidden.second, 3),
-        (hidden.third, 2), (hidden.third, 3),
-    ):
-        step(s)
-    for s in range(1, zs):
-        grads[0].spread(s)
-    feed.first(0)
-    feed.first(1)
-    for copy in local:
-        copy.wait()
-    hidden.end()
-    gsum[...] = jnp.zeros_like(gsum)
+
+    def q_place(ref):
+        def place(dp, z):
+            a, b = lax.div(dp, 2), lax.rem(dp, 2)
+            return ref.at[pl.ds(pl.multiple_of(a * half, half), half), aligned(b * zs + z, HEAD_DIM)]
+
+        return place
+
+    def o_place(dp, z):
+        a, b = lax.div(dp, 2), lax.rem(dp, 2)
+        return o_out.at[pl.ds(pl.multiple_of((b * zs + z) * HEAD_DIM + a * side, side), side)]
+
+    late = [
+        SpreadGrads(net, lambda z, m=m: q_own.at[z, :, pl.ds(m * HEAD_DIM, HEAD_DIM)], q_place(ref), next(ways))
+        for m, ref in enumerate((q_out, k_out, v_out))
+    ]
+    late.append(SpreadGrads(net, lambda z: o_own.at[z], o_place, next(ways)))
+    branch = SumLine(net, part, sib_1, far_1, landed_1)
+    gather = GatherGroup(net, gbr_v, gbr_all)
+    tile = 128
+    outs, pairs, swaps, plane, z_gain = [], [], [], [], []
 
     def total_of(ref, at):
         total = ref[0, at, :].astype(F32)
@@ -760,31 +819,26 @@
         scaled = total * gain
         return inverse * (scaled - normed * jnp.mean(scaled * normed, axis=-1, keepdims=True))
 
-    def back_two(i):
-        at = aligned(i, 16)
-        grad = cot_v[at, :].astype(F32) + norm_back(mid_v[at, :], total_of(landed, at), gains[1:2, :], 1)
-        gm_v[at, :] = grad
-        gbr_v[at, :] = grad.astype(BF)
-
-    loop(rows // 16, back_two)
-    gather = GatherGroup(net, gbr_v, gbr_all)
-    gather.start()
-    for s in range(1, zs):
-        gather.spread(s)
-    grads[1].start()
-    for s in range(zs):
-        grads[0].relay(s)
-    for s in range(zs):
-        gather.far(s)
-    gather.end()
-
-    branch = SumGroup(net, part, sib_1, far_1, landed_1)
-    tile = 128
-    for k in range(2):
+    def hidden_end():
+        for copy in local:
+            copy.wait()
+        hidden.end()
+        gsum[...] = jnp.zeros_like(gsum)
+
+        def back_two(i):
+            at = aligned(i, 16)
+            grad = cot_v[at, :].astype(F32) + norm_back(mid_v[at, :], total_of(landed, at), gains[1:2, :], 1)
+            gm_v[at, :] = grad
+            gbr_v[at, :] = grad.astype(BF)
+
+        loop(rows // 16, back_two)
+
+    def place_of(k):
         b = net.b if k else 1 - net.b
-        base = b * seq
-        every = pl.ds(pl.multiple_of(base, seq), seq)
-        row = docs[pl.ds(b, 1), :]
+        return b, b * seq, pl.ds(pl.multiple_of(b * seq, seq), seq), docs[pl.ds(b, 1), :]
+
+    def queries_back(k):
+        b, base, every, row = place_of(k)
 
         def heads_grad(i):
             at = pl.ds(pl.multiple_of(base + i * 256, 256), 256)
@@ -803,6 +857,9 @@
             gqkv[at, 0:HEAD_DIM] = turn(gq, cos_v[pos, :], -sin_v[pos, :]).astype(BF)
 
         loop(seq // tile, by_query)
+
+    def keys_back(k):
+        b, base, every, row = place_of(k)
 
         def by_key(i):
             at = pl.ds(pl.multiple_of(base + i * tile, tile), tile)
@@ -830,118 +887,115 @@
 
         loop(seq // tile, back_one)
         branch.give(k)
-        if k == 0:
-            feed.first(2)
-            feed.first(3)
-            branch.take(0)
-            for s in range(zs):
-                feed.second(s)
-    branch.take(1)
-    for s in range(zs):
-        grads[1].spread(s)
 
     def qkv_grad(z, a):
         at = pl.ds(pl.multiple_of(z * deep + a * half, half), half)
         return dot(h1[:, at], gqkv[...], ((0,), (0,)), BF)
 
-    def out_grad(z):
-        o_part[z] = dot(attended[...], gbr_all[:, aligned(z, deep)], ((0,), (0,)), BF)
-
-    def theirs(z):
-        q_give[z] = qkv_grad(z, 1 - net.a)
-
-    def ours(z):
-        q_own[z] = qkv_grad(z, net.a)
-
     def side_rows(a):
         return pl.ds(pl.multiple_of(a * side, side), side)
 
-    loop(zs, out_grad)
-    loop(zs, theirs)
-    swaps = []
-    for s in range(zs):
-        z = lax.rem(net.z + s + 1, zs)
-        swaps.append(
-            (
-                z,
-                net.send(q_give.at[z], q_land.at[z], net.over_y),
-                net.send(o_part.at[z, side_rows(1 - net.a)], o_land.at[z], net.over_y),
+    def weights_give():
+        def out_grad(z):
+            o_part[z] = dot(attended[...], gbr_all[:, aligned(z, deep)], ((0,), (0,)), BF)
+
+        def theirs(z):
+            q_give[z] = qkv_grad(z, 1 - net.a)
+
+        loop(zs, out_grad)
+        loop(zs, theirs)
+        for s in range(zs):
+            z = lax.rem(net.z + s + 1, zs)
+            swaps.append(
+                (
+                    z,
+                    net.send(q_give.at[z], q_land.at[z], net.over_y),
+                    net.send(o_part.at[z, side_rows(1 - net.a)], o_land.at[z], net.over_y),
+                )
             )
-        )
-    loop(zs, ours)
-    branch.along()
-    grads[2].start()
-    for s in range(zs):
-        feed.third(s)
-
-    def q_place(ref):
-        def place(dp, z):
-            a, b = lax.div(dp, 2), lax.rem(dp, 2)
-            return ref.at[pl.ds(pl.multiple_of(a * half, half), half), aligned(b * zs + z, HEAD_DIM)]
-
-        return place
-
-    def o_place(dp, z):
-        a, b = lax.div(dp, 2), lax.rem(dp, 2)
-        return o_out.at[pl.ds(pl.multiple_of((b * zs + z) * HEAD_DIM + a * side, side), side)]
-
-    late = [
-        SpreadGrads(net, lambda z, m=m: q_own.at[z, :, pl.ds(m * HEAD_DIM, HEAD_DIM)], q_place(ref), None)
-        for m, ref in enumerate((q_out, k_out, v_out))
-    ]
-    late.append(SpreadGrads(net, lambda z: o_own.at[z], o_place, None))
-    for s, (z, q_in, o_in) in enumerate(swaps):
+
+    def weights_own():
+        def ours(z):
+            q_own[z] = qkv_grad(z, net.a)
+
+        loop(zs, ours)
+
+    def weights_sum(s):
+        z, q_in, o_in = swaps[s]
         q_in.wait_recv()
         add_rows(q_own.at[z], [q_own.at[z], q_land.at[z]], half)
         o_in.wait_recv()
         add_rows(o_own.at[z], [o_part.at[z, side_rows(net.a)], o_land.at[z]], side)
         for grad in late:
-            if s < zs - 1:
-                grad.go(s + 1)
-            else:
-                grad.own()
-    branch.end()
-
-    def back_last(i):
-        at = aligned(i, 16)
-        grad = gm_v[at, :] + norm_back(x_v[at, :].astype(F32), total_of(landed_1, at), gains[0:1, :], 0)
-        out_v[at, :] = grad.astype(BF)
-
-    loop(rows // 16, back_last)
-    outs = [net.keep(out_v, input_grad.at[net.t])]
-    pairs = [net.send(out_v, input_grad.at[net.t], net.sibling)]
-    for s in range(zs):
-        grads[1].relay(s)
-    for s in range(zs):
-        grads[2].spread(s)
-    feed.end()
-
-    def close(i):
-        at = aligned(i, 16)
-        lo_v[at, :] = (mid_v[at, :] + total_of(landed_f, at)).astype(BF)
-
-    loop(rows // 16, close)
-    outs.append(net.keep(lo_v, layer_out.at[net.t]))
-    pairs.append(net.send(lo_v, layer_out.at[net.t], net.sibling))
-    for k, way in enumerate((net.sibling, net.over_x, net.over_y)):
-        swap = net.send(gsum, g_far.at[k], way)
-        swap.wait()
-        net.open = [c for c in net.open if c[0] is not swap]
-        gsum[...] = gsum[...] + g_far[k]
-
-    def cut(z):
-        return gsum.at[:, :, aligned(z, deep)]
-
-    z_gain = [net.send(cut(lax.rem(net.z + s, zs)), g_land.at[net.z], net.along_z(s)) for s in range(1, zs)]
-    outs.append(net.keep(cut(net.z), g_land.at[net.z]))
-    for s in range(zs):
-        for grad in late:
-            grad.spread(s)
-    for s in range(zs):
-        grads[2].relay(s)
-    for s in range(zs):
-        for grad in late:
-            grad.relay(s)
+            grad.go(s + 1) if s < zs - 1 else grad.own()
+
+    def branch_end():
+        branch.end()
+
+        def back_last(i):
+            at = aligned(i, 16)
+            total = total_of(landed_1.at[net.b], at) + far_1[at, :].astype(F32)
+            grad = gm_v[at, :] + norm_back(x_v[at, :].astype(F32), total, gains[0:1, :], 0)
+            out_v[at, :] = grad.astype(BF)
+
+        loop(rows // 16, back_last)
+        outs.append(net.keep(out_v, input_grad.at[net.t]))
+        pairs.append(net.send(out_v, input_grad.at[net.t], net.sibling))
+        plane.append(net.send(gsum, g_far.at[0], net.sibling))
+
+    def gains_plane():
+        plane[0].wait_recv()
+        gall[...] = gsum[...] + g_far[0]
+        for k, way in ((1, net.over_x), (2, net.over_y), (3, net.across)):
+            plane.append(net.send(gall, g_far.at[k], way))
+
+    def gains_line():
+        for copy in plane[1:]:
+            copy.wait_recv()
+        gsum_z[...] = gall[...] + g_far[1] + g_far[2] + g_far[3]
+
+        def cut(z):
+            return gsum_z.at[:, :, aligned(z, deep)]
+
+        z_gain.extend(net.send(cut(lax.rem(net.z + s, zs)), g_land.at[net.z], net.along_z(s)) for s in range(1, zs))
+        outs.append(net.keep(cut(net.z), g_land.at[net.z]))
+
+    def feed_end():
+        feed.end()
+
+        def close(i):
+            at = aligned(i, 16)
+            lo_v[at, :] = (mid_v[at, :] + total_of(landed_f, at)).astype(BF)
+
+        loop(rows // 16, close)
+        outs.append(net.keep(lo_v, layer_out.at[net.t]))
+        pairs.append(net.send(lo_v, layer_out.at[net.t], net.sibling))
+
+    def each(method):
+        def step(s):
+            for grad in late:
+                getattr(grad, method)(s)
+
+        return step
+
+    steps = {
+        "hstart": hidden.start, "hend": hidden_end, "gstart": gather.start, "gend": gather.end, "fstart": feed.start,
+        "fend": feed_end, "W1": weights_give, "W2": weights_own, "bx": branch.across, "bend": branch_end,
+        "gain2": gains_plane, "gain3": gains_line,
+    }
+    counted = {
+        "F": hidden.first, "S": hidden.second, "T": hidden.third, "fF": feed.first, "fS": feed.second,
+        "fT": feed.third, "gs": gather.spread, "gf": gather.far, "A": queries_back, "B": keys_back, "sw": weights_sum,
+        "bt": branch.take, "Ls": each("spread"), "Lr": each("relay"),
+    }
+    for k, grad in enumerate(grads):
+        steps["g%dz" % k] = grad.start
+        counted["g%ds" % k], counted["g%dr" % k] = grad.spread, grad.relay
+    for name in ORDER:
+        if name in steps:
+            steps[name]()
+        else:
+            counted[name[:-1]](int(name[-1]))
     for grad in grads + late:
         grad.end()
     for copy in outs:
@@ -1019,7 +1073,7 @@
             VMEM((stretch, width), BF),
             VMEM((stretch, width), F32),
         ],
-        240,
+        (134, 131, 34),
         (x, w_query, w_key, w_value, w_out, small, cosine, sine, w_gate, w_up, w_down, cot),
         52,
     )
@@ -1067,8 +1121,8 @@
         + [
             VMEM((2, 2, zs, stretch, width), BF),
             VMEM((2, zs, stretch, width), BF),
-            VMEM((zs, stretch, width), BF),
-            VMEM((zs, stretch, width), BF),
+            VMEM((stretch, width), BF),
+            VMEM((2, zs, stretch, width), BF),
             VMEM((pair, width), BF),
             VMEM((pair, 3 * HEAD_DIM), BF),
             VMEM((pair, HEAD_DIM), BF),
@@ -1089,7 +1143,9 @@
             VMEM((stretch, width), BF),
             VMEM((stretch, width), BF),
             VMEM((2, 8, width), F32),
-            VMEM((3, 2, 8, width), F32),
+            VMEM((2, 8, width), F32),
+            VMEM((2, 8, width), F32),
+            VMEM((4, 2, 8, width), F32),
             VMEM((zs, 2, 8, deep), F32),
             VMEM((zs, deep // 2, 3 * HEAD_DIM), BF),
             VMEM((zs, deep // 2, 3 * HEAD_DIM), BF),
@@ -1098,7 +1154,7 @@
             VMEM((zs, HEAD_DIM // 2, deep), BF),
             VMEM((zs, HEAD_DIM // 2, deep), BF),
         ],
-        400,
+        (232, 231, 34),
         (
             gh_part, feed_part, gu_grad, down_grad, middle, cot, x, gains, docs, cosine, sine,
             hidden, qkv, attended, qkv_w, out_w,
@@ -1400,7 +1456,7 @@
     heads = args[3].shape[1] // HEAD_DIM
     zs = sizes["cp"]
     fits = sizes["dp"] == 4 and sizes["tp"] == 2 and zs == 4 and heads == 2 * zs
-    fits = fits and args[0].shape[3] % 32 == 0 and args[8].shape[1] % (4 * zs * HEAD_DIM) == 0
+    fits = fits and args[0].shape[3] % 32 == 0 and args[8].shape[1] % (2 * zs * HEAD_DIM) == 0
     fits = fits and args[3].shape[0] % HEAD_DIM == 0 and args[1].shape[1] % args[3].shape[0] == 0
     fits = fits and args[1].shape[1] <= 6 * args[3].shape[0]
     if fits:

time: 531 us -> 501 us (0.944)
  Pallas kernels: 462 us -> 433 us
    pallas_call x2, Pallas kernels: 462 us -> 433 us  [call(): pl.pallas_call(kernel, out_shape=[jax.ShapeDtypeStruct(shape, kind) for s...]
where the time goes in v4:
time: 501 us
  Pallas kernels  433 us (86%)
  matrix products  37.6 us (8%)
  other arithmetic  25.5 us (5%)
    pallas_call x2, Pallas kernels, call(): pl.pallas_call(kernel, out_shape=[jax.ShapeDtypeStruct(shape, kind) for s...  433 us
    dot_general x6, matrix products, dot(): lax.dot_general(left, right, (dims, ((), ())), preferred_element_type=F32)  37.6 us

profile of v4, /device:TPU:0, one launch (start us, length us, event | category | flops | bytes accessed | tf_op | source)
XLA Modules:
  0.0 500.8 jit_solution(14575587143794043353)
XLA Ops:
  0.7 0.1 pad.5.clone
  0.7 0.7 convert_element_type.47
  1.4 0.7 stack.16
  2.1 0.7 stack.17
  2.8 0.1 maximum_maximum_fusion.small
  2.9 0.9 copy-done
  3.8 0.9 copy-done.1
  4.7 175.6 %shard_map.221 = (bf16[1024,2048]{1,0:T(8,128)(2,1)}, bf16[1024,384]{1,0:T(8,128)(2,1)}, bf16[1024,128]{1,0:T(8,128)(2,1)S(1)}, bf16[2048,384]{1,0:T(8,128)(2,1)...) custom-call(bf16[2,64,2048]{2,1,0:T(8,128)(2,1)} %bitcast.24, ...), custom_call_target="tpu_custom_call" | custom-call | tf_op jit(solution)/shard_map/pallas_call | solution.py:515
  180.3 0.0 copy-start.2
  180.3 0.0 copy-start.3
  180.3 0.0 copy-start.4
  180.4 0.0 copy-start.5
  180.4 0.0 copy-start.6
  180.4 0.0 copy-start.12
  180.4 0.0 slice-start
  180.4 8.3 %fusion.4 = f32[2048,512]{0,1:T(8,128)S(1)} fusion(bf16[2048,2048]{1,0:T(8,128)(2,1)} %bitcast.34, bf16[2048,512]{1,0:T(8,128)(2,1)} %get-tuple-element.36), kind=kOutput, calls=%fused_computation.14 | convolution fusion | flops 4294967296 | bytes 14680064 | tf_op jit(solution)/shard_map/dot_general | solution.py:489
  188.7 0.0 copy-done.2
  188.7 0.0 copy-done.3
  188.7 0.0 copy-done.4
  188.7 0.0 copy-done.5
  188.7 0.0 copy-done.6
  188.8 0.0 copy-done.12
  188.8 0.0 copy-start.15
  188.8 0.0 slice-start.1
  188.8 6.7 %multiply_convert_fusion.2 = (bf16[2048,256]{0,1:T(8,128)(2,1)S(1)}, bf16[2048,256]{0,1:T(8,128)(2,1)S(1)}, bf16[2048,256]{0,1:T(8,128)(2,1)S(1)}) fusion(f32[2048,512]{0,1:T(8,128)S(1)} %fusion.4, bf16[2048,2048]{1,0:T(8,128)(2,1)} %bitcast.38, bf16[256,2048]{1,0:T(8,128)(2,1)S(1)} %copy-done.12), kind=kOutput, calls=%fused_computation.7 | convolution fusion | flops 2155347968 | bytes 16777216 | tf_op jit(solution)/shard_map/dot_general | solution.py:489
  195.5 0.0 copy-done.15
  195.5 3.4 convolution_convert_fusion.3.down_grad
  198.9 0.0 slice-done
  198.9 0.0 slice-done.1
  198.9 6.6 %convolution_convert_fusion.2.gu_grad = bf16[2048,512]{1,0:T(8,128)(2,1)} fusion(bf16[2048,2048]{1,0:T(8,128)(2,1)S(1)} %bitcast.37, bf16[2048,256]{0,1:T(8,128)(2,1)S(1)} %get-tuple-element.56, bf16[2048,256]{0,1:T(8,128)(2,1)S(1)} %get-tuple-element.55), kind=kOutput, calls=%fused_computation.2 | convolution fusion | flops 4300210176 | bytes 12582912 | tf_op jit(solution)/shard_map/dot_general | solution.py:489
  205.6 0.0 copy-done.16
  205.6 6.8 %convolution_convert_fusion.1 = bf16[2048,2048]{1,0:T(8,128)(2,1)} fusion(bf16[2048,512]{1,0:T(8,128)(2,1)S(1)} %copy-done.16, bf16[2048,256]{0,1:T(8,128)(2,1)S(1)} %get-tuple-element.56, bf16[2048,256]{0,1:T(8,128)(2,1)S(1)} %get-tuple-element.55), kind=kOutput, calls=%fused_computation.1 | convolution fusion | flops 4303355904 | bytes 12582912 | tf_op jit(solution)/shard_map/dot_general | solution.py:489
  212.4 5.8 %convolution_convert_fusion = bf16[2048,2048]{1,0:T(8,128)(2,1)} fusion(bf16[2048,256]{0,1:T(8,128)(2,1)S(1)} %get-tuple-element.57, bf16[256,2048]{1,0:T(8,128)(2,1)S(1)} %copy-done.12), kind=kOutput, calls=%fused_computation | convolution fusion | flops 2151677952 | bytes 10485760 | tf_op jit(solution)/shard_map/dot_general | solution.py:489
  218.2 257.0 %shard_map.222 = (bf16[2,64,2048]{2,1,0:T(8,128)(2,1)}, bf16[2,64,2048]{2,1,0:T(8,128)(2,1)}, bf16[512,1024]{1,0:T(8,128)(2,1)}, bf16[512,1024]{1,0:T(8,128)(2,1...) custom-call(bf16[4,4,2,64,2048]{4,3,2,1,0:T(8,128)(2,1)} %bitcast.23, ...), custom_call_target="tpu_custom_call" | custom-call | tf_op jit(solution)/shard_map/pallas_call | solution.py:515
  475.1 0.0 copy-start.11
  475.1 0.9 reduce_sum.9
  476.0 0.6 fusion.3
  476.6 2.9 convert_element_type.55
  479.5 2.9 convert_element_type.56
  482.4 1.6 convert_element_type.57
  484.0 1.6 convert_element_type.58
  485.6 4.5 convert_element_type.59
  490.1 4.5 convert_element_type.60
  494.6 0.0 copy-done.7
  494.6 4.6 convert_element_type.61
  499.2 0.0 copy-done.14
  499.2 0.8 copy.27
  500.0 0.8 copy.28
  (16 shorter events, 0.0 us)
Async XLA Ops:
  2.8 0.9 copy-start
  3.8 0.9 copy-start.1
  180.3 8.4 %copy-start.2 = (bf16[128,2048]{1,0:T(8,128)(2,1)}, bf16[128,2048]{1,0:T(8,128)(2,1)S(1)}, u32[]{:S(2)}) copy-start(bf16[128,2048]{1,0:T(8,128)(2,1)S(1)} %get-tuple-element.44.out_w_in) | copy-start | bytes 1572868
  180.3 8.4 %copy-start.3 = (f32[64,2048]{1,0:T(8,128)}, f32[64,2048]{1,0:T(8,128)S(1)}, u32[]{:S(2)}) copy-start(f32[64,2048]{1,0:T(8,128)S(1)} %get-tuple-element.37.middle) | copy-start | bytes 1572868
  180.3 8.4 %copy-start.4 = (bf16[1024,128]{1,0:T(8,128)(2,1)}, bf16[1024,128]{1,0:T(8,128)(2,1)S(1)}, u32[]{:S(2)}) copy-start(bf16[1024,128]{1,0:T(8,128)(2,1)S(1)} %get-tuple-element.42.attended_in) | copy-start | bytes 786436
  180.4 8.4 %copy-start.5 = (f32[8,2048]{1,0:T(8,128)}, f32[8,2048]{1,0:T(8,128)S(1)}, u32[]{:S(2)}) copy-start(f32[8,2048]{1,0:T(8,128)S(1)} %get-tuple-element.38.gains_in) | copy-start | bytes 196612
  180.4 8.4 %copy-start.6 = (f32[8,512]{1,0:T(8,128)}, f32[8,512]{1,0:T(8,128)S(1)}, u32[]{:S(2)}) copy-start(f32[8,512]{1,0:T(8,128)S(1)} %get-tuple-element.39.docs_in) | copy-start | bytes 49156
  180.4 8.4 %copy-start.12 = (bf16[256,2048]{1,0:T(8,128)(2,1)S(1)}, bf16[256,2048]{1,0:T(8,128)(2,1)}, u32[]{:S(2)}) copy-start(bf16[256,2048]{1,0:T(8,128)(2,1)} %get-tuple-element.34) | copy-start | bytes 3145732
  180.4 18.5 %slice-start = ((s8[8388608]{0:T(1024)(128)(4,1)}), s8[4194304]{0:T(1024)(128)(4,1)S(1)}, s32[]{:S(2)}) async-start(s8[8388608]{0:T(1024)(128)(4,1)} %bitcast.35), calls=%async_computation | async-start | bytes 8388608
  188.8 6.8 %copy-start.15 = (bf16[4,4,2,64,2048]{4,3,2,1,0:T(8,128)(2,1)S(1)}, bf16[4,4,2,64,2048]{4,3,2,1,0:T(8,128)(2,1)}, u32[]{:S(2)}) copy-start(bf16[4,4,2,64,2048]{4,3,2,1,0:T(8,128)(2,1)} %get-tuple-element.33) | copy-start | bytes 25165828
  188.8 10.2 %slice-start.1 = ((s8[8388608]{0:T(1024)(128)(4,1)}), s8[4194304]{0:T(1024)(128)(4,1)S(1)}, s32[]{:S(2)}) async-start(s8[8388608]{0:T(1024)(128)(4,1)} %bitcast.35), calls=%async_computation.1 | async-start | bytes 8388608
  198.9 6.6 %copy-start.16 = (bf16[2048,512]{1,0:T(8,128)(2,1)S(1)}, bf16[2048,512]{1,0:T(8,128)(2,1)}, u32[]{:S(2)}) copy-start(bf16[2048,512]{1,0:T(8,128)(2,1)} %get-tuple-element.36) | copy-start | bytes 6291460
  475.1 7.3 %copy-start.11 = (bf16[512,1024]{1,0:T(8,128)(2,1)S(1)}, bf16[512,1024]{1,0:T(8,128)(2,1)}, u32[]{:S(2)}) copy-start(bf16[512,1024]{1,0:T(8,128)(2,1)} %get-tuple-element.50) | copy-start | bytes 3145732
  476.6 7.4 %copy-start.10 = (bf16[1024,512]{1,0:T(8,128)(2,1)S(1)}, bf16[1024,512]{1,0:T(8,128)(2,1)}, u32[]{:S(2)}) copy-start(bf16[1024,512]{1,0:T(8,128)(2,1)} %get-tuple-element.51) | copy-start | bytes 3145732
  479.5 6.1 %copy-start.9 = (bf16[512,4096]{1,0:T(8,128)(2,1)S(1)}, bf16[512,4096]{1,0:T(8,128)(2,1)}, u32[]{:S(2)}) copy-start(bf16[512,4096]{1,0:T(8,128)(2,1)} %get-tuple-element.52) | copy-start | bytes 12582916
  485.6 4.5 copy-start.8
  490.1 4.5 copy-start.7
  494.6 4.6 copy-start.14
  494.6 5.4 %copy-start.13 = (bf16[2,64,2048]{2,1,0:T(8,128)(2,1)S(1)}, bf16[2,64,2048]{2,1,0:T(8,128)(2,1)}, u32[]{:S(2)}) copy-start(bf16[2,64,2048]{2,1,0:T(8,128)(2,1)} %get-tuple-element.46) | copy-start | bytes 1572868

commit v5 on v4

--- a/solution.py
+++ b/solution.py
@@ -526,9 +526,9 @@
 
 def forward_kernel(
     zs, x, wq, wk, wv, wo, small, cosine, sine, wg, wu, wd, cot,
-    hidden_out, qkv_out, attended_out, qkv_w_out, out_w_out, gains_out, docs_out, middle, h2_all, cot_all, gu_w, down_w,
+    hidden_out, qkv_out, attended_out, qkv_w_out, out_w_out, gains_out, docs_out, middle, h2_out, cot_out, gu_w_out, down_w_out, gate_out, gp_out,
     x_all, h1, qkv_w, out_w, small_z, small_x, gains, docs, cos_v, sin_v, qkv, attended, part, sib, far, landed,
-    x_lane, h2, mid_v, send_sems, recv_sems, local_sems,
+    x_lane, h2, mid_v, h2_all, cot_all, gu_w, down_w, gate_v, gp_v, send_sems, recv_sems, local_sems,
 ):
     net = Net(zs, send_sems, recv_sems, local_sems)
     net.meet()
@@ -569,7 +569,7 @@
         out_sends.append(net.send(wo.at[at], out_w.at[out_rows, mine], net.along_z(s)))
 
     cotan = GatherAll(net, cot.at[net.t], cot_all)
-    mlp_waits, mlp_local = [], []
+    mlp_waits, mlp_local = {}, {}
 
     def block(z):
         return aligned(net.dp * zs + z, wide)
@@ -579,13 +579,17 @@
         (lambda z: wu.at[:, block(z)], gu_w.at[mine, pl.ds(wide, wide)]),
         (lambda z: wd.at[block(z)], down_w.at[:, mine]),
     )
-    for src, dst in mlp:
-        mlp_local.append(net.keep(src(net.z), dst))
+    for k, (src, dst) in enumerate(mlp):
+        mlp_local[k] = net.keep(src(net.z), dst)
 
     def fetch(k):
         src, dst = mlp[k]
-        for s in range(1, zs):
-            mlp_waits.append(net.send(src(lax.rem(net.z + s, zs)), dst, net.along_z(s)))
+        mlp_waits[k] = [net.send(src(lax.rem(net.z + s, zs)), dst, net.along_z(s)) for s in range(1, zs)]
+
+    def fetched(k):
+        for copy in mlp_waits[k]:
+            copy.wait_recv()
+        mlp_local[k].wait()
 
     for copy in small_waits:
         copy.wait_recv()
@@ -621,7 +625,7 @@
     for s in range(1, zs):
         norm_block(offset(net.b, gather.spread(s), net.t))
     cotan.start()
-    fetch(0)
+    fetch(2)
     qkv_y = []
     for s in range(1, zs):
         norm_block(offset(1 - net.b, gather.far(s - 1), net.t))
@@ -709,31 +713,54 @@
     hidden.spread(1)
     hidden.spread(2)
     hidden.spread(3)
+    fetch(0)
     fetch(1)
-    fetch(2)
     cotan.end()
-    for s in range(zs):
+    saved.append(net.keep(cot_all, cot_out))
+
+    few = 256 // (2 * rows)
+
+    def tiles(body):
+        def one(i):
+            dp, z = lax.div(i, zs // few), pl.ds(lax.rem(i, zs // few) * few, few)
+            body(dp, z, aligned(i, 256))
+
+        loop(4 * zs // few, one)
+
+    def gates(dp, z, at):
+        gate_v[at, :] = dot(h2_all[dp, z].reshape(256, -1), gu_w[:, 0:wide])
+
+    def products(dp, z, at):
+        gp_v[at, :] = dot(cot_all[dp, z].reshape(256, -1), down_w[...], ((1,), (1,)))
+
+    hidden.relay(0)
+    fetched(2)
+    tiles(products)
+    saved += [net.keep(down_w, down_w_out), net.keep(gp_v, gp_out)]
+    for s in range(1, zs):
         hidden.relay(s)
     hidden.end()
+    saved.append(net.keep(h2_all, h2_out))
+    fetched(0)
+    tiles(gates)
+    saved.append(net.keep(gate_v, gate_out))
+    fetched(1)
+    saved.append(net.keep(gu_w, gu_w_out))
     for copy in saved:
         copy.wait()
-    for copy in mlp_waits:
-        copy.wait_recv()
-    for copy in mlp_local:
-        copy.wait()
     net.finish()
 
 
 ORDER = (
-    "g2s0", "hstart", "F0", "g0z", "F1", "F2", "S0", "F3", "S1", "fstart", "T0", "g0s0", "S2", "g0r0",
-    "T1", "S3", "fF0", "T2", "g0s1", "fF1", "T3", "g1s0", "hend", "gstart", "fF2", "gs1", "g2z", "g0s2",
-    "g0r1", "g0s3", "fF3", "fS0", "gs2", "gs3", "g2s1", "gf0", "fS1", "gf1", "g1z", "g1s1", "gf2", "gf3",
-    "gend", "g2s2", "fT0", "A0", "fS2", "g2r0", "B0", "A1", "g1s2", "g1s3", "B1", "W1", "bt0", "W2",
-    "sw0", "g2s3", "g2r1", "sw1", "sw2", "g1r0", "sw3", "Ls0", "Ls1", "bt1", "fS3", "Lr0", "g1r1", "fT1",
-    "Ls2", "fT2", "g1r2", "bx", "g1r3", "Lr1", "Ls3", "g0r2", "g2r2", "Lr2", "fT3", "bend", "gain2", "Lr3",
-    "g0r3", "fend", "gain3", "g2r3",
+    "g0s0", "g0z", "g2s0", "g2z", "hstart", "F0", "g0s1", "F1", "F2", "S0", "F3", "S1", "T0", "fstart",
+    "g0r0", "S2", "fF0", "T1", "S3", "T2", "g2s1", "g2s2", "g2r0", "fS0", "T3", "g2r1", "hend", "gstart",
+    "g2s3", "fF1", "g2r2", "gs1", "gs2", "gs3", "gf0", "gf1", "g1z", "g1s0", "fF2", "g0s2", "g1s1", "gf2",
+    "gf3", "gend", "g0s3", "A0", "B0", "bt0", "g0r1", "fF3", "g1s2", "A1", "B1", "fS1", "g1r0", "W1",
+    "W2", "fT0", "sw0", "g1r1", "sw1", "fS2", "g1s3", "sw2", "g0r2", "bt1", "bx", "sw3", "fT1", "Ls0",
+    "g1r2", "Ls1", "Ls2", "Lr0", "fS3", "Ls3", "g0r3", "fT2", "fT3", "Lr1", "bend", "gain2", "Lr2", "g2r3",
+    "Lr3", "g1r3", "gain3", "fend",
 )
-RELAY_WAYS = ("y", "x", "xy", "y", "xy", "xy", "xy")
+RELAY_WAYS = ("xy", "x", "y", "y", "x", "y", "xy")
 
 
 def backward_kernel(
@@ -1009,6 +1036,24 @@
     net.finish()
 
 
+def widen(*arrays):
+    steps = 16
+
+    def kernel(*refs):
+        for src, dst in zip(refs[: len(arrays)], refs[len(arrays) :], strict=True):
+            dst[...] = src[...].astype(F32)
+
+    specs = [pl.BlockSpec((a.shape[0] // steps, a.shape[1]), lambda i: (i, 0)) for a in arrays]
+    return pl.pallas_call(
+        kernel,
+        grid=(steps,),
+        in_specs=specs,
+        out_specs=specs,
+        out_shape=[jax.ShapeDtypeStruct(a.shape, F32) for a in arrays],
+        compiler_params=pltpu.CompilerParams(vmem_limit_bytes=60 * MIB),
+    )(*arrays)
+
+
 def rope_tables(seq):
     half_dim = HEAD_DIM // 2
     frequency = ROPE_BASE ** (-np.arange(half_dim, dtype=np.float32) / half_dim)
@@ -1035,7 +1080,7 @@
     small = jnp.concatenate([small, docs_rows, jnp.zeros((6 - seq // deep, deep), F32)])
     cosine, sine = (jnp.asarray(table) for table in rope_tables(seq))
     half = stretch // 2
-    hidden, qkv, attended, qkv_w, out_w, gains, docs, middle, h2_all, cot_all, gu_w, down_w = call(
+    hidden, qkv, attended, qkv_w, out_w, gains, docs, middle, h2_all, cot_all, gu_w, down_w, gate, grad_product = call(
         functools.partial(forward_kernel, zs),
         1,
         [
@@ -1051,6 +1096,8 @@
             ((4, zs, 2, stretch, width), BF, ANY),
             ((width, 2 * wide), BF, ANY),
             ((wide, width), BF, ANY),
+            ((4 * seq, wide), F32, ANY),
+            ((4 * seq, wide), F32, ANY),
         ],
         [
             VMEM((pair, width), BF),
@@ -1072,17 +1119,21 @@
             VMEM((stretch, width), BF),
             VMEM((stretch, width), BF),
             VMEM((stretch, width), F32),
+            VMEM((4, zs, 2, stretch, width), BF),
+            VMEM((4, zs, 2, stretch, width), BF),
+            VMEM((width, 2 * wide), BF),
+            VMEM((wide, width), BF),
+            VMEM((4 * seq, wide), F32),
+            VMEM((4 * seq, wide), F32),
         ],
         (134, 131, 34),
         (x, w_query, w_key, w_value, w_out, small, cosine, sine, w_gate, w_up, w_down, cot),
-        52,
+        58,
     )
 
     h2 = h2_all.reshape(4 * seq, width)
     cots = cot_all.reshape(4 * seq, width)
-    gate_up = dot(h2, gu_w)
-    gate, upward = gate_up[:, :wide], gate_up[:, wide:]
-    grad_product = dot(cots, down_w, ((1,), (1,)))
+    upward = dot(h2, gu_w[:, wide:])
     sigma_gate = jax.nn.sigmoid(gate)
     silu = gate * sigma_gate
     product = (silu * upward).astype(BF)
@@ -1162,18 +1213,19 @@
         60,
     )
     gain_grads = jnp.sum(gains_g, axis=1)
+    q_g, k_g, v_g, o_g, gate_g, up_g, down_g = widen(q_g, k_g, v_g, o_g, gate_g, up_g, down_g)
     return (
         layer_out.reshape(activations.shape),
         input_grad.reshape(activations.shape),
         gain_grads[0],
-        q_g.astype(F32),
-        k_g.astype(F32),
-        v_g.astype(F32),
-        o_g.astype(F32),
+        q_g,
+        k_g,
+        v_g,
+        o_g,
         gain_grads[1],
-        gate_g.astype(F32),
-        up_g.astype(F32),
-        down_g.astype(F32),
+        gate_g,
+        up_g,
+        down_g,
     )
 
 

time: 501 us -> 477 us (0.952)
  other arithmetic: 25.5 us -> 3.5 us
  matrix products: 37.6 us -> 30.6 us
  Pallas kernels: 433 us -> 440 us
    convert_element_type x7 -> x0, other arithmetic: 22.6 us -> none  [the longest x1 4.6 us: heads_shards(): down_g.astype(F32)]
    pallas_call x0 -> x1, Pallas kernels: none -> 18.9 us  [widen(): pl.pallas_call(kernel, grid=(steps,), in_specs=specs, out_specs=specs, ou...]
    pallas_call x2, Pallas kernels: 433 us -> 421 us  [call(): pl.pallas_call(kernel, out_shape=[jax.ShapeDtypeStruct(shape, kind) for s...]
    dot_general x6 -> x5, matrix products: 37.6 us -> 30.6 us  [dot(): lax.dot_general(left, right, (dims, ((), ())), preferred_element_type=F32)]
where the time goes in v5:
time: 477 us
  Pallas kernels  440 us (92%)
  matrix products  30.6 us (6%)
    pallas_call x2, Pallas kernels, call(): pl.pallas_call(kernel, out_shape=[jax.ShapeDtypeStruct(shape, kind) for s...  421 us
    dot_general x5, matrix products, dot(): lax.dot_general(left, right, (dims, ((), ())), preferred_element_type=F32)  30.6 us
    pallas_call x1, Pallas kernels, widen(): pl.pallas_call(kernel, grid=(steps,), in_specs=specs, out_specs=specs, ou...  18.9 us

profile of v5, /device:TPU:0, one launch (start us, length us, event | category | flops | bytes accessed | tf_op | source)
XLA Modules:
  0.0 476.6 jit_solution(17048800745304150582)
XLA Ops:
  0.7 0.1 pad.5.clone
  0.7 0.7 convert_element_type.26
  1.4 0.7 stack.16
  2.1 0.7 stack.17
  2.8 0.7 maximum_maximum_fusion.small
  3.4 179.0 %shard_map.221 = (bf16[1024,2048]{1,0:T(8,128)(2,1)}, bf16[1024,384]{1,0:T(8,128)(2,1)}, bf16[1024,128]{1,0:T(8,128)(2,1)}, bf16[2048,384]{1,0:T(8,128)(2,1)}, b...) custom-call(bf16[2,64,2048]{2,1,0:T(8,128)(2,1)} %bitcast.24, ...), custom_call_target="tpu_custom_call" | custom-call | tf_op jit(solution)/shard_map/pallas_call | solution.py:515
  182.4 0.0 copy-start.3
  182.5 0.0 slice-start
  182.5 8.2 %multiply_convert_fusion = (bf16[2048,256]{1,0:T(8,128)(2,1)S(1)}, bf16[2048,256]{1,0:T(8,128)(2,1)S(1)}, bf16[2048,256]{1,0:T(8,128)(2,1)S(1)}) fusion(f32[2048,256]{1,0:T(8,128)} %get-tuple-element.45, f32[2048,256]{1,0:T(8,128)} %get-tuple-element.42, bf16[2048,2048]{1,0:T(8,128)(2,1)} %bitcast.34, bf16[2048,512]{1,0:T(8,128)(2,1)} %get-tuple-element.44), kind=kOutput, calls=%fused_computation.5 | convolution fusion | flops 2155347968 | bytes 16777216 | tf_op jit(solution)/shard_map/dot_general | solution.py:489
  190.7 0.0 copy-done.3
  190.7 0.0 slice-start.1
  190.7 6.4 %convolution_convert_fusion.2.gu_grad = bf16[2048,512]{1,0:T(8,128)(2,1)} fusion(bf16[2048,2048]{1,0:T(8,128)(2,1)S(1)} %bitcast.35, bf16[2048,256]{1,0:T(8,128)(2,1)S(1)} %get-tuple-element.75, bf16[2048,256]{1,0:T(8,128)(2,1)S(1)} %get-tuple-element.74), kind=kOutput, calls=%fused_computation.2 | convolution fusion | flops 4300210176 | bytes 12582912 | tf_op jit(solution)/shard_map/dot_general | solution.py:489
  197.1 0.0 slice-done
  197.1 0.0 slice-done.1
  197.1 0.0 copy-start
  197.2 3.3 convolution_convert_fusion.3.down_grad
  200.5 0.0 copy-done
  200.5 0.0 copy-start.4
  200.5 5.7 %convolution_convert_fusion = bf16[2048,2048]{1,0:T(8,128)(2,1)} fusion(bf16[2048,256]{1,0:T(8,128)(2,1)S(1)} %get-tuple-element.73, bf16[256,2048]{1,0:T(8,128)(2,1)S(1)} %copy-done), kind=kOutput, calls=%fused_computation | convolution fusion | flops 2151677952 | bytes 10485760 | tf_op jit(solution)/shard_map/dot_general | solution.py:489
  206.2 0.0 copy-done.4
  206.2 6.9 %convolution_convert_fusion.1 = bf16[2048,2048]{1,0:T(8,128)(2,1)} fusion(bf16[2048,512]{1,0:T(8,128)(2,1)S(1)} %copy-done.4, bf16[2048,256]{1,0:T(8,128)(2,1)S(1)} %get-tuple-element.75, bf16[2048,256]{1,0:T(8,128)(2,1)S(1)} %get-tuple-element.74), kind=kOutput, calls=%fused_computation.1 | convolution fusion | flops 4303355904 | bytes 12582912 | tf_op jit(solution)/shard_map/dot_general | solution.py:489
  213.1 241.7 %shard_map.222 = (bf16[2,64,2048]{2,1,0:T(8,128)(2,1)}, bf16[2,64,2048]{2,1,0:T(8,128)(2,1)}, bf16[512,1024]{1,0:T(8,128)(2,1)}, bf16[512,1024]{1,0:T(8,128)(2,1...) custom-call(bf16[4,4,2,64,2048]{4,3,2,1,0:T(8,128)(2,1)} %bitcast.23, ...), custom_call_target="tpu_custom_call" | custom-call | tf_op jit(solution)/shard_map/pallas_call | solution.py:515
  454.8 0.8 reduce_sum.9
  455.6 0.6 fusion.5
  456.1 0.0 copy-start.2
  456.1 0.0 copy-start.1
  456.1 18.9 %shard_map.223 = (f32[512,1024]{1,0:T(8,128)}, f32[512,1024]{1,0:T(8,128)}, f32[512,1024]{1,0:T(8,128)}, f32[1024,512]{1,0:T(8,128)}, f32[512,4096]{1,0:T(8,128)...) custom-call(bf16[512,1024]{1,0:T(8,128)(2,1)} %get-tuple-element.59.refs_0_, bf16[512,1024]{1,0:T(8,128)(2,1)} %get-tuple-element.60.refs_1_, ...), custom_call_target="tpu_custom_call" | custom-call | tf_op jit(solution)/shard_map/pallas_call | solution.py:1047
  475.0 0.0 copy-done.2
  475.0 0.8 copy.30
  475.8 0.0 copy-done.1
  475.8 0.8 copy.31
  (2 shorter events, 0.0 us)
Async XLA Ops:
  182.4 8.2 %copy-start.3 = (bf16[4,4,2,64,2048]{4,3,2,1,0:T(8,128)(2,1)S(1)}, bf16[4,4,2,64,2048]{4,3,2,1,0:T(8,128)(2,1)}, u32[]{:S(2)}) copy-start(bf16[4,4,2,64,2048]{4,3,2,1,0:T(8,128)(2,1)} %get-tuple-element.43) | copy-start | bytes 25165828
  182.5 14.7 %slice-start = ((s8[8388608]{0:T(1024)(128)(4,1)}), s8[4194304]{0:T(1024)(128)(4,1)S(1)}, s32[]{:S(2)}) async-start(s8[8388608]{0:T(1024)(128)(4,1)} %bitcast.20), calls=%async_computation | async-start | bytes 8388608
  190.7 6.5 %slice-start.1 = ((s8[8388608]{0:T(1024)(128)(4,1)}), s8[4194304]{0:T(1024)(128)(4,1)S(1)}, s32[]{:S(2)}) async-start(s8[8388608]{0:T(1024)(128)(4,1)} %bitcast.20), calls=%async_computation.1 | async-start | bytes 8388608
  197.1 3.3 copy-start
  200.5 5.7 %copy-start.4 = (bf16[2048,512]{1,0:T(8,128)(2,1)S(1)}, bf16[2048,512]{1,0:T(8,128)(2,1)}, u32[]{:S(2)}) copy-start(bf16[2048,512]{1,0:T(8,128)(2,1)} %get-tuple-element.44) | copy-start | bytes 6291460
  456.1 18.9 %copy-start.2 = (bf16[2,64,2048]{2,1,0:T(8,128)(2,1)S(1)}, bf16[2,64,2048]{2,1,0:T(8,128)(2,1)}, u32[]{:S(2)}) copy-start(bf16[2,64,2048]{2,1,0:T(8,128)(2,1)} %get-tuple-element.56) | copy-start | bytes 1572868
  456.1 19.7 %copy-start.1 = (bf16[2,64,2048]{2,1,0:T(8,128)(2,1)S(1)}, bf16[2,64,2048]{2,1,0:T(8,128)(2,1)}, u32[]{:S(2)}) copy-start(bf16[2,64,2048]{2,1,0:T(8,128)(2,1)} %get-tuple-element.57) | copy-start | bytes 1572868

commit v6 on v5

--- a/solution.py
+++ b/solution.py
@@ -517,7 +517,7 @@
         out_shape=[jax.ShapeDtypeStruct(shape, kind) for shape, kind, _ in outs],
         in_specs=[pl.BlockSpec(memory_space=ANY)] * len(args),
         out_specs=[pl.BlockSpec(memory_space=space) for _, _, space in outs],
-        scratch_shapes=list(scratch) + [pltpu.SemaphoreType.DMA((count,)) for count in counts],
+        scratch_shapes=list(scratch) + [pltpu.SemaphoreType.DMA(shape) for shape in counts],
         compiler_params=pltpu.CompilerParams(
             collective_id=name, has_side_effects=True, vmem_limit_bytes=vmem * MIB
         ),
@@ -526,9 +526,10 @@
 
 def forward_kernel(
     zs, x, wq, wk, wv, wo, small, cosine, sine, wg, wu, wd, cot,
-    hidden_out, qkv_out, attended_out, qkv_w_out, out_w_out, gains_out, docs_out, middle, h2_out, cot_out, gu_w_out, down_w_out, gate_out, gp_out,
+    hidden_out, qkv_out, attended_out, qkv_w_out, out_w_out, gains_out, docs_out, middle, h2_out, cot_out, gh_out, feed_out, grad_gu_out, product_out,
     x_all, h1, qkv_w, out_w, small_z, small_x, gains, docs, cos_v, sin_v, qkv, attended, part, sib, far, landed,
-    x_lane, h2, mid_v, h2_all, cot_all, gu_w, down_w, gate_v, gp_v, send_sems, recv_sems, local_sems,
+    x_lane, h2, mid_v, h2_all, cot_all, gu_w, down_w, gate_v, gp_v,
+    grad_gu, product, gh_v, feed_v, send_sems, recv_sems, local_sems, stage_sems,
 ):
     net = Net(zs, send_sems, recv_sems, local_sems)
     net.meet()
@@ -736,40 +737,73 @@
     hidden.relay(0)
     fetched(2)
     tiles(products)
-    saved += [net.keep(down_w, down_w_out), net.keep(gp_v, gp_out)]
     for s in range(1, zs):
         hidden.relay(s)
     hidden.end()
     saved.append(net.keep(h2_all, h2_out))
     fetched(0)
     tiles(gates)
-    saved.append(net.keep(gate_v, gate_out))
     fetched(1)
-    saved.append(net.keep(gu_w, gu_w_out))
+
+    def leave(slot, at):
+        return (
+            pltpu.make_async_copy(gh_v.at[slot], gh_out.at[at], stage_sems.at[0, slot]),
+            pltpu.make_async_copy(feed_v.at[slot], feed_out.at[at], stage_sems.at[1, slot]),
+        )
+
+    def both(pair):
+        for slot in range(2):
+            i = 2 * pair + slot
+            dp, z = lax.div(i, zs // few), pl.ds(lax.rem(i, zs // few) * few, few)
+            at = aligned(i, 256)
+            upward = dot(h2_all[dp, z].reshape(256, -1), gu_w[:, wide:])
+            gate, grad_product = gate_v[at, :], gp_v[at, :]
+            sigma = jax.nn.sigmoid(gate)
+            silu = gate * sigma
+            product[at, :] = (silu * upward).astype(BF)
+            grad_gu[at, 0:wide] = (grad_product * upward * sigma * (1.0 + gate * (1.0 - sigma))).astype(BF)
+            grad_gu[at, wide:] = (grad_product * silu).astype(BF)
+
+            @pl.when(pair > 0)
+            def _():
+                for copy in leave(slot, at):
+                    copy.wait()
+
+            gh_v[slot] = dot(grad_gu[at, :], gu_w[...], ((1,), (1,)), BF)
+            feed_v[slot] = dot(product[at, :], down_w[...], kind=BF)
+            for copy in leave(slot, at):
+                copy.start()
+
+    loop(2 * zs // few, both)
+    saved += [net.keep(grad_gu, grad_gu_out), net.keep(product, product_out)]
+    for slot in range(2):
+        for copy in leave(slot, aligned(slot, 256)):
+            copy.wait()
     for copy in saved:
         copy.wait()
     net.finish()
 
 
 ORDER = (
-    "g0s0", "g0z", "g2s0", "g2z", "hstart", "F0", "g0s1", "F1", "F2", "S0", "F3", "S1", "T0", "fstart",
-    "g0r0", "S2", "fF0", "T1", "S3", "T2", "g2s1", "g2s2", "g2r0", "fS0", "T3", "g2r1", "hend", "gstart",
-    "g2s3", "fF1", "g2r2", "gs1", "gs2", "gs3", "gf0", "gf1", "g1z", "g1s0", "fF2", "g0s2", "g1s1", "gf2",
-    "gf3", "gend", "g0s3", "A0", "B0", "bt0", "g0r1", "fF3", "g1s2", "A1", "B1", "fS1", "g1r0", "W1",
-    "W2", "fT0", "sw0", "g1r1", "sw1", "fS2", "g1s3", "sw2", "g0r2", "bt1", "bx", "sw3", "fT1", "Ls0",
-    "g1r2", "Ls1", "Ls2", "Lr0", "fS3", "Ls3", "g0r3", "fT2", "fT3", "Lr1", "bend", "gain2", "Lr2", "g2r3",
-    "Lr3", "g1r3", "gain3", "fend",
+    "hstart", "F0", "F1", "MG", "g0s0", "F2", "g0z", "S0", "F3", "S1", "T0", "g1s0", "fstart", "S2",
+    "T1", "S3", "g0r0", "T2", "g0s1", "T3", "g0s2", "fF0", "g0r1", "hend", "gstart", "MD", "fF1", "gs1",
+    "fF2", "gs2", "g0r2", "g2s0", "gs3", "g2z", "gf0", "g2s1", "fS0", "g1z", "gf1", "g2r0", "g0s3", "gf2",
+    "gf3", "fS1", "gend", "fS2", "A0", "g2s2", "fF3", "B0", "A1", "g1s1", "g1s2", "bt0", "g1r0", "B1",
+    "g2r1", "W1", "g2r2", "bt1", "g1s3", "g0r3", "bx", "W2", "sw0", "sw1", "fT0", "sw2", "fT1", "fS3",
+    "sw3", "g2s3", "g1r1", "Ls0", "bend", "g1r2", "Ls1", "Lr0", "gain2", "Lr1", "fT2", "Ls2", "Ls3", "fT3",
+    "g2r3", "Lr2", "g1r3", "Lr3", "gain3", "fend",
 )
-RELAY_WAYS = ("xy", "x", "y", "y", "x", "y", "xy")
+RELAY_WAYS = ("y", "xy", "x", "xy", "y", "xy", "xy")
 
 
 def backward_kernel(
-    zs, gh_part, feed_part, gu_grad, down_grad, middle, cot, x, gains_in, docs_in, cosine, sine,
+    zs, gh_part, feed_part, h2_in, cots_in, grad_gu_in, product_in, middle, cot, x, gains_in, docs_in, cosine, sine,
     hidden_in, qkv_in, attended_in, qkv_w_in, out_w_in,
     layer_out, input_grad, q_out, k_out, v_out, o_out, gate_out, up_out, down_out, gains_out,
     own, sib, one, two, landed, own_f, sib_f, one_f, two_f, landed_f, part, sib_1, far_1, landed_1,
     h1, qkv, attended, qkv_w, out_w, gbr_all, gqkv, gains, docs, cos_v, sin_v, hg, mid_v, cot_v, x_v, gm_v, gbr_v, out_v,
-    lo_v, gsum, gall, gsum_z, g_far, g_land, q_give, q_own, q_land, o_part, o_own, o_land, send_sems, recv_sems, local_sems,
+    lo_v, gsum, gall, gsum_z, g_far, g_land, q_give, q_own, q_land, o_part, o_own, o_land,
+    grad_gu, product_t, strip, gu_grad, down_grad, send_sems, recv_sems, local_sems, strip_sems,
 ):
     net = Net(zs, send_sems, recv_sems, local_sems)
     net.meet()
@@ -781,6 +815,7 @@
     scale = HEAD_DIM**-0.5
     hidden = SumAll(net, gh_part, own, sib, one, two, landed)
     feed = SumAll(net, feed_part, own_f, sib_f, one_f, two_f, landed_f)
+    mlp_local = [net.keep(grad_gu_in, grad_gu)]
     local = [net.keep(middle, mid_v), net.keep(cot.at[net.t], cot_v), net.keep(gains_in, gains)]
     local += [net.keep(x.at[net.t], x_v), net.keep(docs_in, docs), net.keep(cosine, cos_v), net.keep(sine, sin_v)]
     local += [net.keep(qkv_in, qkv), net.keep(attended_in, attended), net.keep(qkv_w_in, qkv_w)]
@@ -1005,8 +1040,47 @@
 
         return step
 
+    thin = strip.shape[2]
+
+    def strips(ref, body, first=None):
+        def load(i):
+            return pltpu.make_async_copy(ref.at[:, aligned(i, thin)], strip.at[lax.rem(i, 2)], strip_sems.at[lax.rem(i, 2)])
+
+        count = ref.shape[1] // thin
+        load(0).start()
+        if first:
+            first()
+
+        def one(i):
+            @pl.when(i + 1 < count)
+            def _():
+                load(i + 1).start()
+
+            load(i).wait()
+            body(i, strip.at[lax.rem(i, 2)])
+
+        loop(count, one)
+
+    def gate_up_grads():
+        mlp_local[0].wait()
+
+        def one(i, part):
+            gu_grad[aligned(i, thin), :] = dot(part[...], grad_gu[...], ((0,), (0,)), BF)
+
+        strips(h2_in, one)
+
+    def down_grads():
+        def turn_product():
+            net.keep(product_in, strip.at[1]).wait()
+            product_t[...] = strip[1].T
+
+        def one(i, part):
+            down_grad[:, aligned(i, thin)] = dot(product_t[...], part[...], kind=BF)
+
+        strips(cots_in, one, turn_product)
+
     steps = {
-        "hstart": hidden.start, "hend": hidden_end, "gstart": gather.start, "gend": gather.end, "fstart": feed.start,
+        "MG": gate_up_grads, "MD": down_grads, "hstart": hidden.start, "hend": hidden_end, "gstart": gather.start, "gend": gather.end, "fstart": feed.start,
         "fend": feed_end, "W1": weights_give, "W2": weights_own, "bx": branch.across, "bend": branch_end,
         "gain2": gains_plane, "gain3": gains_line,
     }
@@ -1032,7 +1106,7 @@
     total = g_land[0]
     for z in range(1, zs):
         total += g_land[z]
-    gains_out[...] = total
+    gains_out[...] = jnp.sum(total, axis=1)
     net.finish()
 
 
@@ -1080,7 +1154,7 @@
     small = jnp.concatenate([small, docs_rows, jnp.zeros((6 - seq // deep, deep), F32)])
     cosine, sine = (jnp.asarray(table) for table in rope_tables(seq))
     half = stretch // 2
-    hidden, qkv, attended, qkv_w, out_w, gains, docs, middle, h2_all, cot_all, gu_w, down_w, gate, grad_product = call(
+    hidden, qkv, attended, qkv_w, out_w, gains, docs, middle, h2_all, cot_all, gh_part, feed_part, grad_gu, product = call(
         functools.partial(forward_kernel, zs),
         1,
         [
@@ -1094,10 +1168,10 @@
             ((stretch, width), F32, ANY),
             ((4, zs, 2, stretch, width), BF, ANY),
             ((4, zs, 2, stretch, width), BF, ANY),
-            ((width, 2 * wide), BF, ANY),
-            ((wide, width), BF, ANY),
-            ((4 * seq, wide), F32, ANY),
-            ((4 * seq, wide), F32, ANY),
+            ((4 * seq, width), BF, ANY),
+            ((4 * seq, width), BF, ANY),
+            ((4 * seq, 2 * wide), BF, ANY),
+            ((4 * seq, wide), BF, ANY),
         ],
         [
             VMEM((pair, width), BF),
@@ -1125,25 +1199,20 @@
             VMEM((wide, width), BF),
             VMEM((4 * seq, wide), F32),
             VMEM((4 * seq, wide), F32),
+            VMEM((4 * seq, 2 * wide), BF),
+            VMEM((4 * seq, wide), BF),
+            VMEM((2, 256, width), BF),
+            VMEM((2, 256, width), BF),
         ],
-        (134, 131, 34),
+        ((134,), (131,), (34,), (2, 2)),
         (x, w_query, w_key, w_value, w_out, small, cosine, sine, w_gate, w_up, w_down, cot),
-        58,
+        60,
     )
 
     h2 = h2_all.reshape(4 * seq, width)
     cots = cot_all.reshape(4 * seq, width)
-    upward = dot(h2, gu_w[:, wide:])
-    sigma_gate = jax.nn.sigmoid(gate)
-    silu = gate * sigma_gate
-    product = (silu * upward).astype(BF)
-    grad_gate = (grad_product * upward * sigma_gate * (1.0 + gate * (1.0 - sigma_gate))).astype(BF)
-    grad_up = (grad_product * silu).astype(BF)
-    grad_gu = jnp.concatenate([grad_gate, grad_up], axis=1)
-    gh_part = dot(grad_gu, gu_w, ((1,), (1,)), BF).reshape(4, zs, 2, stretch, width)
-    feed_part = dot(product, down_w, kind=BF).reshape(4, zs, 2, stretch, width)
-    gu_grad = dot(h2, grad_gu, ((0,), (0,)), BF)
-    down_grad = dot(product, cots, ((0,), (0,)), BF)
+    gh_part = gh_part.reshape(4, zs, 2, stretch, width)
+    feed_part = feed_part.reshape(4, zs, 2, stretch, width)
 
     sum_scratch = [
         VMEM((4, zs, stretch, width), BF),
@@ -1165,7 +1234,7 @@
             (w_gate.shape, BF, ANY),
             (w_up.shape, BF, ANY),
             (w_down.shape, BF, ANY),
-            ((2, 8, deep), F32, VMEM),
+            ((2, deep), F32, VMEM),
         ],
         sum_scratch
         + sum_scratch
@@ -1204,25 +1273,29 @@
             VMEM((zs, HEAD_DIM, deep), BF),
             VMEM((zs, HEAD_DIM // 2, deep), BF),
             VMEM((zs, HEAD_DIM // 2, deep), BF),
+            VMEM((4 * seq, 2 * wide), BF),
+            VMEM((wide, 4 * seq), BF),
+            VMEM((2, 4 * seq, 256), BF),
+            VMEM((width, 2 * wide), BF),
+            VMEM((wide, width), BF),
         ],
-        (232, 231, 34),
+        ((232,), (231,), (36,), (2,)),
         (
-            gh_part, feed_part, gu_grad, down_grad, middle, cot, x, gains, docs, cosine, sine,
+            gh_part, feed_part, h2, cots, grad_gu, product, middle, cot, x, gains, docs, cosine, sine,
             hidden, qkv, attended, qkv_w, out_w,
         ),
         60,
     )
-    gain_grads = jnp.sum(gains_g, axis=1)
     q_g, k_g, v_g, o_g, gate_g, up_g, down_g = widen(q_g, k_g, v_g, o_g, gate_g, up_g, down_g)
     return (
         layer_out.reshape(activations.shape),
         input_grad.reshape(activations.shape),
-        gain_grads[0],
+        gains_g[0],
         q_g,
         k_g,
         v_g,
         o_g,
-        gain_grads[1],
+        gains_g[1],
         gate_g,
         up_g,
         down_g,

time: 477 us -> 466 us (0.977)
  matrix products: 30.6 us -> 0 us
  Pallas kernels: 440 us -> 458 us
    dot_general x5 -> x0, matrix products: 30.6 us -> none  [dot(): lax.dot_general(left, right, (dims, ((), ())), preferred_element_type=F32)]
    pallas_call x2, Pallas kernels: 421 us -> 439 us  [call(): pl.pallas_call(kernel, out_shape=[jax.ShapeDtypeStruct(shape, kind) for s...]
where the time goes in v6:
time: 466 us; the launch traced here: 464 us
  Pallas kernels  458 us (98%)
    pallas_call x2, Pallas kernels, call(): pl.pallas_call(kernel, out_shape=[jax.ShapeDtypeStruct(shape, kind) for s...  439 us
    pallas_call x1, Pallas kernels, widen(): pl.pallas_call(kernel, grid=(steps,), in_specs=specs, out_specs=specs, ou...  18.9 us

profile of v6, /device:TPU:0, one launch (start us, length us, event | category | flops | bytes accessed | tf_op | source)
XLA Modules:
  0.0 464.3 jit_solution(3498912044497738164)
XLA Ops:
  0.7 0.1 pad.3.clone
  0.7 0.7 convert_element_type.2
  1.4 0.7 stack.16
  2.1 0.7 stack.17
  2.8 0.7 maximum_maximum_fusion.small
  3.4 191.6 %shard_map.221 = (bf16[1024,2048]{1,0:T(8,128)(2,1)}, bf16[1024,384]{1,0:T(8,128)(2,1)}, bf16[1024,128]{1,0:T(8,128)(2,1)}, bf16[2048,384]{1,0:T(8,128)(2,1)}, b...) custom-call(bf16[2,64,2048]{2,1,0:T(8,128)(2,1)} %bitcast.16, ...), custom_call_target="tpu_custom_call" | custom-call | tf_op jit(solution)/shard_map/pallas_call | solution.py:515
  195.0 247.5 %shard_map.222 = (bf16[2,64,2048]{2,1,0:T(8,128)(2,1)}, bf16[2,64,2048]{2,1,0:T(8,128)(2,1)}, bf16[512,1024]{1,0:T(8,128)(2,1)}, bf16[512,1024]{1,0:T(8,128)(2,1...) custom-call(bf16[4,4,2,64,2048]{4,3,2,1,0:T(8,128)(2,1)} %bitcast.14, ...), custom_call_target="tpu_custom_call" | custom-call | tf_op jit(solution)/shard_map/pallas_call | solution.py:515
  442.5 1.3 fusion
  443.9 0.0 copy-start.1
  443.9 0.0 copy-start
  443.9 18.9 %shard_map.223 = (f32[512,1024]{1,0:T(8,128)}, f32[512,1024]{1,0:T(8,128)}, f32[512,1024]{1,0:T(8,128)}, f32[1024,512]{1,0:T(8,128)}, f32[512,4096]{1,0:T(8,128)...) custom-call(bf16[512,1024]{1,0:T(8,128)(2,1)} %get-tuple-element.59.refs_0_, bf16[512,1024]{1,0:T(8,128)(2,1)} %get-tuple-element.60.refs_1_, ...), custom_call_target="tpu_custom_call" | custom-call | tf_op jit(solution)/shard_map/pallas_call | solution.py:1121
  462.7 0.0 copy-done.1
  462.7 0.8 copy.27
  463.5 0.0 copy-done
  463.5 0.8 copy.28
  (1 shorter events, 0.0 us)
Async XLA Ops:
  443.9 18.9 %copy-start.1 = (bf16[2,64,2048]{2,1,0:T(8,128)(2,1)S(1)}, bf16[2,64,2048]{2,1,0:T(8,128)(2,1)}, u32[]{:S(2)}) copy-start(bf16[2,64,2048]{2,1,0:T(8,128)(2,1)} %get-tuple-element.56) | copy-start | bytes 1572868
  443.9 19.7 %copy-start = (bf16[2,64,2048]{2,1,0:T(8,128)(2,1)S(1)}, bf16[2,64,2048]{2,1,0:T(8,128)(2,1)}, u32[]{:S(2)}) copy-start(bf16[2,64,2048]{2,1,0:T(8,128)(2,1)} %get-tuple-element.57) | copy-start | bytes 1572868

commit v7 on v6

--- a/solution.py
+++ b/solution.py
@@ -585,7 +585,7 @@
 
     def fetch(k):
         src, dst = mlp[k]
-        mlp_waits[k] = [net.send(src(lax.rem(net.z + s, zs)), dst, net.along_z(s)) for s in range(1, zs)]
+        mlp_waits[k] = [net.send(src(lax.rem(net.z + s, zs)), dst, net.along_z(s)) for s in range(zs - 1, 0, -1)]
 
     def fetched(k):
         for copy in mlp_waits[k]:

time: 466 us -> 463 us (level)
  no operation moved by 1% of the time
where the time goes in v7:
time: 463 us; the launch traced here: 462 us
  Pallas kernels  456 us (98%)
    pallas_call x2, Pallas kernels, call(): pl.pallas_call(kernel, out_shape=[jax.ShapeDtypeStruct(shape, kind) for s...  437 us
    pallas_call x1, Pallas kernels, widen(): pl.pallas_call(kernel, grid=(steps,), in_specs=specs, out_specs=specs, ou...  18.9 us

profile of v7, /device:TPU:0, one launch (start us, length us, event | category | flops | bytes accessed | tf_op | source)
XLA Modules:
  0.0 462.2 jit_solution(12122892717201830685)
XLA Ops:
  0.7 0.1 pad.3.clone
  0.7 0.7 convert_element_type.2
  1.4 0.7 stack.16
  2.1 0.7 stack.17
  2.8 0.7 maximum_maximum_fusion.small
  3.4 186.3 %shard_map.221 = (bf16[1024,2048]{1,0:T(8,128)(2,1)}, bf16[1024,384]{1,0:T(8,128)(2,1)}, bf16[1024,128]{1,0:T(8,128)(2,1)}, bf16[2048,384]{1,0:T(8,128)(2,1)}, b...) custom-call(bf16[2,64,2048]{2,1,0:T(8,128)(2,1)} %bitcast.16, ...), custom_call_target="tpu_custom_call" | custom-call | tf_op jit(solution)/shard_map/pallas_call | solution.py:515
  189.8 250.7 %shard_map.222 = (bf16[2,64,2048]{2,1,0:T(8,128)(2,1)}, bf16[2,64,2048]{2,1,0:T(8,128)(2,1)}, bf16[512,1024]{1,0:T(8,128)(2,1)}, bf16[512,1024]{1,0:T(8,128)(2,1...) custom-call(bf16[4,4,2,64,2048]{4,3,2,1,0:T(8,128)(2,1)} %bitcast.14, ...), custom_call_target="tpu_custom_call" | custom-call | tf_op jit(solution)/shard_map/pallas_call | solution.py:515
  440.4 1.3 fusion
  441.8 0.0 copy-start.1
  441.8 0.0 copy-start
  441.8 18.9 %shard_map.223 = (f32[512,1024]{1,0:T(8,128)}, f32[512,1024]{1,0:T(8,128)}, f32[512,1024]{1,0:T(8,128)}, f32[1024,512]{1,0:T(8,128)}, f32[512,4096]{1,0:T(8,128)...) custom-call(bf16[512,1024]{1,0:T(8,128)(2,1)} %get-tuple-element.59.refs_0_, bf16[512,1024]{1,0:T(8,128)(2,1)} %get-tuple-element.60.refs_1_, ...), custom_call_target="tpu_custom_call" | custom-call | tf_op jit(solution)/shard_map/pallas_call | solution.py:1121
  460.6 0.0 copy-done.1
  460.6 0.8 copy.27
  461.4 0.0 copy-done
  461.4 0.8 copy.28
  (1 shorter events, 0.0 us)
Async XLA Ops:
  441.8 18.9 %copy-start.1 = (bf16[2,64,2048]{2,1,0:T(8,128)(2,1)S(1)}, bf16[2,64,2048]{2,1,0:T(8,128)(2,1)}, u32[]{:S(2)}) copy-start(bf16[2,64,2048]{2,1,0:T(8,128)(2,1)} %get-tuple-element.56) | copy-start | bytes 1572868
  441.8 19.7 %copy-start = (bf16[2,64,2048]{2,1,0:T(8,128)(2,1)S(1)}, bf16[2,64,2048]{2,1,0:T(8,128)(2,1)}, u32[]{:S(2)}) copy-start(bf16[2,64,2048]{2,1,0:T(8,128)(2,1)} %get-tuple-element.57) | copy-start | bytes 1572868

commit v8 on v7

--- a/solution.py
+++ b/solution.py
@@ -553,7 +553,7 @@
     for m, w in enumerate((wq, wk, wv)):
         col = pl.ds(m * HEAD_DIM, HEAD_DIM)
         w_local.append(net.keep(w.at[:, head(net.z)], qkv_w.at[mine, col]))
-    for s in range(1, zs):
+    for s in range(zs - 1, 0, -1):
         z = lax.rem(net.z + s, zs)
         rows = pl.ds(pl.multiple_of(net.z * deep + net.a * half, half), half)
         qkv_sends.append(
@@ -564,10 +564,12 @@
         )
     out_rows = pl.ds(pl.multiple_of(net.a * side, side), side)
     w_local.append(net.keep(wo.at[head(net.z)], out_w.at[:, mine]))
-    for s in range(1, zs):
+    for s in range(zs - 1, 0, -1):
         z = lax.rem(net.z + s, zs)
         at = pl.ds(pl.multiple_of((net.b * zs + z) * HEAD_DIM + net.a * side, side), side)
         out_sends.append(net.send(wo.at[at], out_w.at[out_rows, mine], net.along_z(s)))
+    qkv_sends.reverse()
+    out_sends.reverse()
 
     cotan = GatherAll(net, cot.at[net.t], cot_all)
     mlp_waits, mlp_local = {}, {}

time: 463 us -> 467 us (level)
  no operation moved by 1% of the time
where the time goes in v8:
time: 467 us; the launch traced here: 466 us
  Pallas kernels  459 us (98%)
    pallas_call x2, Pallas kernels, call(): pl.pallas_call(kernel, out_shape=[jax.ShapeDtypeStruct(shape, kind) for s...  440 us
    pallas_call x1, Pallas kernels, widen(): pl.pallas_call(kernel, grid=(steps,), in_specs=specs, out_specs=specs, ou...  18.9 us

profile of v8, /device:TPU:0, one launch (start us, length us, event | category | flops | bytes accessed | tf_op | source)
XLA Modules:
  0.0 465.7 jit_solution(4474500346072211122)
XLA Ops:
  0.7 0.1 pad.3.clone
  0.7 0.7 convert_element_type.2
  1.4 0.7 stack.16
  2.1 0.7 stack.17
  2.8 0.7 maximum_maximum_fusion.small
  3.4 194.0 %shard_map.221 = (bf16[1024,2048]{1,0:T(8,128)(2,1)}, bf16[1024,384]{1,0:T(8,128)(2,1)}, bf16[1024,128]{1,0:T(8,128)(2,1)}, bf16[2048,384]{1,0:T(8,128)(2,1)}, b...) custom-call(bf16[2,64,2048]{2,1,0:T(8,128)(2,1)} %bitcast.16, ...), custom_call_target="tpu_custom_call" | custom-call | tf_op jit(solution)/shard_map/pallas_call | solution.py:515
  197.4 246.5 %shard_map.222 = (bf16[2,64,2048]{2,1,0:T(8,128)(2,1)}, bf16[2,64,2048]{2,1,0:T(8,128)(2,1)}, bf16[512,1024]{1,0:T(8,128)(2,1)}, bf16[512,1024]{1,0:T(8,128)(2,1...) custom-call(bf16[4,4,2,64,2048]{4,3,2,1,0:T(8,128)(2,1)} %bitcast.14, ...), custom_call_target="tpu_custom_call" | custom-call | tf_op jit(solution)/shard_map/pallas_call | solution.py:515
  443.9 1.3 fusion
  445.3 0.0 copy-start.1
  445.3 0.0 copy-start
  445.3 18.9 %shard_map.223 = (f32[512,1024]{1,0:T(8,128)}, f32[512,1024]{1,0:T(8,128)}, f32[512,1024]{1,0:T(8,128)}, f32[1024,512]{1,0:T(8,128)}, f32[512,4096]{1,0:T(8,128)...) custom-call(bf16[512,1024]{1,0:T(8,128)(2,1)} %get-tuple-element.59.refs_0_, bf16[512,1024]{1,0:T(8,128)(2,1)} %get-tuple-element.60.refs_1_, ...), custom_call_target="tpu_custom_call" | custom-call | tf_op jit(solution)/shard_map/pallas_call | solution.py:1123
  464.1 0.0 copy-done.1
  464.1 0.8 copy.27
  464.9 0.0 copy-done
  464.9 0.8 copy.28
  (1 shorter events, 0.0 us)
Async XLA Ops:
  445.3 18.9 %copy-start.1 = (bf16[2,64,2048]{2,1,0:T(8,128)(2,1)S(1)}, bf16[2,64,2048]{2,1,0:T(8,128)(2,1)}, u32[]{:S(2)}) copy-start(bf16[2,64,2048]{2,1,0:T(8,128)(2,1)} %get-tuple-element.56) | copy-start | bytes 1572868
  445.3 19.7 %copy-start = (bf16[2,64,2048]{2,1,0:T(8,128)(2,1)S(1)}, bf16[2,64,2048]{2,1,0:T(8,128)(2,1)}, u32[]{:S(2)}) copy-start(bf16[2,64,2048]{2,1,0:T(8,128)(2,1)} %get-tuple-element.57) | copy-start | bytes 1572868
